TPU v7x, 32 devices: a whole 2x2x4 slice. The times are simulated.
32 devices in a mesh: group: 4 (over y, x), member: 8 (over z, core).
Axes of the slice: x: 2, y: 2, z: 4, core: 2. Of those that a mesh axis runs over, the one named last changes fastest.
Arguments:
- entity: bfloat16 [8192, 800], P(('group', 'member')), may hold values from -3 to 7.5
- adagrad_state: float32 [8192], P(('group', 'member')), may hold values from 0.01 to 1
- relation: bfloat16 [1345, 800], replicated, may hold values from -1.8 to 1.8
- source_ids: int32 [2, 16384], P(None, ('group', 'member')), may hold values from 0 to 255
- relation_ids: int32 [2, 16384], P(None, ('group', 'member')), may hold values from 0 to 1344
- dest_groups: int32 [2, 16384, 1], P(None, ('group', 'member')), may hold values from 0 to 3; in each aligned block of 512 rows (0 to 511, 512 to 1023, ..., all dimensions but the last counted through in order) at most 256 rows name the same one
- dest_rows: int32 [2, 16384], P(None, ('group', 'member')), may hold values from 0 to 255
- negative_ids: int32 [2, 32000], P(None, ('group', 'member')), may hold values from 0 to 255
- owners: int32 [2, 4], replicated, may hold values from 0 to 7
Outputs:
- new_entity: bfloat16 [8192, 800], P(('group', 'member'))
- new_state: float32 [8192], P(('group', 'member'))
Inputs may be any that keep to these rules, and one draw needn't show every extreme that they name: `dest_groups`: for each sub-step and each device's 512 edges, at most 256 name any one destination group, a bound that some block reaches.
All inputs are finite; a program needn't handle non-finite values.
Results may differ from a plain program's by a relative error of at most 0.017.
Values may be sent and summed in bfloat16 or wider, within the bound.
No kernel may reach another device: no remote copies, remote signals or barrier semaphores. Data moves between devices by JAX's collectives and lax.ppermute only.
A program may use at most 64 MiB of HBM per device.

v0:
```python
import jax
import jax.numpy as jnp
from jax import lax
from jax.sharding import PartitionSpec as P


def broadcast(value, axis, source):
    kept = jnp.where(lax.axis_index(axis) == source, value, 0).astype(value.dtype)
    return lax.psum(kept, axis)


def complex_query(source, rel):
    half = source.shape[-1] // 2
    sr, si = (source[..., :half], source[..., half:])
    rr, ri = (rel[..., :half], rel[..., half:])
    return jnp.concatenate([sr * rr - si * ri, sr * ri + si * rr], -1)


def source_grad(grad_query, rel):
    half = grad_query.shape[-1] // 2
    gr, gi = (grad_query[..., :half], grad_query[..., half:])
    rr, ri = (rel[..., :half], rel[..., half:])
    return jnp.concatenate([gr * rr + gi * ri, gi * rr - gr * ri], -1)


def edge_terms(source_rows, rel_rows, dest_rows, negatives):
    rel = rel_rows.astype(jnp.float32)
    query = complex_query(source_rows.astype(jnp.float32), rel).astype(jnp.bfloat16)
    dest = dest_rows.astype(jnp.float32)
    positive = jnp.sum(query.astype(jnp.float32) * dest, -1)
    scores = lax.dot_general(
        query, negatives, (((1,), (1,)), ((), ())), preferred_element_type=jnp.float32
    )
    top = jnp.maximum(jnp.max(scores, 1), positive)
    pos_exp = jnp.exp(positive - top)
    neg_exp = jnp.exp(scores - top[:, None])
    total = pos_exp + jnp.sum(neg_exp, 1)
    coef_pos = pos_exp / total - 1.0
    coef_neg = (neg_exp / total[:, None]).astype(jnp.bfloat16)
    grad_query = coef_pos[:, None] * dest + jnp.dot(
        coef_neg, negatives, preferred_element_type=jnp.float32
    )
    grad_source = source_grad(grad_query, rel)
    grad_neg = lax.dot_general(
        coef_neg, query, (((0,), (0,)), ((), ())), preferred_element_type=jnp.float32
    )
    return (grad_source, query, coef_pos, grad_neg)


def scatter_rows(values, row_ids, count):
    onehot = (row_ids[:, None] == jnp.arange(count, dtype=jnp.int32)[None, :]).astype(jnp.float32)
    return lax.dot_general(
        onehot,
        values,
        (((0,), (0,)), ((), ())),
        precision=lax.Precision.HIGHEST,
        preferred_element_type=jnp.float32,
    )


def per_device(
    entity,
    adagrad_state,
    relation,
    source_ids,
    relation_ids,
    dest_groups,
    dest_rows,
    negative_ids,
    owners,
):
    groups = lax.axis_size("group")
    group_index = lax.axis_index("group")
    member_index = lax.axis_index("member")
    shard_rows = entity.shape[0]
    table = entity
    state = adagrad_state
    for step in range(source_ids.shape[0]):
        root = owners[step, group_index]
        block = broadcast(table, "member", root)
        src = source_ids[step]
        rel = relation_ids[step]
        dgr = dest_groups[step, :, 0]
        drw = dest_rows[step]
        neg = negative_ids[step]
        source_rows = jnp.take(block, src, axis=0)
        rel_rows = jnp.take(relation, rel, axis=0)
        negatives = jnp.take(table, neg, axis=0)
        whole = lax.all_gather(table, "group", axis=0, tiled=True)
        flat = dgr * shard_rows + drw
        dest_vals = jnp.take(whole, flat, axis=0)
        grad_source, query, coef_pos, grad_neg = edge_terms(
            source_rows, rel_rows, dest_vals, negatives
        )
        grad_dest = coef_pos[:, None] * query.astype(jnp.float32)
        spread = scatter_rows(grad_dest, flat, groups * shard_rows)
        dest_total = lax.psum_scatter(spread, "group", scatter_dimension=0, tiled=True)
        source_part = scatter_rows(grad_source, src, shard_rows)
        source_total = lax.psum(source_part, "member")
        neg_total = scatter_rows(grad_neg, neg, shard_rows)
        grads = dest_total + neg_total + jnp.where(member_index == root, source_total, 0.0)
        state = state + jnp.mean(grads * grads, -1)
        table = (table.astype(jnp.float32) - 1.0 * grads / jnp.sqrt(state)[:, None]).astype(
            jnp.bfloat16
        )
    return (table, state)


def solution(mesh):
    placed = (
        P(("group", "member"), None),
        P(("group", "member")),
        P(),
        P(None, ("group", "member")),
        P(None, ("group", "member")),
        P(None, ("group", "member"), None),
        P(None, ("group", "member")),
        P(None, ("group", "member")),
        P(),
    )
    return jax.shard_map(
        per_device,
        mesh=mesh,
        in_specs=placed,
        out_specs=(P(("group", "member"), None), P(("group", "member"))),
        check_vma=False,
    )
```

profile of v0, /device:TPU:0, one launch (start us, length us, event | category | flops | bytes accessed | tf_op | source)
XLA Modules:
  0.0 309.8 jit_solution(10393002538043568739)
XLA Ops:
  8.1 1.3 constant_dynamic-slice_fusion.1
  10.1 1.8 broadcast_select_fusion.9
  11.9 2.0 copy.15
  14.2 0.8 copy-done
  14.9 5.3 %gather_fusion.3 = bf16[1000,800]{1,0:T(8,128)(2,1)} fusion(bf16[256,800]{1,0:T(8,128)(2,1)S(1)} %copy-done, s32[1024]{0:T(1024)S(1)} %pad_clamp_fusion.4), kind=kCustom, calls=%fused_computation.3.clone | custom fusion | bytes 3204000 | tf_op jit(solution)/shard_map/jit(_take)/gather | solution.py:88
  20.2 3.4 %copy.13 = bf16[1345,800]{1,0:T(8,128)(2,1)S(1)} copy(bf16[1345,800]{0,1:T(8,128)(2,1)} %param.19) | data formatting | bytes 4304000 | tf_op args[2]
  23.7 2.1 gather_fusion.1
  25.7 1.2 copy.14
  27.1 40.9 %all-reduce.5.cloned.1.call-done = bf16[256,800]{0,1:T(8,128)(2,1)} async-done(((bf16[256,800]{0,1:T(8,128)(2,1)}), bf16[256,800]{0,1:T(8,128)(2,1)}) %all-reduce.5.cloned.1.call-update) | async-done | bytes 409616 | tf_op jit(solution)/shard_map/psum | solution.py:9
  68.0 1.2 copy.11
  69.2 2.7 gather_fusion
  72.0 2.2 copy.12
  74.2 1.4 select_convert_fusion.2
  76.1 0.7 copy-done.1
  76.8 0.8 copy-done.13
  77.7 2.7 fusion.44
  80.3 4.3 %gather_fusion.2 = bf16[512,800]{1,0:T(8,128)(2,1)S(1)} fusion(bf16[1024,800]{1,0:T(8,128)(2,1)} %all-gather.3.cloned.1.call-done, s32[1024]{0:T(1024)S(1)} %pad_clamp_fusion.5), kind=kCustom, calls=%fused_computation.2.clone | custom fusion | bytes 1640448 | tf_op jit(solution)/shard_map/jit(_take)/gather | solution.py:91
  84.6 1.3 copy.16
  85.9 1.8 fusion.4
  87.7 1.9 fusion.2
  89.7 3.0 fusion.5
  93.1 1.9 fusion.8
  95.3 4.7 %fusion = f32[1024,800]{0,1:T(8,128)} fusion(s32[512]{0:T(512)S(1)} %get-tuple-element.13, f32[512]{0:T(512)S(1)} %get-tuple-element.27, bf16[512,400]{0,1:T(8,128)(2,1)S(1)} %copy-done.16, bf16[512,400]{0,1:T(8,128)(2,1)S(1)} %copy-done.14), kind=kOutput, calls=%fused_computation.10 | convolution fusion | flops 5035737088 | bytes 4100096 | tf_op jit(solution)/shard_map/dot_general | solution.py:52
  100.7 4.6 %fusion.38 = f32[1000,800]{1,0:T(8,128)} fusion(bf16[512,400]{0,1:T(8,128)(2,1)S(1)} %copy-done.16, bf16[512,400]{0,1:T(8,128)(2,1)S(1)} %copy-done.14, f32[512,1000]{0,1:T(8,128)} %get-tuple-element.39, f32[512]{0:T(512)S(1)} %get-tuple-element.26, f32[512]{0:T(512)S(1)} %max.26), kind=kOutput, calls=%fused_computation.122 | convolution fusion | flops 822374400 | bytes 6071296 | tf_op jit(solution)/shard_map/dot_general | solution.py:44
  105.3 48.3 %all-reduce.7.cloned.1.call-done = f32[256,800]{0,1:T(8,128)} async-done(((f32[256,800]{0,1:T(8,128)}), f32[256,800]{0,1:T(8,128)}) %all-reduce.7.cloned.1.call-update) | async-done | bytes 819216 | tf_op jit(solution)/shard_map/psum | solution.py:99
  153.6 5.7 %multiply_reduce_fusion.1 = (f32[256]{0:T(256)S(1)}, f32[256,800]{0,1:T(8,128)S(1)}) fusion(f32[256,800]{0,1:T(8,128)} %all-reduce.7.cloned.1.call-done, pred[]{:T(512)S(6)} %eq.43, f32[256,800]{0,1:T(8,128)} %reduce-scatter.3.cloned.1.call-done, f32[1000,800]{1,0:T(8,128)} %fusion.38, s32[1000]{0:T(1024)S(1)} %bitcast.19), kind=kOutput, calls=%fused_computation.60 | convolution fusion | flops 2458879744 | bytes 5662625 | tf_op jit(solution)/shard_map/dot_general | solution.py:52
  159.3 1.1 broadcast_select_fusion.8
  161.3 2.1 gather_fusion.5
  163.4 1.3 copy.21
  164.7 1.3 select_convert_fusion
  166.3 5.2 %gather_fusion.7 = bf16[1000,800]{1,0:T(8,128)(2,1)} fusion(bf16[256,800]{1,0:T(8,128)(2,1)S(1)} %copy.24, s32[1024]{0:T(1024)S(1)} %pad_clamp_fusion), kind=kCustom, calls=%fused_computation.7.clone | custom fusion | bytes 3204000 | tf_op jit(solution)/shard_map/jit(_take)/gather | solution.py:88
  171.5 42.3 %all-reduce.9.cloned.1.call-done = bf16[256,800]{0,1:T(8,128)(2,1)} async-done(((bf16[256,800]{0,1:T(8,128)(2,1)}), bf16[256,800]{0,1:T(8,128)(2,1)}) %all-reduce.9.cloned.1.call-update) | async-done | bytes 409616 | tf_op jit(solution)/shard_map/psum | solution.py:9
  213.9 1.2 copy.18
  215.1 2.1 gather_fusion.4
  218.3 0.7 copy-done.17
  219.4 2.6 fusion.45
  222.0 3.0 copy.22
  225.0 2.8 gather_fusion.6
  227.8 1.5 copy.23
  229.6 2.1 fusion.3
  231.7 2.9 fusion.7
  235.0 2.0 fusion.12
  237.3 4.7 %fusion.1 = f32[1024,800]{0,1:T(8,128)} fusion(s32[512]{0:T(512)S(1)} %get-tuple-element.11, f32[512]{0:T(512)S(1)} %get-tuple-element.25, bf16[512,400]{0,1:T(8,128)(2,1)S(1)} %copy-done.20, bf16[512,400]{0,1:T(8,128)(2,1)S(1)} %copy-done.18), kind=kOutput, calls=%fused_computation.11 | convolution fusion | flops 5035737088 | bytes 4100096 | tf_op jit(solution)/shard_map/dot_general | solution.py:52
  242.0 1.5 copy-done.10
  243.5 3.0 fusion.37
  246.6 49.0 %all-reduce.11.cloned.1.call-done = f32[256,800]{0,1:T(8,128)} async-done(((f32[256,800]{0,1:T(8,128)}), f32[256,800]{0,1:T(8,128)}) %all-reduce.11.cloned.1.call-update) | async-done | bytes 819216 | tf_op jit(solution)/shard_map/psum | solution.py:99
  295.5 5.4 %multiply_reduce_fusion = (f32[256]{0:T(256)S(1)}, f32[256,800]{0,1:T(8,128)S(1)}) fusion(f32[256,800]{0,1:T(8,128)} %all-reduce.11.cloned.1.call-done, pred[]{:T(512)S(6)} %eq.99, f32[256,800]{0,1:T(8,128)} %reduce-scatter.5.cloned.1.call-done, f32[1000,800]{1,0:T(8,128)} %fusion.37, s32[1000]{0:T(1024)S(1)} %bitcast.16), kind=kOutput, calls=%fused_computation.53 | convolution fusion | flops 2458879744 | bytes 5662625 | tf_op jit(solution)/shard_map/dot_general | solution.py:52
  301.6 0.9 subtract_convert_fusion
  (112 shorter events, 5.9 us)
Async XLA Ops:
  8.0 6.0 %copy-start.23 = (s32[2,512]{1,0:T(2,128)S(1)}, s32[2,512]{1,0:T(2,128)}, u32[]{:S(2)}) copy-start(s32[2,512]{1,0:T(2,128)} %param.20) | copy-start | bytes 12292
  8.0 6.0 %copy-start.24 = (s32[2,512]{1,0:T(2,128)S(1)}, s32[2,512]{1,0:T(2,128)}, u32[]{:S(2)}) copy-start(s32[2,512]{1,0:T(2,128)} %param.21) | copy-start | bytes 12292
  8.0 6.1 %copy-start.25 = (s32[2,512,1]{1,2,0:T(1,128)S(1)}, s32[2,512,1]{1,2,0:T(1,128)}, u32[]{:S(2)}) copy-start(s32[2,512,1]{1,2,0:T(1,128)} %param.22) | copy-start | bytes 12292
  8.0 6.1 %copy-start.21 = (s32[2,1000]{1,0:T(2,128)S(1)}, s32[2,1000]{1,0:T(2,128)}, u32[]{:S(2)}) copy-start(s32[2,1000]{1,0:T(2,128)} %param.24) | copy-start | bytes 24004
  8.0 60.0 %all-reduce.5.cloned.1.call-start = ((), (), s32[]{:S(2)}) async-start(), calls=%async_computation.2 | async-start | bytes 819200 | tf_op jit(solution)/shard_map/psum | solution.py:9
  11.9 68.4 %all-gather.3.cloned.1.call-start = ((), (), s32[]{:S(2)}) async-start(), calls=%async_computation.3 | async-start | bytes 2293760 | tf_op jit(solution)/shard_map/all_gather | solution.py:89
  13.9 1.0 copy-start
  14.0 139.7 %all-reduce.7.cloned.1.call-start = ((), (), s32[]{:S(2)}) async-start(), calls=%async_computation.5 | async-start | bytes 1638400 | tf_op jit(solution)/shard_map/psum | solution.py:99
  23.7 3.3 %copy-start.26 = (s32[2,512]{1,0:T(2,128)S(1)}, s32[2,512]{1,0:T(2,128)}, u32[]{:S(2)}) copy-start(s32[2,512]{1,0:T(2,128)} %param.23) | copy-start | bytes 12292
  72.0 2.2 copy-start.7
  75.6 1.2 copy-start.1
  75.6 2.1 copy-start.11
  76.8 0.8 copy-start.13
  76.8 0.9 copy-start.15
  85.9 3.8 %copy-start.6 = (bf16[512,800]{0,1:T(8,128)(2,1)S(1)}, bf16[512,800]{0,1:T(8,128)(2,1)}, u32[]{:S(2)}) copy-start(bf16[512,800]{0,1:T(8,128)(2,1)} %copy.16) | copy-start | bytes 2457604
  85.9 3.8 %copy-start.8 = (f32[512,1000]{0,1:T(8,128)S(1)}, f32[512,1000]{0,1:T(8,128)}, u32[]{:S(2)}) copy-start(f32[512,1000]{0,1:T(8,128)} %get-tuple-element.39) | copy-start | bytes 6144004
  89.7 3.0 copy-start.2
  93.1 2.2 copy-start.14
  93.1 2.2 copy-start.16
  95.0 58.6 %reduce-scatter.3.cloned.1.call-start = ((), (), s32[]{:S(2)}) async-start(), calls=%async_computation.4 | async-start | bytes 4096000 | tf_op jit(solution)/shard_map/reduce_scatter | solution.py:97
  100.0 113.9 %all-reduce.9.cloned.1.call-start = ((), (), s32[]{:S(2)}) async-start(), calls=%async_computation.6 | async-start | bytes 819200 | tf_op jit(solution)/shard_map/psum | solution.py:9
  105.3 54.0 %copy-start.22 = (f32[256]{0:T(256)S(1)}, f32[256]{0:T(256)}, u32[]{:S(2)}) copy-start(f32[256]{0:T(256)} %param.18) | copy-start | bytes 3076
  105.3 54.0 %copy-start.5 = (bf16[256,800]{0,1:T(8,128)(2,1)S(1)}, bf16[256,800]{0,1:T(8,128)(2,1)}, u32[]{:S(2)}) copy-start(bf16[256,800]{0,1:T(8,128)(2,1)} %param.17) | copy-start | bytes 1228804
  160.4 61.6 %all-gather.5.cloned.1.call-start = ((), (), s32[]{:S(2)}) async-start(), calls=%async_computation.7 | async-start | bytes 2048000 | tf_op jit(solution)/shard_map/all_gather | solution.py:89
  161.0 134.5 %all-reduce.11.cloned.1.call-start = ((), (), s32[]{:S(2)}) async-start(), calls=%async_computation.9 | async-start | bytes 1638400 | tf_op jit(solution)/shard_map/psum | solution.py:99
  163.4 2.7 copy-start.3
  217.8 1.6 copy-start.12
  218.2 0.8 copy-start.17
  218.3 0.9 copy-start.19
  227.8 1.5 copy-start.18
  227.8 1.5 copy-start.20
  229.3 2.4 copy-start.9
  237.0 58.6 %reduce-scatter.5.cloned.1.call-start = ((), (), s32[]{:S(2)}) async-start(), calls=%async_computation.8 | async-start | bytes 4096000 | tf_op jit(solution)/shard_map/reduce_scatter | solution.py:97
  242.0 1.6 copy-start.10
  246.6 55.0 %copy-start.4 = (bf16[256,800]{0,1:T(8,128)(2,1)S(1)}, bf16[256,800]{0,1:T(8,128)(2,1)}, u32[]{:S(2)}) copy-start(bf16[256,800]{0,1:T(8,128)(2,1)} %get-tuple-element.9) | copy-start | bytes 1228804
Sparse Core Ops, SparseCore 0:
  12.0 55.9 all-reduce.4
  95.2 58.4 all-reduce.6
  160.6 53.2 all-reduce.8
  237.1 58.4 all-reduce.10
Sparse Core Ops, SparseCore 1:
  14.4 34.6 all-gather.2
  100.1 46.3 reduce-scatter.2
  162.9 31.0 all-gather.4
  242.1 46.3 reduce-scatter.4
where the time goes:
time: 311 us; the launch traced here: 310 us
  waiting for transfers between devices  181 us (58%)
  local copies, waits for them, and re-layouts  52.1 us (17%)
  matrix products  43.1 us (14%)
  between operations  17.3 us (6%)
  other arithmetic  15.1 us (5%)
    psum x2, waiting for transfers between devices, per_device(): source_total = lax.psum(source_part, 'member')  97.3 us
    psum x2, waiting for transfers between devices, broadcast(): return lax.psum(kept, axis)  83.3 us
    dot_general x6, matrix products, scatter_rows(): lax.dot_general(onehot, values, (((0,), (0,)), ((), ())), precision=lax.P...  24.4 us
    unnamed x56, local copies, waits for them, and re-layouts  10.6 us
    gather x2, local copies, waits for them, and re-layouts, per_device(): negatives = jnp.take(table, neg, axis=0)  10.5 us
    gather x4, local copies, waits for them, and re-layouts, per_device(): dest_vals = jnp.take(whole, flat, axis=0)  9.76 us
    dot_general x2, matrix products, edge_terms(): lax.dot_general(coef_neg, query, (((0,), (0,)), ((), ())), preferred_elem...  7.67 us
    gather x4, local copies, waits for them, and re-layouts, per_device(): source_rows = jnp.take(block, src, axis=0)  7.53 us
  transfers between devices with their start and end apart: 8, of which 4 were waited for; matrix products, arithmetic and copies ran while one was open for 19% of the time, Pallas kernels for 0%

commit v1 on v0

v1 whole, which is shorter than its diff:
```python
import functools

import jax
import jax.numpy as jnp
from jax import lax
from jax.experimental import pallas as pl
from jax.experimental.pallas import tpu as pltpu
from jax.sharding import PartitionSpec as P

BF = jnp.bfloat16
F32 = jnp.float32
LANES = 128
VMEM = pl.BlockSpec(memory_space=pltpu.VMEM)
SMEM = pl.BlockSpec(memory_space=pltpu.SMEM)
PARAMS = pltpu.CompilerParams(vmem_limit_bytes=14 * 1024 * 1024)


def call(body, outs, *args, smem=()):
    return pl.pallas_call(
        body,
        out_shape=outs,
        in_specs=[SMEM if i in smem else VMEM for i in range(len(args))],
        out_specs=[VMEM] * len(outs),
        compiler_params=PARAMS,
        cost_estimate=pl.CostEstimate(flops=1000, bytes_accessed=1000, transcendentals=0),
    )(*args)


def sds(shape, dtype):
    return jax.ShapeDtypeStruct(shape, dtype)


def onehot(row, count, base=0):
    sub = lax.broadcasted_iota(jnp.int32, (count, row.shape[1]), 0) + base
    return (sub == row).astype(F32).astype(BF)


def dot(a, b):
    return jnp.dot(a, b, preferred_element_type=F32)


def dot_t(a, b):
    return lax.dot_general(a, b, (((1,), (1,)), ((), ())), preferred_element_type=F32)


def dot_c(a, b):
    return lax.dot_general(a, b, (((0,), (0,)), ((), ())), preferred_element_type=F32)


def masks_body(owners, *outs):
    group, member = lax.axis_index("group"), lax.axis_index("member")
    per_step = len(outs) // owners.shape[0]
    for step in range(owners.shape[0]):
        root = owners[step, group]
        differ = root ^ member
        for index in range(per_step - 1):
            bit = (differ >> index) & 1
            outs[step * per_step + index][...] = jnp.full(outs[0].shape, bit, jnp.int32)
        outs[(step + 1) * per_step - 1][...] = jnp.full(outs[0].shape, (root == member).astype(jnp.int32))


def prepare_body(step, rel_ids, neg_ids, relation, tail, rel, counts):
    full = relation.shape[1] // LANES * LANES
    hot = onehot(rel_ids[step : step + 1, :], full + LANES)
    rel[...] = (dot(relation[:, :full], hot[:full]) + dot(tail[...], hot[full:])).astype(BF)
    negs = neg_ids[step : step + 1, :]
    sub = lax.broadcasted_iota(jnp.int32, (counts.shape[0], negs.shape[1]), 0)
    counts[...] = jnp.sum((sub == negs).astype(F32), 1, keepdims=True)


def query_body(step, src, real, imag, rel, table, counts, query, probs, top, total):
    rows, half = table.shape[1], real.shape[0]
    hot = onehot(src[step : step + 1, :], rows)
    sr, si = dot(real[...], hot), dot(imag[...], hot)
    rr, ri = rel[:half, :].astype(F32), rel[half:, :].astype(F32)
    query[:half, :] = (sr * rr - si * ri).astype(BF)
    query[half:, :] = (sr * ri + si * rr).astype(BF)
    scores = dot_c(table[...], query[...])
    count = counts[...]
    scores = jnp.where(count > 0.0, scores, -jnp.inf)
    best = jnp.max(scores, 0, keepdims=True)
    prob = count * jnp.exp(scores - best)
    probs[...] = prob
    top[...] = best
    total[...] = jnp.sum(prob, 0, keepdims=True)


def place(step, groups, count, rows, dest_groups, dest_rows, first=0):
    near = dest_groups[step] ^ lax.axis_index("group")
    return onehot(near * rows + dest_rows[step : step + 1, :], count * rows, first * rows)


def dest_body(step, groups, dest_groups, dest_rows, table, *refs):
    shards, dest = refs[:-1], refs[-1]
    hot = place(step, groups, groups - 1, table.shape[1], dest_groups, dest_rows)
    whole = jnp.concatenate([x[...] for x in (table, *shards)], 1)
    dest[...] = dot(whole, hot).astype(BF)


def source_body(
    step, groups, src, dest_groups, dest_rows, query, probs, top_neg, total_neg, rel, table, dest, far_r, far_i,
    out_r, out_i, coef_pos, coef_neg,
):
    rows, half = table.shape[1], out_r.shape[0]
    hot = place(step, groups, 1, rows, dest_groups, dest_rows, groups - 1)
    dr = dest[:half, :].astype(F32) + dot(far_r[...], hot)
    di = dest[half:, :].astype(F32) + dot(far_i[...], hot)
    qr, qi = query[:half, :].astype(F32), query[half:, :].astype(F32)
    positive = jnp.sum(qr * dr + qi * di, 0, keepdims=True)
    best = top_neg[...]
    top = jnp.maximum(best, positive)
    pos_exp = jnp.exp(positive - top)
    scale = jnp.exp(best - top)
    total = pos_exp + scale * total_neg[...]
    pos = pos_exp / total - 1.0
    neg = (probs[...] * (scale / total)).astype(BF)
    coef_pos[...] = pos
    coef_neg[...] = neg
    gr = pos * dr + dot(table[:half, :], neg)
    gi = pos * di + dot(table[half:, :], neg)
    rr, ri = rel[:half, :].astype(F32), rel[half:, :].astype(F32)
    back = onehot(src[step : step + 1, :], rows)
    out_r[...] = dot_t((gr * rr + gi * ri).astype(BF), back).astype(BF)
    out_i[...] = dot_t((gi * rr - gr * ri).astype(BF), back).astype(BF)


def spread_body(step, groups, dest_groups, dest_rows, query, coef_pos, coef_neg, base_grad, *sends):
    rows, half = base_grad.shape[1], base_grad.shape[0] // 2
    hot = place(step, groups, groups, rows, dest_groups, dest_rows)
    for part in (0, 1):
        span = slice(part * half, (part + 1) * half)
        q = query[span, :]
        spread = dot_t((coef_pos[...] * q.astype(F32)).astype(BF), hot)
        base_grad[span, :] = spread[:, :rows] + dot_t(q, coef_neg[...])
        grads = [spread[:, k * rows : (k + 1) * rows].astype(BF) for k in range(1, groups)]
        if groups == 4:
            sends[part][:half, :] = grads[2]
            sends[part][half:, :] = grads[part]
            sends[2 + part][...] = grads[1 - part]
        else:
            for send, grad in zip(sends, grads):
                send[span, :] = grad


def update_body(halves, table, state, base_grad, src_r, src_i, *refs):
    parts = refs[: len(halves)]
    new_table, new_state = refs[len(halves) :]
    width, half = table.shape[0], src_r.shape[0]
    grads = []
    for part, source in enumerate((src_r, src_i)):
        span = slice(part * half, (part + 1) * half)
        grad = base_grad[span, :] + source[...].astype(F32)
        for piece, held in zip(parts, halves):
            if held is None:
                grad = grad + piece[span, :].astype(F32)
            elif held == part:
                grad = grad + piece[...].astype(F32)
        grads.append(grad)
    square = sum(jnp.sum(g * g, 0, keepdims=True) for g in grads)
    after = state[...] + square * (1.0 / width)
    new_state[...] = after
    rate = lax.rsqrt(after)
    for part, grad in enumerate(grads):
        span = slice(part * half, (part + 1) * half)
        new_table[span, :] = (table[span, :].astype(F32) - grad * rate).astype(BF)


def add(a, b):
    return (a.astype(F32) + b.astype(F32)).astype(BF)


def shift(value, axis, bit):
    size = lax.axis_size(axis)
    return lax.ppermute(value, axis, [(i, i ^ bit) for i in range(size)])


def z_bits():
    bits = []
    bit = 2
    while bit < lax.axis_size("member"):
        bits.append(bit)
        bit *= 2
    return bits[::-1]


def after(value, *others):
    return lax.optimization_barrier((value, *others))[0]


def cut(value):
    at = (value.shape[0] // 2 + 15) // 16 * 16
    return [value[:at], value[at:]]


def gather_shards(table):
    groups, half = lax.axis_size("group"), table.shape[0] // 2
    near = [shift(table, "group", k) for k in range(1, groups - 1)]
    if groups != 4:
        far = [shift(table[:half], "group", groups - 1), shift(table[half:], "group", groups - 1)]
    else:
        far = [shift(near[0][:half], "group", 2), shift(near[1][half:], "group", 1)]
    return near + far


def spread_grads(sends):
    groups, half = lax.axis_size("group"), sends[0].shape[0] // 2
    if groups != 4:
        got = [shift(x, "group", k + 1) for k, x in enumerate(sends)]
        return got[:2], [(None, x) for x in got]
    x, y = shift(sends[0], "group", 1), shift(sends[1], "group", 2)
    y_real = shift(add(sends[2], x[:half]), "group", 2)
    x_imag = shift(add(sends[3], y[:half]), "group", 1)
    return [x, y], [(0, y_real), (1, x_imag), (0, x[half:]), (1, y[half:])]


def per_device(
    entity,
    adagrad_state,
    relation,
    source_ids,
    relation_ids,
    dest_groups,
    dest_rows,
    negative_ids,
    owners,
):
    groups = lax.axis_size("group")
    first = lax.axis_index("member") % 2 == 0
    steps, edges = source_ids.shape
    rows, width = entity.shape
    half = width // 2
    table = entity.T
    state = adagrad_state[None, :]
    rel_t = relation.T
    full = rel_t.shape[1] // LANES * LANES
    groups = lax.axis_size("group")
    dest_groups = jnp.transpose(dest_groups, (0, 2, 1))
    bits = z_bits()
    kinds = 2 + len(bits)

    def root_masks(owners):
        return call(masks_body, [sds((1, rows), jnp.int32)] * (steps * kinds), owners, smem=(0,))

    def prepare(step, earlier):
        held = after(rel_t, earlier)
        tail = jnp.pad(held[:, full:], ((0, 0), (0, LANES - rel_t.shape[1] + full)))
        return call(
            functools.partial(prepare_body, step),
            [sds((width, edges), BF), sds((rows, 1), F32)],
            relation_ids, negative_ids, held, tail,
        )

    for step in range(steps):
        real, imag = table[:half], table[half:]
        keep, give = jnp.where(first, real, imag), jnp.where(first, imag, real)
        if step == 0:
            keep, give = lax.optimization_barrier((keep, give))
            masks = root_masks(after(owners, give))
        mask = [x != 0 for x in masks[step * kinds : (step + 1) * kinds]]
        shards = gather_shards(table)
        held = jnp.where(mask[0], shift(give, "member", 1), keep)
        (dest,) = call(
            functools.partial(dest_body, step, groups),
            [sds((width, edges), BF)],
            dest_groups, dest_rows, table, *shards[:-2],
        )
        pieces = cut(held)
        for turn in range(len(bits)):
            if turn == 1:
                pieces[1] = after(pieces[1], *shards[:-2])
            for index, bit in enumerate((bits[turn], bits[-1 - turn])):
                got = shift(pieces[index], "member", bit)
                pieces[index] = jnp.where(mask[bit.bit_length() - 1], got, pieces[index])
        pieces[1] = after(pieces[1], shards[-1], dest)
        others = [shift(x, "member", 1) for x in pieces]
        block = [jnp.concatenate([jnp.where(first, x, y) for x, y in zip(*pair)], 0) for pair in ((pieces, others), (others, pieces))]
        if step == 0:
            rel, counts = prepare(0, pieces[0])
        query, probs, top, total = call(
            functools.partial(query_body, step),
            [sds((width, edges), BF), sds((rows, edges), F32), sds((1, edges), F32), sds((1, edges), F32)],
            source_ids, *block, rel, table, counts,
        )
        out_r, out_i, coef_pos, coef_neg = call(
            functools.partial(source_body, step, groups),
            [sds((half, rows), BF)] * 2 + [sds((1, edges), F32), sds((rows, edges), BF)],
            source_ids, dest_groups, dest_rows, query, probs, top, total, rel, table, dest, *shards[-2:],
        )
        give = shift(jnp.where(first, out_i, out_r), "member", 1)
        shapes = [(width, rows)] * 2 + [(half, rows)] * 2 if groups == 4 else [(width, rows)] * (groups - 1)
        base_grad, *sends = call(
            functools.partial(spread_body, step, groups),
            [sds((width, rows), F32)] + [sds(shape, BF) for shape in shapes],
            dest_groups, dest_rows, query, coef_pos, coef_neg,
        )
        early, parts = spread_grads(sends)
        part = add(jnp.where(first, out_r, out_i), give)
        pieces = cut(part)
        for turn in range(len(bits)):
            for index, bit in enumerate((bits[turn], bits[-1 - turn])):
                pieces[index] = add(pieces[index], shift(pieces[index], "member", bit))
            if turn == 0:
                if step + 1 < steps:
                    ahead = prepare(step + 1, pieces[0])
                    state = after(state, *ahead)
                pieces[1] = after(pieces[1], *early)
        pieces[1] = after(pieces[1], parts[0][1])
        others = [shift(x, "member", 1) for x in pieces]
        source = []
        for pair in ((pieces, others), (others, pieces)):
            both = jnp.concatenate([jnp.where(first, x, y) for x, y in zip(*pair)], 0)
            source.append(jnp.where(mask[-1], both, 0))
        table, state = call(
            functools.partial(update_body, [at for at, _ in parts]),
            [sds((width, rows), BF), sds((1, rows), F32)],
            table, state, base_grad, *source, *[p for _, p in parts],
        )
        if step + 1 < steps:
            rel, counts = ahead
    return (table.T, state[0])


def solution(mesh):
    placed = (
        P(("group", "member"), None),
        P(("group", "member")),
        P(),
        P(None, ("group", "member")),
        P(None, ("group", "member")),
        P(None, ("group", "member"), None),
        P(None, ("group", "member")),
        P(None, ("group", "member")),
        P(),
    )
    return jax.shard_map(
        per_device,
        mesh=mesh,
        in_specs=placed,
        out_specs=(P(("group", "member"), None), P(("group", "member"))),
        check_vma=False,
    )
```

time: 311 us -> 106 us (0.34)
  waiting for transfers between devices: 181 us -> 47 us
  local copies, waits for them, and re-layouts: 52.1 us -> 1.02 us
  matrix products: 43.1 us -> 0 us
  starting transfers between devices: 1 us -> 39 us
  between operations: 17.3 us -> 1.34 us
  Pallas kernels: 0 us -> 14.7 us
  other arithmetic: 15.1 us -> 2.51 us
    psum x4 -> x0, waiting for transfers between devices: 181 us -> none  [the longest x2 97.3 us: per_device(): source_total = lax.psum(source_part, 'member')]
    ppermute x0 -> x44, waiting for transfers between devices: none -> 47 us  [shift(): return lax.ppermute(value, axis, [(i, i ^ bit) for i in range(size)])]
    dot_general x12 -> x0, matrix products: 43.1 us -> none  [the longest x6 24.4 us: scatter_rows(): lax.dot_general(onehot, values, (((0,), (0,)), ((), ())), precision=lax.P...]
    ppermute x0 -> x44, starting transfers between devices: none -> 39 us  [shift(): return lax.ppermute(value, axis, [(i, i ^ bit) for i in range(size)])]
    gather x14 -> x0, local copies, waits for them, and re-layouts: 34.4 us -> none  [the longest x2 10.5 us: per_device(): negatives = jnp.take(table, neg, axis=0)]
    pallas_call x0 -> x13, Pallas kernels: none -> 14.7 us  [call(): pl.pallas_call(body, out_shape=outs, in_specs=[SMEM if i in smem else VME...]
    unnamed x56 -> x18, local copies, waits for them, and re-layouts: 10.6 us -> 0.72 us
    reduce_sum x4 -> x0, other arithmetic: 6.16 us -> none  [the longest x2 4.01 us: edge_terms(): total = pos_exp + jnp.sum(neg_exp, 1)]
  transfers between devices with their start and end apart: 8 -> 44, of which waited for: 4 -> 22; matrix products, arithmetic and copies ran while one was open for 19% -> 2% of each run, Pallas kernels for 0% -> 9%
where the time goes in v1:
time: 106 us
  waiting for transfers between devices  47 us (44%)
  starting transfers between devices  39 us (37%)
  Pallas kernels  14.7 us (14%)
  other arithmetic  2.51 us (2%)
  between operations  1.34 us (1%)
    ppermute x44, waiting for transfers between devices, shift(): return lax.ppermute(value, axis, [(i, i ^ bit) for i in range(size)])  47 us
    ppermute x44, starting transfers between devices, shift(): return lax.ppermute(value, axis, [(i, i ^ bit) for i in range(size)])  39 us
    pallas_call x13, Pallas kernels, call(): pl.pallas_call(body, out_shape=outs, in_specs=[SMEM if i in smem else VME...  14.7 us
  transfers between devices with their start and end apart: 44, of which 22 were waited for; matrix products, arithmetic and copies ran while one was open for 2% of the time, Pallas kernels for 9%

profile of v1, /device:TPU:0, one launch (start us, length us, event | category | flops | bytes accessed | tf_op | source)
XLA Modules:
  0.0 105.6 jit_solution(3673028231337076006)
XLA Ops:
  0.7 3.0 %collective-permute-start.6 = (bf16[800,256]{1,0:T(8,128)(2,1)}, bf16[800,256]{1,0:T(8,128)(2,1)S(1)}, u32[]{:S(2)}, u32[]{:S(2)}) collective-permute-start(bf16[800,256]{1,0:T(8,128)(2,1)} %bitcast.10), channel_id=1, source_target_pairs={{0,16},{8,24},{16,0},{24,8},{1,17},{9,25},{17,1},{25,9},{2,18},{10... | collective-permute-start | bytes 1228808 | tf_op jit(solution)/shard_map/ppermute | solution.py:174
  3.7 1.5 %collective-permute-start.5 = (bf16[800,256]{1,0:T(8,128)(2,1)}, bf16[800,256]{1,0:T(8,128)(2,1)S(1)}, u32[]{:S(2)}, u32[]{:S(2)}) collective-permute-start(bf16[800,256]{1,0:T(8,128)(2,1)} %bitcast.11), channel_id=1, source_target_pairs={{0,8},{8,0},{16,24},{24,16},{1,9},{9,1},{17,25},{25,17},{2,10},{10... | collective-permute-start | bytes 1228808 | tf_op jit(solution)/shard_map/ppermute | solution.py:174
  5.2 1.1 %broadcast_select_fusion.4 = (bf16[400,256]{1,0:T(8,128)(2,1)S(1)}, bf16[400,256]{1,0:T(8,128)(2,1)S(1)}) fusion(pred[]{:T(512)S(6)} %eq.5, bf16[800,256]{1,0:T(8,128)(2,1)} %bitcast.12), kind=kLoop, calls=%fused_computation.23 | loop fusion | flops 204800 | bytes 819201 | tf_op jit(solution)/shard_map/jit(_where)/select_n | solution.py:255
  7.8 2.7 %collective-permute-start.1 = (bf16[208,256]{1,0:T(8,128)(2,1)S(1)}, bf16[208,256]{1,0:T(8,128)(2,1)S(1)}, u32[]{:S(2)}, u32[]{:S(2)}) collective-permute-start(bf16[208,256]{1,0:T(8,128)(2,1)S(1)} %slice.106), channel_id=1, source_target_pairs={{0,4},{1,5},{2,6},{3,7},{4,0},{5,1},{6,2},{7,3},{8,12},{9,13},{10,... | collective-permute-start | bytes 319496 | tf_op jit(solution)/shard_map/ppermute | solution.py:174
  10.6 1.6 %collective-permute-start.4 = (bf16[192,256]{1,0:T(8,128)(2,1)S(1)}, bf16[192,256]{1,0:T(8,128)(2,1)S(1)}, u32[]{:S(2)}, u32[]{:S(2)}) collective-permute-start(bf16[192,256]{1,0:T(8,128)(2,1)S(1)} %slice.107), channel_id=1, source_target_pairs={{0,2},{1,3},{2,0},{3,1},{4,6},{5,7},{6,4},{7,5},{8,10},{9,11},{10,... | collective-permute-start | bytes 294920 | tf_op jit(solution)/shard_map/ppermute | solution.py:174
  12.2 4.2 %collective-permute-done.1 = bf16[208,256]{1,0:T(8,128)(2,1)S(1)} collective-permute-done((bf16[208,256]{1,0:T(8,128)(2,1)S(1)}, bf16[208,256]{1,0:T(8,128)(2,1)S(1)}, u32[]{:S(2)}, u32[]{:S(2)}) %collective-permute-start.1) | collective-permute-done | bytes 106528 | tf_op jit(solution)/shard_map/ppermute | solution.py:174
  17.7 3.4 %collective-permute-start.7 = (bf16[192,256]{1,0:T(8,128)(2,1)S(1)}, bf16[192,256]{1,0:T(8,128)(2,1)S(1)}, u32[]{:S(2)}, u32[]{:S(2)}) collective-permute-start(bf16[192,256]{1,0:T(8,128)(2,1)S(1)} %broadcast_select_fusion.20), channel_id=1, source_target_pairs={{0,4},{1,5},{2,6},{3,7},{4,0},{5,1},{6,2},{7,3},{8,12},{9,13},{10,... | collective-permute-start | bytes 294920 | tf_op jit(solution)/shard_map/ppermute | solution.py:174
  21.7 0.8 shard_map.105.dest
  22.8 1.4 %shard_map.106 = (bf16[800,512]{1,0:T(8,128)(2,1)S(1)}, f32[256,1]{1,0:T(8,128)S(1)}) custom-call(s32[2,512]{1,0:T(2,128)S(1)} %copy-done.6, s32[2,1000]{1,0:T(2,128)S(1)} %copy-done.5, bf16[800,1345]{1,0:T(8,128)(2,1)S(1)} %bitcast.7, bf16[800,128]{1,0:T(8,128)(2,1)S(1)} %pad.7.tail), custom_call_target="tpu_custom_call" | custom-call | flops 1000 | bytes 1000 | tf_op jit(solution)/shard_map/pallas_call | solution.py:19
  24.2 1.5 %collective-permute-done.7 = bf16[192,256]{1,0:T(8,128)(2,1)S(1)} collective-permute-done((bf16[192,256]{1,0:T(8,128)(2,1)S(1)}, bf16[192,256]{1,0:T(8,128)(2,1)S(1)}, u32[]{:S(2)}, u32[]{:S(2)}) %collective-permute-start.7) | collective-permute-done | bytes 98336 | tf_op jit(solution)/shard_map/ppermute | solution.py:174
  25.9 1.2 %collective-permute-done.9 = bf16[192,256]{1,0:T(8,128)(2,1)S(1)} collective-permute-done((bf16[192,256]{1,0:T(8,128)(2,1)S(1)}, bf16[192,256]{1,0:T(8,128)(2,1)S(1)}, u32[]{:S(2)}, u32[]{:S(2)}) %collective-permute-start.9) | collective-permute-done | bytes 98336 | tf_op jit(solution)/shard_map/ppermute | solution.py:174
  27.2 1.1 %shard_map.107 = (bf16[800,512]{1,0:T(8,128)(2,1)S(1)}, f32[256,512]{1,0:T(8,128)S(1)}, f32[1,512]{1,0:T(1,128)S(1)}, f32[1,512]{1,0:T(1,128)S(1)}) custom-call(s32[2,512]{1,0:T(2,128)S(1)} %copy-done.4, bf16[400,256]{1,0:T(8,128)(2,1)S(1)} %get-tuple-element.136.real, bf16[400,256]{1,0:T(8,128)(2,1)S(1)} %get-tuple-element.137.imag, ...), custom_call_target="tpu_custom_call" | custom-call | flops 1000 | bytes 1000 | tf_op jit(solution)/shard_map/pallas_call | solution.py:19
  28.3 1.4 %shard_map.108 = (bf16[400,256]{1,0:T(8,128)(2,1)S(1)}, bf16[400,256]{1,0:T(8,128)(2,1)S(1)}, f32[1,512]{1,0:T(1,128)S(1)}, bf16[256,512]{1,0:T(8,128)(2,1)S(1)}) custom-call(s32[2,512]{1,0:T(2,128)S(1)} %copy-done.4, s32[2,1,512]{2,1,0:T(1,128)S(1)} %bitcast.18, s32[2,512]{1,0:T(2,128)S(1)} %copy-done.3, bf16[800,512]{1,0:T(8,128)(2,1)S(1)} %get-tuple-element.69.query, ...), custom_call_target="tpu_custom_call" | custom-call | flops 1000 | bytes 1000 | tf_op jit(solution)/shard_map/pallas_call | solution.py:19
  30.0 1.3 %collective-permute-done.11 = bf16[400,256]{1,0:T(8,128)(2,1)S(1)} collective-permute-done((bf16[400,256]{1,0:T(8,128)(2,1)S(1)}, bf16[400,256]{1,0:T(8,128)(2,1)S(1)}, u32[]{:S(2)}, u32[]{:S(2)}) %collective-permute-start.11) | collective-permute-done | bytes 204832 | tf_op jit(solution)/shard_map/ppermute | solution.py:174
  31.6 1.3 %shard_map.110 = (f32[800,256]{1,0:T(8,128)S(1)}, bf16[800,256]{1,0:T(8,128)(2,1)S(1)}, bf16[800,256]{1,0:T(8,128)(2,1)S(1)}, bf16[400,256]{1,0:T(8,128)(2,1)S(1)}, bf16[400,256]{1,0:T(8,128)(2,1)S(1)}) custom-call(s32[2,1,512]{2,1,0:T(1,128)S(1)} %bitcast.19, s32[2,512]{1,0:T(2,128)S(1)} %copy-done.3, bf16[800,512]{1,0:T(8,128)(2,1)S(1)} %get-tuple-element.69.query, ...), custom_call_target="tpu_custom_call" | custom-call | flops 1000 | bytes 1000 | tf_op jit(solution)/shard_map/pallas_call | solution.py:19
  33.0 1.4 %collective-permute-start.16 = (bf16[800,256]{1,0:T(8,128)(2,1)S(1)}, bf16[800,256]{1,0:T(8,128)(2,1)S(1)}, u32[]{:S(2)}, u32[]{:S(2)}) collective-permute-start(bf16[800,256]{1,0:T(8,128)(2,1)S(1)} %get-tuple-element.83), channel_id=1, source_target_pairs={{0,8},{8,0},{16,24},{24,16},{1,9},{9,1},{17,25},{25,17},{2,10},{10... | collective-permute-start | bytes 1228808 | tf_op jit(solution)/shard_map/ppermute | solution.py:174
  34.9 3.1 %collective-permute-start.12 = (bf16[208,256]{1,0:T(8,128)(2,1)S(1)}, bf16[208,256]{1,0:T(8,128)(2,1)S(1)}, u32[]{:S(2)}, u32[]{:S(2)}) collective-permute-start(bf16[208,256]{1,0:T(8,128)(2,1)S(1)} %slice.110), channel_id=1, source_target_pairs={{0,4},{1,5},{2,6},{3,7},{4,0},{5,1},{6,2},{7,3},{8,12},{9,13},{10,... | collective-permute-start | bytes 319496 | tf_op jit(solution)/shard_map/ppermute | solution.py:174
  38.0 4.8 %collective-permute-done.12 = bf16[208,256]{1,0:T(8,128)(2,1)S(1)} collective-permute-done((bf16[208,256]{1,0:T(8,128)(2,1)S(1)}, bf16[208,256]{1,0:T(8,128)(2,1)S(1)}, u32[]{:S(2)}, u32[]{:S(2)}) %collective-permute-start.12) | collective-permute-done | bytes 106528 | tf_op jit(solution)/shard_map/ppermute | solution.py:174
  43.0 1.4 %shard_map.109 = (bf16[800,512]{1,0:T(8,128)(2,1)S(1)}, f32[256,1]{1,0:T(8,128)S(1)}) custom-call(s32[2,512]{1,0:T(2,128)S(1)} %copy-done.6, s32[2,1000]{1,0:T(2,128)S(1)} %copy-done.5, bf16[800,1345]{1,0:T(8,128)(2,1)S(1)} %bitcast.9, bf16[800,128]{1,0:T(8,128)(2,1)S(1)} %pad.8.tail), custom_call_target="tpu_custom_call" | custom-call | flops 1000 | bytes 1000 | tf_op jit(solution)/shard_map/pallas_call | solution.py:19
  44.5 1.6 %collective-permute-start.19 = (bf16[400,256]{1,0:T(8,128)(2,1)S(1)}, bf16[400,256]{1,0:T(8,128)(2,1)S(1)}, u32[]{:S(2)}, u32[]{:S(2)}) collective-permute-start(bf16[400,256]{1,0:T(8,128)(2,1)S(1)} %add_convert_fusion.4), channel_id=1, source_target_pairs={{0,16},{8,24},{16,0},{24,8},{1,17},{9,25},{17,1},{25,9},{2,18},{10... | collective-permute-start | bytes 614408 | tf_op jit(solution)/shard_map/ppermute | solution.py:174
  46.1 2.9 %collective-permute-start.18 = (bf16[192,256]{1,0:T(8,128)(2,1)S(1)}, bf16[192,256]{1,0:T(8,128)(2,1)S(1)}, u32[]{:S(2)}, u32[]{:S(2)}) collective-permute-start(bf16[192,256]{1,0:T(8,128)(2,1)S(1)} %add_convert_fusion.13), channel_id=1, source_target_pairs={{0,4},{1,5},{2,6},{3,7},{4,0},{5,1},{6,2},{7,3},{8,12},{9,13},{10,... | collective-permute-start | bytes 294920 | tf_op jit(solution)/shard_map/ppermute | solution.py:174
  50.0 1.7 %collective-permute-done.18 = bf16[192,256]{1,0:T(8,128)(2,1)S(1)} collective-permute-done((bf16[192,256]{1,0:T(8,128)(2,1)S(1)}, bf16[192,256]{1,0:T(8,128)(2,1)S(1)}, u32[]{:S(2)}, u32[]{:S(2)}) %collective-permute-start.18) | collective-permute-done | bytes 98336 | tf_op jit(solution)/shard_map/ppermute | solution.py:174
  51.8 1.2 %collective-permute-done.20 = bf16[192,256]{1,0:T(8,128)(2,1)S(1)} collective-permute-done((bf16[192,256]{1,0:T(8,128)(2,1)S(1)}, bf16[192,256]{1,0:T(8,128)(2,1)S(1)}, u32[]{:S(2)}, u32[]{:S(2)}) %collective-permute-start.20) | collective-permute-done | bytes 98336 | tf_op jit(solution)/shard_map/ppermute | solution.py:174
  53.2 1.8 %collective-permute-done.21.refs_1_ = bf16[400,256]{1,0:T(8,128)(2,1)S(1)} collective-permute-done((bf16[400,256]{1,0:T(8,128)(2,1)S(1)}, bf16[400,256]{1,0:T(8,128)(2,1)S(1)}, u32[]{:S(2)}, u32[]{:S(2)}) %collective-permute-start.21) | collective-permute-done | bytes 204832 | tf_op jit(solution)/shard_map/ppermute | solution.py:174
  55.5 1.4 %collective-permute-done.22 = bf16[400,256]{1,0:T(8,128)(2,1)S(1)} collective-permute-done((bf16[400,256]{1,0:T(8,128)(2,1)S(1)}, bf16[400,256]{1,0:T(8,128)(2,1)S(1)}, u32[]{:S(2)}, u32[]{:S(2)}) %collective-permute-start.22) | collective-permute-done | bytes 204832 | tf_op jit(solution)/shard_map/ppermute | solution.py:174
  57.0 1.2 %collective-permute-start.23 = (bf16[208,256]{1,0:T(8,128)(2,1)S(1)}, bf16[208,256]{1,0:T(8,128)(2,1)S(1)}, u32[]{:S(2)}, u32[]{:S(2)}) collective-permute-start(bf16[208,256]{1,0:T(8,128)(2,1)S(1)} %slice.116), channel_id=1, source_target_pairs={{0,4},{1,5},{2,6},{3,7},{4,0},{5,1},{6,2},{7,3},{8,12},{9,13},{10,... | collective-permute-start | bytes 319496 | tf_op jit(solution)/shard_map/ppermute | solution.py:174
  58.8 1.3 %collective-permute-start.27 = (bf16[800,256]{1,0:T(8,128)(2,1)S(1)}, bf16[800,256]{1,0:T(8,128)(2,1)S(1)}, u32[]{:S(2)}, u32[]{:S(2)}) collective-permute-start(bf16[800,256]{1,0:T(8,128)(2,1)S(1)} %get-tuple-element.89.table), channel_id=1, source_target_pairs={{0,8},{8,0},{16,24},{24,16},{1,9},{9,1},{17,25},{25,17},{2,10},{10... | collective-permute-start | bytes 1228808 | tf_op jit(solution)/shard_map/ppermute | solution.py:174
  60.8 4.2 %collective-permute-done.23 = bf16[208,256]{1,0:T(8,128)(2,1)S(1)} collective-permute-done((bf16[208,256]{1,0:T(8,128)(2,1)S(1)}, bf16[208,256]{1,0:T(8,128)(2,1)S(1)}, u32[]{:S(2)}, u32[]{:S(2)}) %collective-permute-start.23) | collective-permute-done | bytes 106528 | tf_op jit(solution)/shard_map/ppermute | solution.py:174
  65.1 1.2 %collective-permute-done.26 = bf16[192,256]{1,0:T(8,128)(2,1)S(1)} collective-permute-done((bf16[192,256]{1,0:T(8,128)(2,1)S(1)}, bf16[192,256]{1,0:T(8,128)(2,1)S(1)}, u32[]{:S(2)}, u32[]{:S(2)}) %collective-permute-start.26) | collective-permute-done | bytes 98336 | tf_op jit(solution)/shard_map/ppermute | solution.py:174
  66.4 3.2 %collective-permute-done.28.refs_1_ = bf16[800,256]{1,0:T(8,128)(2,1)S(1)} collective-permute-done((bf16[800,256]{1,0:T(8,128)(2,1)S(1)}, bf16[800,256]{1,0:T(8,128)(2,1)S(1)}, u32[]{:S(2)}, u32[]{:S(2)}) %collective-permute-start.28) | collective-permute-done | bytes 409632 | tf_op jit(solution)/shard_map/ppermute | solution.py:174
  70.3 1.7 %collective-permute-start.29 = (bf16[192,256]{1,0:T(8,128)(2,1)S(1)}, bf16[192,256]{1,0:T(8,128)(2,1)S(1)}, u32[]{:S(2)}, u32[]{:S(2)}) collective-permute-start(bf16[192,256]{1,0:T(8,128)(2,1)S(1)} %broadcast_select_fusion.18), channel_id=1, source_target_pairs={{0,4},{1,5},{2,6},{3,7},{4,0},{5,1},{6,2},{7,3},{8,12},{9,13},{10,... | collective-permute-start | bytes 294920 | tf_op jit(solution)/shard_map/ppermute | solution.py:174
  72.0 1.2 %collective-permute-start.32 = (bf16[400,256]{1,0:T(8,128)(2,1)S(1)}, bf16[400,256]{1,0:T(8,128)(2,1)S(1)}, u32[]{:S(2)}, u32[]{:S(2)}) collective-permute-start(bf16[400,256]{1,0:T(8,128)(2,1)S(1)} %slice.119), channel_id=1, source_target_pairs={{0,16},{8,24},{16,0},{24,8},{1,17},{9,25},{17,1},{25,9},{2,18},{10... | collective-permute-start | bytes 614408 | tf_op jit(solution)/shard_map/ppermute | solution.py:174
  73.2 0.8 shard_map.112.dest
  74.1 2.7 %collective-permute-done.29 = bf16[192,256]{1,0:T(8,128)(2,1)S(1)} collective-permute-done((bf16[192,256]{1,0:T(8,128)(2,1)S(1)}, bf16[192,256]{1,0:T(8,128)(2,1)S(1)}, u32[]{:S(2)}, u32[]{:S(2)}) %collective-permute-start.29) | collective-permute-done | bytes 98336 | tf_op jit(solution)/shard_map/ppermute | solution.py:174
  77.0 1.2 %collective-permute-done.31 = bf16[192,256]{1,0:T(8,128)(2,1)S(1)} collective-permute-done((bf16[192,256]{1,0:T(8,128)(2,1)S(1)}, bf16[192,256]{1,0:T(8,128)(2,1)S(1)}, u32[]{:S(2)}, u32[]{:S(2)}) %collective-permute-start.31) | collective-permute-done | bytes 98336 | tf_op jit(solution)/shard_map/ppermute | solution.py:174
  78.3 1.2 %shard_map.113 = (bf16[800,512]{1,0:T(8,128)(2,1)S(1)}, f32[256,512]{1,0:T(8,128)S(1)}, f32[1,512]{1,0:T(1,128)S(1)}, f32[1,512]{1,0:T(1,128)S(1)}) custom-call(s32[2,512]{1,0:T(2,128)S(1)} %copy-done.4, bf16[400,256]{1,0:T(8,128)(2,1)S(1)} %pad_maximum_fusion.2.real, bf16[400,256]{1,0:T(8,128)(2,1)S(1)} %pad_maximum_fusion.3.imag, ...), custom_call_target="tpu_custom_call" | custom-call | flops 1000 | bytes 1000 | tf_op jit(solution)/shard_map/pallas_call | solution.py:19
  79.5 1.7 %shard_map.114 = (bf16[400,256]{1,0:T(8,128)(2,1)S(1)}, bf16[400,256]{1,0:T(8,128)(2,1)S(1)}, f32[1,512]{1,0:T(1,128)S(1)}, bf16[256,512]{1,0:T(8,128)(2,1)S(1)}) custom-call(s32[2,512]{1,0:T(2,128)S(1)} %copy-done.4, s32[2,1,512]{2,1,0:T(1,128)S(1)} %bitcast.21, s32[2,512]{1,0:T(2,128)S(1)} %copy-done.3, bf16[800,512]{1,0:T(8,128)(2,1)S(1)} %get-tuple-element.96.query, ...), custom_call_target="tpu_custom_call" | custom-call | flops 1000 | bytes 1000 | tf_op jit(solution)/shard_map/pallas_call | solution.py:19
  81.4 1.3 %collective-permute-done.33 = bf16[400,256]{1,0:T(8,128)(2,1)S(1)} collective-permute-done((bf16[400,256]{1,0:T(8,128)(2,1)S(1)}, bf16[400,256]{1,0:T(8,128)(2,1)S(1)}, u32[]{:S(2)}, u32[]{:S(2)}) %collective-permute-start.33) | collective-permute-done | bytes 204832 | tf_op jit(solution)/shard_map/ppermute | solution.py:174
  82.9 1.3 %shard_map.115 = (f32[800,256]{1,0:T(8,128)S(1)}, bf16[800,256]{1,0:T(8,128)(2,1)S(1)}, bf16[800,256]{1,0:T(8,128)(2,1)S(1)}, bf16[400,256]{1,0:T(8,128)(2,1)S(1)}, bf16[400,256]{1,0:T(8,128)(2,1)S(1)}) custom-call(s32[2,1,512]{2,1,0:T(1,128)S(1)} %bitcast.22, s32[2,512]{1,0:T(2,128)S(1)} %copy-done.3, bf16[800,512]{1,0:T(8,128)(2,1)S(1)} %get-tuple-element.96.query, ...), custom_call_target="tpu_custom_call" | custom-call | flops 1000 | bytes 1000 | tf_op jit(solution)/shard_map/pallas_call | solution.py:19
  84.2 1.4 %collective-permute-start.38 = (bf16[800,256]{1,0:T(8,128)(2,1)S(1)}, bf16[800,256]{1,0:T(8,128)(2,1)S(1)}, u32[]{:S(2)}, u32[]{:S(2)}) collective-permute-start(bf16[800,256]{1,0:T(8,128)(2,1)S(1)} %get-tuple-element.106), channel_id=1, source_target_pairs={{0,8},{8,0},{16,24},{24,16},{1,9},{9,1},{17,25},{25,17},{2,10},{10... | collective-permute-start | bytes 1228808 | tf_op jit(solution)/shard_map/ppermute | solution.py:174
  86.2 1.0 collective-permute-start.34
  87.7 6.3 %collective-permute-done.34 = bf16[208,256]{1,0:T(8,128)(2,1)S(1)} collective-permute-done((bf16[208,256]{1,0:T(8,128)(2,1)S(1)}, bf16[208,256]{1,0:T(8,128)(2,1)S(1)}, u32[]{:S(2)}, u32[]{:S(2)}) %collective-permute-start.34) | collective-permute-done | bytes 106528 | tf_op jit(solution)/shard_map/ppermute | solution.py:174
  94.2 1.7 %collective-permute-done.38 = bf16[800,256]{1,0:T(8,128)(2,1)S(1)} collective-permute-done((bf16[800,256]{1,0:T(8,128)(2,1)S(1)}, bf16[800,256]{1,0:T(8,128)(2,1)S(1)}, u32[]{:S(2)}, u32[]{:S(2)}) %collective-permute-start.38) | collective-permute-done | bytes 409632 | tf_op jit(solution)/shard_map/ppermute | solution.py:174
  95.9 1.2 %collective-permute-start.41 = (bf16[400,256]{1,0:T(8,128)(2,1)S(1)}, bf16[400,256]{1,0:T(8,128)(2,1)S(1)}, u32[]{:S(2)}, u32[]{:S(2)}) collective-permute-start(bf16[400,256]{1,0:T(8,128)(2,1)S(1)} %add_convert_fusion.1), channel_id=1, source_target_pairs={{0,16},{8,24},{16,0},{24,8},{1,17},{9,25},{17,1},{25,9},{2,18},{10... | collective-permute-start | bytes 614408 | tf_op jit(solution)/shard_map/ppermute | solution.py:174
  97.9 0.8 collective-permute-start.43
  99.0 3.9 %collective-permute-done.40 = bf16[192,256]{1,0:T(8,128)(2,1)S(1)} collective-permute-done((bf16[192,256]{1,0:T(8,128)(2,1)S(1)}, bf16[192,256]{1,0:T(8,128)(2,1)S(1)}, u32[]{:S(2)}, u32[]{:S(2)}) %collective-permute-start.40) | collective-permute-done | bytes 98336 | tf_op jit(solution)/shard_map/ppermute | solution.py:174
  103.0 1.2 %collective-permute-done.42 = bf16[192,256]{1,0:T(8,128)(2,1)S(1)} collective-permute-done((bf16[192,256]{1,0:T(8,128)(2,1)S(1)}, bf16[192,256]{1,0:T(8,128)(2,1)S(1)}, u32[]{:S(2)}, u32[]{:S(2)}) %collective-permute-start.42) | collective-permute-done | bytes 98336 | tf_op jit(solution)/shard_map/ppermute | solution.py:174
  104.3 1.2 %shard_map.116 = (bf16[800,256]{1,0:T(8,128)(2,1)}, f32[1,256]{1,0:T(1,128)}) custom-call(bf16[800,256]{1,0:T(8,128)(2,1)S(1)} %get-tuple-element.89.table, f32[1,256]{1,0:T(1,128)S(1)} %get-tuple-element.90.state, f32[800,256]{1,0:T(8,128)S(1)} %get-tuple-element.102.base_grad, bf16[400,256]{1,0:T(8,128)(2,1)S(1)} %get-tuple-element.133.src_r, ...), custom_call_target="tpu_custom_call" | custom-call | flops 1000 | bytes 1000 | tf_op jit(solution)/shard_map/pallas_call | solution.py:19
  (140 shorter events, 12.1 us)
Async XLA Ops:
  0.6 21.1 %copy-start.1 = (bf16[256,800]{0,1:T(8,128)(2,1)S(1)}, bf16[256,800]{0,1:T(8,128)(2,1)}, u32[]{:S(2)}) copy-start(bf16[256,800]{0,1:T(8,128)(2,1)} %param.9) | copy-start | bytes 1228804
  0.6 21.1 %copy-start.3 = (s32[2,512]{1,0:T(2,128)S(1)}, s32[2,512]{1,0:T(2,128)}, u32[]{:S(2)}) copy-start(s32[2,512]{1,0:T(2,128)} %dest_rows.11) | copy-start | bytes 12292
  0.6 21.1 %copy-start.2 = (s32[2,512,1]{1,2,0:T(1,128)S(1)}, s32[2,512,1]{1,2,0:T(1,128)}, u32[]{:S(2)}) copy-start(s32[2,512,1]{1,2,0:T(1,128)} %param.14) | copy-start | bytes 12292
  0.7 16.5 %collective-permute-start.6 = (bf16[800,256]{1,0:T(8,128)(2,1)}, bf16[800,256]{1,0:T(8,128)(2,1)S(1)}, u32[]{:S(2)}, u32[]{:S(2)}) collective-permute-start(bf16[800,256]{1,0:T(8,128)(2,1)} %bitcast.10), channel_id=1, source_target_pairs={{0,16},{8,24},{16,0},{24,8},{1,17},{9,25},{17,1},{25,9},{2,18},{10... | collective-permute-start | bytes 1228808 | tf_op jit(solution)/shard_map/ppermute | solution.py:174
  3.7 14.1 %collective-permute-start.5 = (bf16[800,256]{1,0:T(8,128)(2,1)}, bf16[800,256]{1,0:T(8,128)(2,1)S(1)}, u32[]{:S(2)}, u32[]{:S(2)}) collective-permute-start(bf16[800,256]{1,0:T(8,128)(2,1)} %bitcast.11), channel_id=1, source_target_pairs={{0,8},{8,0},{16,24},{24,16},{1,9},{9,1},{17,25},{25,17},{2,10},{10... | collective-permute-start | bytes 1228808 | tf_op jit(solution)/shard_map/ppermute | solution.py:174
  6.2 1.5 %collective-permute-start = (bf16[400,256]{1,0:T(8,128)(2,1)S(1)}, bf16[400,256]{1,0:T(8,128)(2,1)S(1)}, u32[]{:S(2)}, u32[]{:S(2)}) collective-permute-start(bf16[400,256]{1,0:T(8,128)(2,1)S(1)} %get-tuple-element.58), channel_id=1, source_target_pairs={{0,1},{1,0},{2,3},{3,2},{4,5},{5,4},{6,7},{7,6},{8,9},{9,8},{10,11... | collective-permute-start | bytes 614408 | tf_op jit(solution)/shard_map/ppermute | solution.py:174
  7.8 14.8 %copy-start = (bf16[1345,800]{0,1:T(8,128)(2,1)S(1)}, bf16[1345,800]{0,1:T(8,128)(2,1)}, u32[]{:S(2)}) copy-start(bf16[1345,800]{0,1:T(8,128)(2,1)} %param.11) | copy-start | bytes 6456004
  7.8 8.6 %collective-permute-start.1 = (bf16[208,256]{1,0:T(8,128)(2,1)S(1)}, bf16[208,256]{1,0:T(8,128)(2,1)S(1)}, u32[]{:S(2)}, u32[]{:S(2)}) collective-permute-start(bf16[208,256]{1,0:T(8,128)(2,1)S(1)} %slice.106), channel_id=1, source_target_pairs={{0,4},{1,5},{2,6},{3,7},{4,0},{5,1},{6,2},{7,3},{8,12},{9,13},{10,... | collective-permute-start | bytes 319496 | tf_op jit(solution)/shard_map/ppermute | solution.py:174
  10.6 6.5 %collective-permute-start.4 = (bf16[192,256]{1,0:T(8,128)(2,1)S(1)}, bf16[192,256]{1,0:T(8,128)(2,1)S(1)}, u32[]{:S(2)}, u32[]{:S(2)}) collective-permute-start(bf16[192,256]{1,0:T(8,128)(2,1)S(1)} %slice.107), channel_id=1, source_target_pairs={{0,2},{1,3},{2,0},{3,1},{4,6},{5,7},{6,4},{7,5},{8,10},{9,11},{10,... | collective-permute-start | bytes 294920 | tf_op jit(solution)/shard_map/ppermute | solution.py:174
  16.4 6.1 %collective-permute-start.2 = (bf16[208,256]{1,0:T(8,128)(2,1)S(1)}, bf16[208,256]{1,0:T(8,128)(2,1)S(1)}, u32[]{:S(2)}, u32[]{:S(2)}) collective-permute-start(bf16[208,256]{1,0:T(8,128)(2,1)S(1)} %broadcast_select_fusion.8), channel_id=1, source_target_pairs={{0,2},{1,3},{2,0},{3,1},{4,6},{5,7},{6,4},{7,5},{8,10},{9,11},{10,... | collective-permute-start | bytes 319496 | tf_op jit(solution)/shard_map/ppermute | solution.py:174
  17.1 8.6 %collective-permute-start.8 = (bf16[400,256]{1,0:T(8,128)(2,1)S(1)}, bf16[400,256]{1,0:T(8,128)(2,1)S(1)}, u32[]{:S(2)}, u32[]{:S(2)}) collective-permute-start(bf16[400,256]{1,0:T(8,128)(2,1)S(1)} %slice.108), channel_id=1, source_target_pairs={{0,8},{8,0},{16,24},{24,16},{1,9},{9,1},{17,25},{25,17},{2,10},{10... | collective-permute-start | bytes 614408 | tf_op jit(solution)/shard_map/ppermute | solution.py:174
  17.7 8.0 %collective-permute-start.7 = (bf16[192,256]{1,0:T(8,128)(2,1)S(1)}, bf16[192,256]{1,0:T(8,128)(2,1)S(1)}, u32[]{:S(2)}, u32[]{:S(2)}) collective-permute-start(bf16[192,256]{1,0:T(8,128)(2,1)S(1)} %broadcast_select_fusion.20), channel_id=1, source_target_pairs={{0,4},{1,5},{2,6},{3,7},{4,0},{5,1},{6,2},{7,3},{8,12},{9,13},{10,... | collective-permute-start | bytes 294920 | tf_op jit(solution)/shard_map/ppermute | solution.py:174
  21.1 7.2 %collective-permute-start.10 = (bf16[400,256]{1,0:T(8,128)(2,1)S(1)}, bf16[400,256]{1,0:T(8,128)(2,1)S(1)}, u32[]{:S(2)}, u32[]{:S(2)}) collective-permute-start(bf16[400,256]{1,0:T(8,128)(2,1)S(1)} %slice.109), channel_id=1, source_target_pairs={{0,16},{8,24},{16,0},{24,8},{1,17},{9,25},{17,1},{25,9},{2,18},{10... | collective-permute-start | bytes 614408 | tf_op jit(solution)/shard_map/ppermute | solution.py:174
  22.6 3.3 %collective-permute-start.3 = (bf16[208,256]{1,0:T(8,128)(2,1)S(1)}, bf16[208,256]{1,0:T(8,128)(2,1)S(1)}, u32[]{:S(2)}, u32[]{:S(2)}) collective-permute-start(bf16[208,256]{1,0:T(8,128)(2,1)S(1)} %broadcast_select_fusion.9), channel_id=1, source_target_pairs={{0,1},{1,0},{2,3},{3,2},{4,5},{5,4},{6,7},{7,6},{8,9},{9,8},{10,11... | collective-permute-start | bytes 319496 | tf_op jit(solution)/shard_map/ppermute | solution.py:174
  25.8 1.4 %collective-permute-start.9 = (bf16[192,256]{1,0:T(8,128)(2,1)S(1)}, bf16[192,256]{1,0:T(8,128)(2,1)S(1)}, u32[]{:S(2)}, u32[]{:S(2)}) collective-permute-start(bf16[192,256]{1,0:T(8,128)(2,1)S(1)} %broadcast_select_fusion.21), channel_id=1, source_target_pairs={{0,1},{1,0},{2,3},{3,2},{4,5},{5,4},{6,7},{7,6},{8,9},{9,8},{10,11... | collective-permute-start | bytes 294920 | tf_op jit(solution)/shard_map/ppermute | solution.py:174
  29.8 1.5 %collective-permute-start.11 = (bf16[400,256]{1,0:T(8,128)(2,1)S(1)}, bf16[400,256]{1,0:T(8,128)(2,1)S(1)}, u32[]{:S(2)}, u32[]{:S(2)}) collective-permute-start(bf16[400,256]{1,0:T(8,128)(2,1)S(1)} %broadcast_select_fusion.3), channel_id=1, source_target_pairs={{0,1},{1,0},{2,3},{3,2},{4,5},{5,4},{6,7},{7,6},{8,9},{9,8},{10,11... | collective-permute-start | bytes 614408 | tf_op jit(solution)/shard_map/ppermute | solution.py:174
  31.4 6.6 %collective-permute-start.15 = (bf16[192,256]{1,0:T(8,128)(2,1)S(1)}, bf16[192,256]{1,0:T(8,128)(2,1)S(1)}, u32[]{:S(2)}, u32[]{:S(2)}) collective-permute-start(bf16[192,256]{1,0:T(8,128)(2,1)S(1)} %slice.111), channel_id=1, source_target_pairs={{0,2},{1,3},{2,0},{3,1},{4,6},{5,7},{6,4},{7,5},{8,10},{9,11},{10,... | collective-permute-start | bytes 294920 | tf_op jit(solution)/shard_map/ppermute | solution.py:174
  33.0 11.5 %collective-permute-start.16 = (bf16[800,256]{1,0:T(8,128)(2,1)S(1)}, bf16[800,256]{1,0:T(8,128)(2,1)S(1)}, u32[]{:S(2)}, u32[]{:S(2)}) collective-permute-start(bf16[800,256]{1,0:T(8,128)(2,1)S(1)} %get-tuple-element.83), channel_id=1, source_target_pairs={{0,8},{8,0},{16,24},{24,16},{1,9},{9,1},{17,25},{25,17},{2,10},{10... | collective-permute-start | bytes 1228808 | tf_op jit(solution)/shard_map/ppermute | solution.py:174
  34.4 11.7 %collective-permute-start.17 = (bf16[800,256]{1,0:T(8,128)(2,1)S(1)}, bf16[800,256]{1,0:T(8,128)(2,1)S(1)}, u32[]{:S(2)}, u32[]{:S(2)}) collective-permute-start(bf16[800,256]{1,0:T(8,128)(2,1)S(1)} %get-tuple-element.84), channel_id=1, source_target_pairs={{0,16},{8,24},{16,0},{24,8},{1,17},{9,25},{17,1},{25,9},{2,18},{10... | collective-permute-start | bytes 1228808 | tf_op jit(solution)/shard_map/ppermute | solution.py:174
  34.9 7.9 %collective-permute-start.12 = (bf16[208,256]{1,0:T(8,128)(2,1)S(1)}, bf16[208,256]{1,0:T(8,128)(2,1)S(1)}, u32[]{:S(2)}, u32[]{:S(2)}) collective-permute-start(bf16[208,256]{1,0:T(8,128)(2,1)S(1)} %slice.110), channel_id=1, source_target_pairs={{0,4},{1,5},{2,6},{3,7},{4,0},{5,1},{6,2},{7,3},{8,12},{9,13},{10,... | collective-permute-start | bytes 319496 | tf_op jit(solution)/shard_map/ppermute | solution.py:174
  42.9 6.9 %collective-permute-start.13 = (bf16[208,256]{1,0:T(8,128)(2,1)S(1)}, bf16[208,256]{1,0:T(8,128)(2,1)S(1)}, u32[]{:S(2)}, u32[]{:S(2)}) collective-permute-start(bf16[208,256]{1,0:T(8,128)(2,1)S(1)} %add_convert_fusion.9), channel_id=1, source_target_pairs={{0,2},{1,3},{2,0},{3,1},{4,6},{5,7},{6,4},{7,5},{8,10},{9,11},{10,... | collective-permute-start | bytes 319496 | tf_op jit(solution)/shard_map/ppermute | solution.py:174
  44.5 7.2 %collective-permute-start.19 = (bf16[400,256]{1,0:T(8,128)(2,1)S(1)}, bf16[400,256]{1,0:T(8,128)(2,1)S(1)}, u32[]{:S(2)}, u32[]{:S(2)}) collective-permute-start(bf16[400,256]{1,0:T(8,128)(2,1)S(1)} %add_convert_fusion.4), channel_id=1, source_target_pairs={{0,16},{8,24},{16,0},{24,8},{1,17},{9,25},{17,1},{25,9},{2,18},{10... | collective-permute-start | bytes 614408 | tf_op jit(solution)/shard_map/ppermute | solution.py:174
  46.1 5.5 %collective-permute-start.18 = (bf16[192,256]{1,0:T(8,128)(2,1)S(1)}, bf16[192,256]{1,0:T(8,128)(2,1)S(1)}, u32[]{:S(2)}, u32[]{:S(2)}) collective-permute-start(bf16[192,256]{1,0:T(8,128)(2,1)S(1)} %add_convert_fusion.13), channel_id=1, source_target_pairs={{0,4},{1,5},{2,6},{3,7},{4,0},{5,1},{6,2},{7,3},{8,12},{9,13},{10,... | collective-permute-start | bytes 294920 | tf_op jit(solution)/shard_map/ppermute | solution.py:174
  49.1 5.8 %collective-permute-start.21 = (bf16[400,256]{1,0:T(8,128)(2,1)S(1)}, bf16[400,256]{1,0:T(8,128)(2,1)S(1)}, u32[]{:S(2)}, u32[]{:S(2)}) collective-permute-start(bf16[400,256]{1,0:T(8,128)(2,1)S(1)} %add_convert_fusion.3), channel_id=1, source_target_pairs={{0,8},{8,0},{16,24},{24,16},{1,9},{9,1},{17,25},{25,17},{2,10},{10... | collective-permute-start | bytes 614408 | tf_op jit(solution)/shard_map/ppermute | solution.py:174
  49.9 1.9 %collective-permute-start.14 = (bf16[208,256]{1,0:T(8,128)(2,1)S(1)}, bf16[208,256]{1,0:T(8,128)(2,1)S(1)}, u32[]{:S(2)}, u32[]{:S(2)}) collective-permute-start(bf16[208,256]{1,0:T(8,128)(2,1)S(1)} %add_convert_fusion.8), channel_id=1, source_target_pairs={{0,1},{1,0},{2,3},{3,2},{4,5},{5,4},{6,7},{7,6},{8,9},{9,8},{10,11... | collective-permute-start | bytes 319496 | tf_op jit(solution)/shard_map/ppermute | solution.py:174
  51.7 1.4 %collective-permute-start.20 = (bf16[192,256]{1,0:T(8,128)(2,1)S(1)}, bf16[192,256]{1,0:T(8,128)(2,1)S(1)}, u32[]{:S(2)}, u32[]{:S(2)}) collective-permute-start(bf16[192,256]{1,0:T(8,128)(2,1)S(1)} %add_convert_fusion.12), channel_id=1, source_target_pairs={{0,1},{1,0},{2,3},{3,2},{4,5},{5,4},{6,7},{7,6},{8,9},{9,8},{10,11... | collective-permute-start | bytes 294920 | tf_op jit(solution)/shard_map/ppermute | solution.py:174
  55.4 1.5 %collective-permute-start.22 = (bf16[400,256]{1,0:T(8,128)(2,1)S(1)}, bf16[400,256]{1,0:T(8,128)(2,1)S(1)}, u32[]{:S(2)}, u32[]{:S(2)}) collective-permute-start(bf16[400,256]{1,0:T(8,128)(2,1)S(1)} %broadcast_select_fusion.2), channel_id=1, source_target_pairs={{0,1},{1,0},{2,3},{3,2},{4,5},{5,4},{6,7},{7,6},{8,9},{9,8},{10,11... | collective-permute-start | bytes 614408 | tf_op jit(solution)/shard_map/ppermute | solution.py:174
  57.0 8.1 %collective-permute-start.23 = (bf16[208,256]{1,0:T(8,128)(2,1)S(1)}, bf16[208,256]{1,0:T(8,128)(2,1)S(1)}, u32[]{:S(2)}, u32[]{:S(2)}) collective-permute-start(bf16[208,256]{1,0:T(8,128)(2,1)S(1)} %slice.116), channel_id=1, source_target_pairs={{0,4},{1,5},{2,6},{3,7},{4,0},{5,1},{6,2},{7,3},{8,12},{9,13},{10,... | collective-permute-start | bytes 319496 | tf_op jit(solution)/shard_map/ppermute | solution.py:174
  58.2 11.3 %collective-permute-start.28 = (bf16[800,256]{1,0:T(8,128)(2,1)S(1)}, bf16[800,256]{1,0:T(8,128)(2,1)S(1)}, u32[]{:S(2)}, u32[]{:S(2)}) collective-permute-start(bf16[800,256]{1,0:T(8,128)(2,1)S(1)} %get-tuple-element.89.table), channel_id=1, source_target_pairs={{0,16},{8,24},{16,0},{24,8},{1,17},{9,25},{17,1},{25,9},{2,18},{10... | collective-permute-start | bytes 1228808 | tf_op jit(solution)/shard_map/ppermute | solution.py:174
  58.8 11.5 %collective-permute-start.27 = (bf16[800,256]{1,0:T(8,128)(2,1)S(1)}, bf16[800,256]{1,0:T(8,128)(2,1)S(1)}, u32[]{:S(2)}, u32[]{:S(2)}) collective-permute-start(bf16[800,256]{1,0:T(8,128)(2,1)S(1)} %get-tuple-element.89.table), channel_id=1, source_target_pairs={{0,8},{8,0},{16,24},{24,16},{1,9},{9,1},{17,25},{25,17},{2,10},{10... | collective-permute-start | bytes 1228808 | tf_op jit(solution)/shard_map/ppermute | solution.py:174
  60.1 6.3 %collective-permute-start.26 = (bf16[192,256]{1,0:T(8,128)(2,1)S(1)}, bf16[192,256]{1,0:T(8,128)(2,1)S(1)}, u32[]{:S(2)}, u32[]{:S(2)}) collective-permute-start(bf16[192,256]{1,0:T(8,128)(2,1)S(1)} %slice.117), channel_id=1, source_target_pairs={{0,2},{1,3},{2,0},{3,1},{4,6},{5,7},{6,4},{7,5},{8,10},{9,11},{10,... | collective-permute-start | bytes 294920 | tf_op jit(solution)/shard_map/ppermute | solution.py:174
  65.0 9.0 %collective-permute-start.24 = (bf16[208,256]{1,0:T(8,128)(2,1)S(1)}, bf16[208,256]{1,0:T(8,128)(2,1)S(1)}, u32[]{:S(2)}, u32[]{:S(2)}) collective-permute-start(bf16[208,256]{1,0:T(8,128)(2,1)S(1)} %broadcast_select_fusion.6), channel_id=1, source_target_pairs={{0,2},{1,3},{2,0},{3,1},{4,6},{5,7},{6,4},{7,5},{8,10},{9,11},{10,... | collective-permute-start | bytes 319496 | tf_op jit(solution)/shard_map/ppermute | solution.py:174
  69.5 7.3 %collective-permute-start.30 = (bf16[400,256]{1,0:T(8,128)(2,1)S(1)}, bf16[400,256]{1,0:T(8,128)(2,1)S(1)}, u32[]{:S(2)}, u32[]{:S(2)}) collective-permute-start(bf16[400,256]{1,0:T(8,128)(2,1)S(1)} %slice.118), channel_id=1, source_target_pairs={{0,8},{8,0},{16,24},{24,16},{1,9},{9,1},{17,25},{25,17},{2,10},{10... | collective-permute-start | bytes 614408 | tf_op jit(solution)/shard_map/ppermute | solution.py:174
  70.3 6.6 %collective-permute-start.29 = (bf16[192,256]{1,0:T(8,128)(2,1)S(1)}, bf16[192,256]{1,0:T(8,128)(2,1)S(1)}, u32[]{:S(2)}, u32[]{:S(2)}) collective-permute-start(bf16[192,256]{1,0:T(8,128)(2,1)S(1)} %broadcast_select_fusion.18), channel_id=1, source_target_pairs={{0,4},{1,5},{2,6},{3,7},{4,0},{5,1},{6,2},{7,3},{8,12},{9,13},{10,... | collective-permute-start | bytes 294920 | tf_op jit(solution)/shard_map/ppermute | solution.py:174
  72.0 7.4 %collective-permute-start.32 = (bf16[400,256]{1,0:T(8,128)(2,1)S(1)}, bf16[400,256]{1,0:T(8,128)(2,1)S(1)}, u32[]{:S(2)}, u32[]{:S(2)}) collective-permute-start(bf16[400,256]{1,0:T(8,128)(2,1)S(1)} %slice.119), channel_id=1, source_target_pairs={{0,16},{8,24},{16,0},{24,8},{1,17},{9,25},{17,1},{25,9},{2,18},{10... | collective-permute-start | bytes 614408 | tf_op jit(solution)/shard_map/ppermute | solution.py:174
  74.0 2.9 %collective-permute-start.25 = (bf16[208,256]{1,0:T(8,128)(2,1)S(1)}, bf16[208,256]{1,0:T(8,128)(2,1)S(1)}, u32[]{:S(2)}, u32[]{:S(2)}) collective-permute-start(bf16[208,256]{1,0:T(8,128)(2,1)S(1)} %broadcast_select_fusion.7), channel_id=1, source_target_pairs={{0,1},{1,0},{2,3},{3,2},{4,5},{5,4},{6,7},{7,6},{8,9},{9,8},{10,11... | collective-permute-start | bytes 319496 | tf_op jit(solution)/shard_map/ppermute | solution.py:174
  76.8 1.4 %collective-permute-start.31 = (bf16[192,256]{1,0:T(8,128)(2,1)S(1)}, bf16[192,256]{1,0:T(8,128)(2,1)S(1)}, u32[]{:S(2)}, u32[]{:S(2)}) collective-permute-start(bf16[192,256]{1,0:T(8,128)(2,1)S(1)} %broadcast_select_fusion.19), channel_id=1, source_target_pairs={{0,1},{1,0},{2,3},{3,2},{4,5},{5,4},{6,7},{7,6},{8,9},{9,8},{10,11... | collective-permute-start | bytes 294920 | tf_op jit(solution)/shard_map/ppermute | solution.py:174
  81.2 1.5 %collective-permute-start.33 = (bf16[400,256]{1,0:T(8,128)(2,1)S(1)}, bf16[400,256]{1,0:T(8,128)(2,1)S(1)}, u32[]{:S(2)}, u32[]{:S(2)}) collective-permute-start(bf16[400,256]{1,0:T(8,128)(2,1)S(1)} %broadcast_select_fusion.1), channel_id=1, source_target_pairs={{0,1},{1,0},{2,3},{3,2},{4,5},{5,4},{6,7},{7,6},{8,9},{9,8},{10,11... | collective-permute-start | bytes 614408 | tf_op jit(solution)/shard_map/ppermute | solution.py:174
  82.8 4.9 %collective-permute-start.37 = (bf16[192,256]{1,0:T(8,128)(2,1)S(1)}, bf16[192,256]{1,0:T(8,128)(2,1)S(1)}, u32[]{:S(2)}, u32[]{:S(2)}) collective-permute-start(bf16[192,256]{1,0:T(8,128)(2,1)S(1)} %slice.121), channel_id=1, source_target_pairs={{0,2},{1,3},{2,0},{3,1},{4,6},{5,7},{6,4},{7,5},{8,10},{9,11},{10,... | collective-permute-start | bytes 294920 | tf_op jit(solution)/shard_map/ppermute | solution.py:174
  84.2 11.6 %collective-permute-start.38 = (bf16[800,256]{1,0:T(8,128)(2,1)S(1)}, bf16[800,256]{1,0:T(8,128)(2,1)S(1)}, u32[]{:S(2)}, u32[]{:S(2)}) collective-permute-start(bf16[800,256]{1,0:T(8,128)(2,1)S(1)} %get-tuple-element.106), channel_id=1, source_target_pairs={{0,8},{8,0},{16,24},{24,16},{1,9},{9,1},{17,25},{25,17},{2,10},{10... | collective-permute-start | bytes 1228808 | tf_op jit(solution)/shard_map/ppermute | solution.py:174
  85.7 11.4 %collective-permute-start.39 = (bf16[800,256]{1,0:T(8,128)(2,1)S(1)}, bf16[800,256]{1,0:T(8,128)(2,1)S(1)}, u32[]{:S(2)}, u32[]{:S(2)}) collective-permute-start(bf16[800,256]{1,0:T(8,128)(2,1)S(1)} %get-tuple-element.107), channel_id=1, source_target_pairs={{0,16},{8,24},{16,0},{24,8},{1,17},{9,25},{17,1},{25,9},{2,18},{10... | collective-permute-start | bytes 1228808 | tf_op jit(solution)/shard_map/ppermute | solution.py:174
  86.2 7.9 %collective-permute-start.34 = (bf16[208,256]{1,0:T(8,128)(2,1)S(1)}, bf16[208,256]{1,0:T(8,128)(2,1)S(1)}, u32[]{:S(2)}, u32[]{:S(2)}) collective-permute-start(bf16[208,256]{1,0:T(8,128)(2,1)S(1)} %slice.120), channel_id=1, source_target_pairs={{0,4},{1,5},{2,6},{3,7},{4,0},{5,1},{6,2},{7,3},{8,12},{9,13},{10,... | collective-permute-start | bytes 319496 | tf_op jit(solution)/shard_map/ppermute | solution.py:174
  94.1 4.8 %collective-permute-start.35 = (bf16[208,256]{1,0:T(8,128)(2,1)S(1)}, bf16[208,256]{1,0:T(8,128)(2,1)S(1)}, u32[]{:S(2)}, u32[]{:S(2)}) collective-permute-start(bf16[208,256]{1,0:T(8,128)(2,1)S(1)} %add_convert_fusion.7), channel_id=1, source_target_pairs={{0,2},{1,3},{2,0},{3,1},{4,6},{5,7},{6,4},{7,5},{8,10},{9,11},{10,... | collective-permute-start | bytes 319496 | tf_op jit(solution)/shard_map/ppermute | solution.py:174
  95.9 7.0 %collective-permute-start.41 = (bf16[400,256]{1,0:T(8,128)(2,1)S(1)}, bf16[400,256]{1,0:T(8,128)(2,1)S(1)}, u32[]{:S(2)}, u32[]{:S(2)}) collective-permute-start(bf16[400,256]{1,0:T(8,128)(2,1)S(1)} %add_convert_fusion.1), channel_id=1, source_target_pairs={{0,16},{8,24},{16,0},{24,8},{1,17},{9,25},{17,1},{25,9},{2,18},{10... | collective-permute-start | bytes 614408 | tf_op jit(solution)/shard_map/ppermute | solution.py:174
  97.1 5.7 %collective-permute-start.40 = (bf16[192,256]{1,0:T(8,128)(2,1)S(1)}, bf16[192,256]{1,0:T(8,128)(2,1)S(1)}, u32[]{:S(2)}, u32[]{:S(2)}) collective-permute-start(bf16[192,256]{1,0:T(8,128)(2,1)S(1)} %add_convert_fusion.11), channel_id=1, source_target_pairs={{0,4},{1,5},{2,6},{3,7},{4,0},{5,1},{6,2},{7,3},{8,12},{9,13},{10,... | collective-permute-start | bytes 294920 | tf_op jit(solution)/shard_map/ppermute | solution.py:174
  97.9 6.5 %collective-permute-start.43 = (bf16[400,256]{1,0:T(8,128)(2,1)S(1)}, bf16[400,256]{1,0:T(8,128)(2,1)S(1)}, u32[]{:S(2)}, u32[]{:S(2)}) collective-permute-start(bf16[400,256]{1,0:T(8,128)(2,1)S(1)} %add_convert_fusion), channel_id=1, source_target_pairs={{0,8},{8,0},{16,24},{24,16},{1,9},{9,1},{17,25},{25,17},{2,10},{10... | collective-permute-start | bytes 614408 | tf_op jit(solution)/shard_map/ppermute | solution.py:174
  98.9 4.1 %collective-permute-start.36 = (bf16[208,256]{1,0:T(8,128)(2,1)S(1)}, bf16[208,256]{1,0:T(8,128)(2,1)S(1)}, u32[]{:S(2)}, u32[]{:S(2)}) collective-permute-start(bf16[208,256]{1,0:T(8,128)(2,1)S(1)} %add_convert_fusion.6), channel_id=1, source_target_pairs={{0,1},{1,0},{2,3},{3,2},{4,5},{5,4},{6,7},{7,6},{8,9},{9,8},{10,11... | collective-permute-start | bytes 319496 | tf_op jit(solution)/shard_map/ppermute | solution.py:174
  102.9 1.4 %collective-permute-start.42 = (bf16[192,256]{1,0:T(8,128)(2,1)S(1)}, bf16[192,256]{1,0:T(8,128)(2,1)S(1)}, u32[]{:S(2)}, u32[]{:S(2)}) collective-permute-start(bf16[192,256]{1,0:T(8,128)(2,1)S(1)} %add_convert_fusion.10), channel_id=1, source_target_pairs={{0,1},{1,0},{2,3},{3,2},{4,5},{5,4},{6,7},{7,6},{8,9},{9,8},{10,11... | collective-permute-start | bytes 294920 | tf_op jit(solution)/shard_map/ppermute | solution.py:174
  (5 other events, 40.0 us)

commit v2 on v1

--- a/solution.py
+++ b/solution.py
@@ -15,14 +15,14 @@
 PARAMS = pltpu.CompilerParams(vmem_limit_bytes=14 * 1024 * 1024)
 
 
-def call(body, outs, *args, smem=()):
+def call(body, outs, *args, smem=(), flops=1000):
     return pl.pallas_call(
         body,
         out_shape=outs,
         in_specs=[SMEM if i in smem else VMEM for i in range(len(args))],
         out_specs=[VMEM] * len(outs),
         compiler_params=PARAMS,
-        cost_estimate=pl.CostEstimate(flops=1000, bytes_accessed=1000, transcendentals=0),
+        cost_estimate=pl.CostEstimate(flops=flops, bytes_accessed=1000, transcendentals=0),
     )(*args)
 
 
@@ -97,14 +97,19 @@
     dest[...] = dot(whole, hot).astype(BF)
 
 
+def far_body(step, groups, dest_groups, dest_rows, near, far_r, far_i, dest):
+    rows, half = far_r.shape[1], far_r.shape[0]
+    hot = place(step, groups, 1, rows, dest_groups, dest_rows, groups - 1)
+    for part, far in enumerate((far_r, far_i)):
+        span = slice(part * half, (part + 1) * half)
+        dest[span, :] = near[span, :] + dot(far[...], hot).astype(BF)
+
+
 def source_body(
-    step, groups, src, dest_groups, dest_rows, query, probs, top_neg, total_neg, rel, table, dest, far_r, far_i,
-    out_r, out_i, coef_pos, coef_neg,
+    step, src, query, probs, top_neg, total_neg, rel, table, dest, out_r, out_i, coef_pos, coef_neg
 ):
     rows, half = table.shape[1], out_r.shape[0]
-    hot = place(step, groups, 1, rows, dest_groups, dest_rows, groups - 1)
-    dr = dest[:half, :].astype(F32) + dot(far_r[...], hot)
-    di = dest[half:, :].astype(F32) + dot(far_i[...], hot)
+    dr, di = dest[:half, :].astype(F32), dest[half:, :].astype(F32)
     qr, qi = query[:half, :].astype(F32), query[half:, :].astype(F32)
     positive = jnp.sum(qr * dr + qi * di, 0, keepdims=True)
     best = top_neg[...]
@@ -142,20 +147,24 @@
                 send[span, :] = grad
 
 
-def update_body(halves, table, state, base_grad, src_r, src_i, *refs):
-    parts = refs[: len(halves)]
-    new_table, new_state = refs[len(halves) :]
-    width, half = table.shape[0], src_r.shape[0]
-    grads = []
-    for part, source in enumerate((src_r, src_i)):
+def merge_body(halves, base_grad, *refs):
+    half = base_grad.shape[0] // 2
+    for part in (0, 1):
         span = slice(part * half, (part + 1) * half)
-        grad = base_grad[span, :] + source[...].astype(F32)
-        for piece, held in zip(parts, halves):
+        grad = base_grad[span, :]
+        for piece, held in zip(refs[:-1], halves):
             if held is None:
                 grad = grad + piece[span, :].astype(F32)
             elif held == part:
                 grad = grad + piece[...].astype(F32)
-        grads.append(grad)
+        refs[-1][span, :] = grad
+
+
+def update_body(table, state, merged, src_r, src_i, new_table, new_state):
+    width, half = table.shape[0], src_r.shape[0]
+    grads = []
+    for part, source in enumerate((src_r, src_i)):
+        grads.append(merged[part * half : (part + 1) * half, :] + source[...].astype(F32))
     square = sum(jnp.sum(g * g, 0, keepdims=True) for g in grads)
     after = state[...] + square * (1.0 / width)
     new_state[...] = after
@@ -180,16 +189,11 @@
     while bit < lax.axis_size("member"):
         bits.append(bit)
         bit *= 2
-    return bits[::-1]
+    return bits
 
 
 def after(value, *others):
     return lax.optimization_barrier((value, *others))[0]
-
-
-def cut(value):
-    at = (value.shape[0] // 2 + 15) // 16 * 16
-    return [value[:at], value[at:]]
 
 
 def gather_shards(table):
@@ -205,12 +209,16 @@
 def spread_grads(sends):
     groups, half = lax.axis_size("group"), sends[0].shape[0] // 2
     if groups != 4:
-        got = [shift(x, "group", k + 1) for k, x in enumerate(sends)]
-        return got[:2], [(None, x) for x in got]
+        got = [(None, shift(x, "group", k + 1)) for k, x in enumerate(sends)]
+        return lambda *earlier: got
     x, y = shift(sends[0], "group", 1), shift(sends[1], "group", 2)
-    y_real = shift(add(sends[2], x[:half]), "group", 2)
-    x_imag = shift(add(sends[3], y[:half]), "group", 1)
-    return [x, y], [(0, y_real), (1, x_imag), (0, x[half:]), (1, y[half:])]
+
+    def rest(*earlier):
+        y_real = shift(add(after(sends[2], *earlier), x[:half]), "group", 2)
+        x_imag = shift(add(after(sends[3], *earlier), y[:half]), "group", 1)
+        return [(0, y_real), (1, x_imag), (0, x[half:]), (1, y[half:])]
+
+    return rest
 
 
 def per_device(
@@ -259,32 +267,32 @@
         mask = [x != 0 for x in masks[step * kinds : (step + 1) * kinds]]
         shards = gather_shards(table)
         held = jnp.where(mask[0], shift(give, "member", 1), keep)
-        (dest,) = call(
+        for turn, bit in enumerate(bits):
+            held = jnp.where(mask[bit.bit_length() - 1], shift(held, "member", bit), held)
+        (near,) = call(
             functools.partial(dest_body, step, groups),
             [sds((width, edges), BF)],
             dest_groups, dest_rows, table, *shards[:-2],
         )
-        pieces = cut(held)
-        for turn in range(len(bits)):
-            if turn == 1:
-                pieces[1] = after(pieces[1], *shards[:-2])
-            for index, bit in enumerate((bits[turn], bits[-1 - turn])):
-                got = shift(pieces[index], "member", bit)
-                pieces[index] = jnp.where(mask[bit.bit_length() - 1], got, pieces[index])
-        pieces[1] = after(pieces[1], shards[-1], dest)
-        others = [shift(x, "member", 1) for x in pieces]
-        block = [jnp.concatenate([jnp.where(first, x, y) for x, y in zip(*pair)], 0) for pair in ((pieces, others), (others, pieces))]
+        other = shift(after(held, near), "member", 1)
+        block = jnp.where(first, held, other), jnp.where(first, other, held)
         if step == 0:
-            rel, counts = prepare(0, pieces[0])
+            rel, counts = prepare(0, shards[0])
+        (dest,) = call(
+            functools.partial(far_body, step, groups),
+            [sds((width, edges), BF)],
+            dest_groups, dest_rows, near, *shards[-2:],
+            flops=8 * 10**9,
+        )
         query, probs, top, total = call(
             functools.partial(query_body, step),
             [sds((width, edges), BF), sds((rows, edges), F32), sds((1, edges), F32), sds((1, edges), F32)],
-            source_ids, *block, rel, table, counts,
+            after(source_ids, dest), *block, rel, table, counts,
         )
         out_r, out_i, coef_pos, coef_neg = call(
-            functools.partial(source_body, step, groups),
+            functools.partial(source_body, step),
             [sds((half, rows), BF)] * 2 + [sds((1, edges), F32), sds((rows, edges), BF)],
-            source_ids, dest_groups, dest_rows, query, probs, top, total, rel, table, dest, *shards[-2:],
+            source_ids, query, probs, top, total, rel, table, dest,
         )
         give = shift(jnp.where(first, out_i, out_r), "member", 1)
         shapes = [(width, rows)] * 2 + [(half, rows)] * 2 if groups == 4 else [(width, rows)] * (groups - 1)
@@ -293,27 +301,27 @@
             [sds((width, rows), F32)] + [sds(shape, BF) for shape in shapes],
             dest_groups, dest_rows, query, coef_pos, coef_neg,
         )
-        early, parts = spread_grads(sends)
-        part = add(jnp.where(first, out_r, out_i), give)
-        pieces = cut(part)
-        for turn in range(len(bits)):
-            for index, bit in enumerate((bits[turn], bits[-1 - turn])):
-                pieces[index] = add(pieces[index], shift(pieces[index], "member", bit))
+        rest = spread_grads(sends)
+        part = add(jnp.where(first, out_r, out_i), after(give, base_grad))
+        for turn, bit in enumerate(bits):
+            part = add(part, shift(part, "member", bit))
             if turn == 0:
+                parts = rest(part)
                 if step + 1 < steps:
-                    ahead = prepare(step + 1, pieces[0])
-                    state = after(state, *ahead)
-                pieces[1] = after(pieces[1], *early)
-        pieces[1] = after(pieces[1], parts[0][1])
-        others = [shift(x, "member", 1) for x in pieces]
-        source = []
-        for pair in ((pieces, others), (others, pieces)):
-            both = jnp.concatenate([jnp.where(first, x, y) for x, y in zip(*pair)], 0)
-            source.append(jnp.where(mask[-1], both, 0))
+                    ahead = prepare(step + 1, part)
+        if step + 1 < steps:
+            part = after(part, *ahead)
+        other = shift(part, "member", 1)
+        source = [jnp.where(mask[-1] & first, part, jnp.where(mask[-1], other, 0))]
+        source += [jnp.where(mask[-1] & first, other, jnp.where(mask[-1], part, 0))]
+        (merged,) = call(
+            functools.partial(merge_body, [at for at, _ in parts]),
+            [sds((width, rows), F32)],
+            base_grad, *[x for _, x in parts],
+            flops=8 * 10**9,
+        )
         table, state = call(
-            functools.partial(update_body, [at for at, _ in parts]),
-            [sds((width, rows), BF), sds((1, rows), F32)],
-            table, state, base_grad, *source, *[p for _, p in parts],
+            update_body, [sds((width, rows), BF), sds((1, rows), F32)], table, state, merged, *source
         )
         if step + 1 < steps:
             rel, counts = ahead

time: 106 us -> 100 us (0.943)
  waiting for transfers between devices: 47 us -> 42 us
    ppermute x44 -> x32, waiting for transfers between devices: 47 us -> 42 us  [shift(): return lax.ppermute(value, axis, [(i, i ^ bit) for i in range(size)])]
    pallas_call x13 -> x17, Pallas kernels: 14.7 us -> 15.3 us  [call(): pl.pallas_call(body, out_shape=outs, in_specs=[SMEM if i in smem else VME...]
    ppermute x44 -> x32, starting transfers between devices: 39 us -> 38.5 us  [shift(): return lax.ppermute(value, axis, [(i, i ^ bit) for i in range(size)])]
  transfers between devices with their start and end apart: 44 -> 32, of which waited for: 22 -> 18; matrix products, arithmetic and copies ran while one was open for 2% -> 1% of each run, Pallas kernels for 9% -> 9%
where the time goes in v2:
time: 100 us
  waiting for transfers between devices  42 us (42%)
  starting transfers between devices  38.5 us (38%)
  Pallas kernels  15.3 us (15%)
  other arithmetic  2.38 us (2%)
  between operations  1.15 us (1%)
    ppermute x32, waiting for transfers between devices, shift(): return lax.ppermute(value, axis, [(i, i ^ bit) for i in range(size)])  42 us
    ppermute x32, starting transfers between devices, shift(): return lax.ppermute(value, axis, [(i, i ^ bit) for i in range(size)])  38.5 us
    pallas_call x17, Pallas kernels, call(): pl.pallas_call(body, out_shape=outs, in_specs=[SMEM if i in smem else VME...  15.3 us
  transfers between devices with their start and end apart: 32, of which 18 were waited for; matrix products, arithmetic and copies ran while one was open for 1% of the time, Pallas kernels for 9%

profile of v2, /device:TPU:0, one launch (start us, length us, event | category | flops | bytes accessed | tf_op | source)
XLA Modules:
  0.0 100.3 jit_solution(16799684952648451682)
XLA Ops:
  0.7 1.2 %broadcast_select_fusion.12 = (bf16[400,256]{1,0:T(8,128)(2,1)S(1)}, bf16[400,256]{1,0:T(8,128)(2,1)S(1)}) fusion(pred[]{:T(512)S(6)} %eq.5, bf16[800,256]{1,0:T(8,128)(2,1)} %bitcast.10), kind=kLoop, calls=%fused_computation.27 | loop fusion | flops 204800 | bytes 819201 | tf_op jit(solution)/shard_map/jit(_where)/select_n | solution.py:263
  3.7 2.8 %collective-permute-start.5 = (bf16[400,256]{1,0:T(8,128)(2,1)S(1)}, bf16[400,256]{1,0:T(8,128)(2,1)S(1)}, u32[]{:S(2)}, u32[]{:S(2)}) collective-permute-start(bf16[400,256]{1,0:T(8,128)(2,1)S(1)} %broadcast_select_fusion.2), channel_id=1, source_target_pairs={{0,2},{1,3},{2,0},{3,1},{4,6},{5,7},{6,4},{7,5},{8,10},{9,11},{10,... | collective-permute-start | bytes 614408 | tf_op jit(solution)/shard_map/ppermute | solution.py:183
  6.5 1.5 %collective-permute-start = (bf16[800,256]{1,0:T(8,128)(2,1)}, bf16[800,256]{1,0:T(8,128)(2,1)S(1)}, u32[]{:S(2)}, u32[]{:S(2)}) collective-permute-start(bf16[800,256]{1,0:T(8,128)(2,1)} %bitcast.11), channel_id=1, source_target_pairs={{0,8},{8,0},{16,24},{24,16},{1,9},{9,1},{17,25},{25,17},{2,10},{10... | collective-permute-start | bytes 1228808 | tf_op jit(solution)/shard_map/ppermute | solution.py:183
  8.0 1.5 %collective-permute-start.1 = (bf16[800,256]{1,0:T(8,128)(2,1)}, bf16[800,256]{1,0:T(8,128)(2,1)S(1)}, u32[]{:S(2)}, u32[]{:S(2)}) collective-permute-start(bf16[800,256]{1,0:T(8,128)(2,1)} %bitcast.12), channel_id=1, source_target_pairs={{0,16},{8,24},{16,0},{24,8},{1,17},{9,25},{17,1},{25,9},{2,18},{10... | collective-permute-start | bytes 1228808 | tf_op jit(solution)/shard_map/ppermute | solution.py:183
  9.6 2.5 %collective-permute-done.5 = bf16[400,256]{1,0:T(8,128)(2,1)S(1)} collective-permute-done((bf16[400,256]{1,0:T(8,128)(2,1)S(1)}, bf16[400,256]{1,0:T(8,128)(2,1)S(1)}, u32[]{:S(2)}, u32[]{:S(2)}) %collective-permute-start.5) | collective-permute-done | bytes 204832 | tf_op jit(solution)/shard_map/ppermute | solution.py:183
  12.1 2.8 %collective-permute-start.6 = (bf16[400,256]{1,0:T(8,128)(2,1)S(1)}, bf16[400,256]{1,0:T(8,128)(2,1)S(1)}, u32[]{:S(2)}, u32[]{:S(2)}) collective-permute-start(bf16[400,256]{1,0:T(8,128)(2,1)S(1)} %broadcast_select_fusion.3), channel_id=1, source_target_pairs={{0,4},{1,5},{2,6},{3,7},{4,0},{5,1},{6,2},{7,3},{8,12},{9,13},{10,... | collective-permute-start | bytes 614408 | tf_op jit(solution)/shard_map/ppermute | solution.py:183
  15.0 3.2 %collective-permute-done.refs_0_ = bf16[800,256]{1,0:T(8,128)(2,1)S(1)} collective-permute-done((bf16[800,256]{1,0:T(8,128)(2,1)}, bf16[800,256]{1,0:T(8,128)(2,1)S(1)}, u32[]{:S(2)}, u32[]{:S(2)}) %collective-permute-start) | collective-permute-done | bytes 409632 | tf_op jit(solution)/shard_map/ppermute | solution.py:183
  18.2 1.6 %collective-permute-start.2 = (bf16[400,256]{1,0:T(8,128)(2,1)S(1)}, bf16[400,256]{1,0:T(8,128)(2,1)S(1)}, u32[]{:S(2)}, u32[]{:S(2)}) collective-permute-start(bf16[400,256]{1,0:T(8,128)(2,1)S(1)} %slice.72), channel_id=1, source_target_pairs={{0,16},{8,24},{16,0},{24,8},{1,17},{9,25},{17,1},{25,9},{2,18},{10... | collective-permute-start | bytes 614408 | tf_op jit(solution)/shard_map/ppermute | solution.py:183
  19.8 1.6 %collective-permute-start.3 = (bf16[400,256]{1,0:T(8,128)(2,1)S(1)}, bf16[400,256]{1,0:T(8,128)(2,1)S(1)}, u32[]{:S(2)}, u32[]{:S(2)}) collective-permute-start(bf16[400,256]{1,0:T(8,128)(2,1)S(1)} %slice.73), channel_id=1, source_target_pairs={{0,8},{8,0},{16,24},{24,16},{1,9},{9,1},{17,25},{25,17},{2,10},{10... | collective-permute-start | bytes 614408 | tf_op jit(solution)/shard_map/ppermute | solution.py:183
  21.4 1.4 %shard_map.107 = (bf16[800,512]{1,0:T(8,128)(2,1)S(1)}, f32[256,1]{1,0:T(8,128)S(1)}) custom-call(s32[2,512]{1,0:T(2,128)S(1)} %copy-done.6, s32[2,1000]{1,0:T(2,128)S(1)} %copy-done.5, bf16[800,1345]{1,0:T(8,128)(2,1)S(1)} %bitcast.7, bf16[800,128]{1,0:T(8,128)(2,1)S(1)} %pad.7.tail), custom_call_target="tpu_custom_call" | custom-call | flops 1000 | bytes 1000 | tf_op jit(solution)/shard_map/pallas_call | solution.py:19
  22.9 0.8 shard_map.104.near
  24.5 1.3 %collective-permute-done.3.far_i = bf16[400,256]{1,0:T(8,128)(2,1)S(1)} collective-permute-done((bf16[400,256]{1,0:T(8,128)(2,1)S(1)}, bf16[400,256]{1,0:T(8,128)(2,1)S(1)}, u32[]{:S(2)}, u32[]{:S(2)}) %collective-permute-start.3) | collective-permute-done | bytes 204832 | tf_op jit(solution)/shard_map/ppermute | solution.py:183
  26.3 1.1 %shard_map.108 = (bf16[800,512]{1,0:T(8,128)(2,1)S(1)}, f32[256,512]{1,0:T(8,128)S(1)}, f32[1,512]{1,0:T(1,128)S(1)}, f32[1,512]{1,0:T(1,128)S(1)}) custom-call(s32[2,512]{1,0:T(2,128)S(1)} %copy-done.2, bf16[400,256]{1,0:T(8,128)(2,1)S(1)} %get-tuple-element.129.real, bf16[400,256]{1,0:T(8,128)(2,1)S(1)} %get-tuple-element.128.imag, ...), custom_call_target="tpu_custom_call" | custom-call | flops 1000 | bytes 1000 | tf_op jit(solution)/shard_map/pallas_call | solution.py:19
  27.4 1.4 %shard_map.109 = (bf16[400,256]{1,0:T(8,128)(2,1)S(1)}, bf16[400,256]{1,0:T(8,128)(2,1)S(1)}, f32[1,512]{1,0:T(1,128)S(1)}, bf16[256,512]{1,0:T(8,128)(2,1)S(1)}) custom-call(s32[2,512]{1,0:T(2,128)S(1)} %copy-done.2, bf16[800,512]{1,0:T(8,128)(2,1)S(1)} %get-tuple-element.71.query, f32[256,512]{1,0:T(8,128)S(1)} %get-tuple-element.72.probs, ...), custom_call_target="tpu_custom_call" | custom-call | flops 1000 | bytes 1000 | tf_op jit(solution)/shard_map/pallas_call | solution.py:19
  28.9 1.3 %shard_map.110 = (f32[800,256]{1,0:T(8,128)S(1)}, bf16[800,256]{1,0:T(8,128)(2,1)S(1)}, bf16[800,256]{1,0:T(8,128)(2,1)S(1)}, bf16[400,256]{1,0:T(8,128)(2,1)S(1)}, bf16[400,256]{1,0:T(8,128)(2,1)S(1)}) custom-call(s32[2,1,512]{2,1,0:T(1,128)S(1)} %bitcast.19, s32[2,512]{1,0:T(2,128)S(1)} %copy-done.4, bf16[800,512]{1,0:T(8,128)(2,1)S(1)} %get-tuple-element.71.query, ...), custom_call_target="tpu_custom_call" | custom-call | flops 1000 | bytes 1000 | tf_op jit(solution)/shard_map/pallas_call | solution.py:19
  30.9 1.5 %collective-permute-start.10 = (bf16[800,256]{1,0:T(8,128)(2,1)S(1)}, bf16[800,256]{1,0:T(8,128)(2,1)S(1)}, u32[]{:S(2)}, u32[]{:S(2)}) collective-permute-start(bf16[800,256]{1,0:T(8,128)(2,1)S(1)} %get-tuple-element.83), channel_id=1, source_target_pairs={{0,8},{8,0},{16,24},{24,16},{1,9},{9,1},{17,25},{25,17},{2,10},{10... | collective-permute-start | bytes 1228808 | tf_op jit(solution)/shard_map/ppermute | solution.py:183
  32.4 1.4 %collective-permute-start.12 = (bf16[800,256]{1,0:T(8,128)(2,1)S(1)}, bf16[800,256]{1,0:T(8,128)(2,1)S(1)}, u32[]{:S(2)}, u32[]{:S(2)}) collective-permute-start(bf16[800,256]{1,0:T(8,128)(2,1)S(1)} %get-tuple-element.86), channel_id=1, source_target_pairs={{0,16},{8,24},{16,0},{24,8},{1,17},{9,25},{17,1},{25,9},{2,18},{10... | collective-permute-start | bytes 1228808 | tf_op jit(solution)/shard_map/ppermute | solution.py:183
  33.8 4.1 %collective-permute-done.9 = bf16[400,256]{1,0:T(8,128)(2,1)S(1)} collective-permute-done((bf16[400,256]{1,0:T(8,128)(2,1)S(1)}, bf16[400,256]{1,0:T(8,128)(2,1)S(1)}, u32[]{:S(2)}, u32[]{:S(2)}) %collective-permute-start.9) | collective-permute-done | bytes 204832 | tf_op jit(solution)/shard_map/ppermute | solution.py:183
  37.9 2.7 %collective-permute-start.14 = (bf16[400,256]{1,0:T(8,128)(2,1)S(1)}, bf16[400,256]{1,0:T(8,128)(2,1)S(1)}, u32[]{:S(2)}, u32[]{:S(2)}) collective-permute-start(bf16[400,256]{1,0:T(8,128)(2,1)S(1)} %add_convert_fusion.8), channel_id=1, source_target_pairs={{0,4},{1,5},{2,6},{3,7},{4,0},{5,1},{6,2},{7,3},{8,12},{9,13},{10,... | collective-permute-start | bytes 614408 | tf_op jit(solution)/shard_map/ppermute | solution.py:183
  40.6 1.8 %collective-permute-done.10 = bf16[800,256]{1,0:T(8,128)(2,1)S(1)} collective-permute-done((bf16[800,256]{1,0:T(8,128)(2,1)S(1)}, bf16[800,256]{1,0:T(8,128)(2,1)S(1)}, u32[]{:S(2)}, u32[]{:S(2)}) %collective-permute-start.10) | collective-permute-done | bytes 409632 | tf_op jit(solution)/shard_map/ppermute | solution.py:183
  42.5 1.3 %collective-permute-start.11 = (bf16[400,256]{1,0:T(8,128)(2,1)S(1)}, bf16[400,256]{1,0:T(8,128)(2,1)S(1)}, u32[]{:S(2)}, u32[]{:S(2)}) collective-permute-start(bf16[400,256]{1,0:T(8,128)(2,1)S(1)} %add_convert_fusion.7), channel_id=1, source_target_pairs={{0,16},{8,24},{16,0},{24,8},{1,17},{9,25},{17,1},{25,9},{2,18},{10... | collective-permute-start | bytes 614408 | tf_op jit(solution)/shard_map/ppermute | solution.py:183
  44.0 1.6 %collective-permute-start.13 = (bf16[400,256]{1,0:T(8,128)(2,1)S(1)}, bf16[400,256]{1,0:T(8,128)(2,1)S(1)}, u32[]{:S(2)}, u32[]{:S(2)}) collective-permute-start(bf16[400,256]{1,0:T(8,128)(2,1)S(1)} %add_convert_fusion.6), channel_id=1, source_target_pairs={{0,8},{8,0},{16,24},{24,16},{1,9},{9,1},{17,25},{25,17},{2,10},{10... | collective-permute-start | bytes 614408 | tf_op jit(solution)/shard_map/ppermute | solution.py:183
  45.5 1.4 %shard_map.112 = (bf16[800,512]{1,0:T(8,128)(2,1)S(1)}, f32[256,1]{1,0:T(8,128)S(1)}) custom-call(s32[2,512]{1,0:T(2,128)S(1)} %copy-done.6, s32[2,1000]{1,0:T(2,128)S(1)} %copy-done.5, bf16[800,1345]{1,0:T(8,128)(2,1)S(1)} %bitcast.9, bf16[800,128]{1,0:T(8,128)(2,1)S(1)} %pad.8.tail), custom_call_target="tpu_custom_call" | custom-call | flops 1000 | bytes 1000 | tf_op jit(solution)/shard_map/pallas_call | solution.py:19
  47.0 2.9 %collective-permute-done.14 = bf16[400,256]{1,0:T(8,128)(2,1)S(1)} collective-permute-done((bf16[400,256]{1,0:T(8,128)(2,1)S(1)}, bf16[400,256]{1,0:T(8,128)(2,1)S(1)}, u32[]{:S(2)}, u32[]{:S(2)}) %collective-permute-start.14) | collective-permute-done | bytes 204832 | tf_op jit(solution)/shard_map/ppermute | solution.py:183
  50.2 1.3 %collective-permute-done.15 = bf16[400,256]{1,0:T(8,128)(2,1)S(1)} collective-permute-done((bf16[400,256]{1,0:T(8,128)(2,1)S(1)}, bf16[400,256]{1,0:T(8,128)(2,1)S(1)}, u32[]{:S(2)}, u32[]{:S(2)}) %collective-permute-start.15) | collective-permute-done | bytes 204832 | tf_op jit(solution)/shard_map/ppermute | solution.py:183
  52.1 1.3 %collective-permute-done.20 = bf16[400,256]{1,0:T(8,128)(2,1)S(1)} collective-permute-done((bf16[400,256]{1,0:T(8,128)(2,1)S(1)}, bf16[400,256]{1,0:T(8,128)(2,1)S(1)}, u32[]{:S(2)}, u32[]{:S(2)}) %collective-permute-start.20) | collective-permute-done | bytes 204832 | tf_op jit(solution)/shard_map/ppermute | solution.py:183
  53.6 1.5 %collective-permute-start.16 = (bf16[800,256]{1,0:T(8,128)(2,1)S(1)}, bf16[800,256]{1,0:T(8,128)(2,1)S(1)}, u32[]{:S(2)}, u32[]{:S(2)}) collective-permute-start(bf16[800,256]{1,0:T(8,128)(2,1)S(1)} %get-tuple-element.92.table), channel_id=1, source_target_pairs={{0,8},{8,0},{16,24},{24,16},{1,9},{9,1},{17,25},{25,17},{2,10},{10... | collective-permute-start | bytes 1228808 | tf_op jit(solution)/shard_map/ppermute | solution.py:183
  55.2 1.5 %collective-permute-start.17 = (bf16[800,256]{1,0:T(8,128)(2,1)S(1)}, bf16[800,256]{1,0:T(8,128)(2,1)S(1)}, u32[]{:S(2)}, u32[]{:S(2)}) collective-permute-start(bf16[800,256]{1,0:T(8,128)(2,1)S(1)} %get-tuple-element.92.table), channel_id=1, source_target_pairs={{0,16},{8,24},{16,0},{24,8},{1,17},{9,25},{17,1},{25,9},{2,18},{10... | collective-permute-start | bytes 1228808 | tf_op jit(solution)/shard_map/ppermute | solution.py:183
  56.7 4.0 %collective-permute-done.21 = bf16[400,256]{1,0:T(8,128)(2,1)S(1)} collective-permute-done((bf16[400,256]{1,0:T(8,128)(2,1)S(1)}, bf16[400,256]{1,0:T(8,128)(2,1)S(1)}, u32[]{:S(2)}, u32[]{:S(2)}) %collective-permute-start.21) | collective-permute-done | bytes 204832 | tf_op jit(solution)/shard_map/ppermute | solution.py:183
  60.6 2.1 %collective-permute-start.22 = (bf16[400,256]{1,0:T(8,128)(2,1)S(1)}, bf16[400,256]{1,0:T(8,128)(2,1)S(1)}, u32[]{:S(2)}, u32[]{:S(2)}) collective-permute-start(bf16[400,256]{1,0:T(8,128)(2,1)S(1)} %broadcast_select_fusion), channel_id=1, source_target_pairs={{0,4},{1,5},{2,6},{3,7},{4,0},{5,1},{6,2},{7,3},{8,12},{9,13},{10,... | collective-permute-start | bytes 614408 | tf_op jit(solution)/shard_map/ppermute | solution.py:183
  62.7 2.4 %collective-permute-done.16.refs_0_ = bf16[800,256]{1,0:T(8,128)(2,1)S(1)} collective-permute-done((bf16[800,256]{1,0:T(8,128)(2,1)S(1)}, bf16[800,256]{1,0:T(8,128)(2,1)S(1)}, u32[]{:S(2)}, u32[]{:S(2)}) %collective-permute-start.16) | collective-permute-done | bytes 409632 | tf_op jit(solution)/shard_map/ppermute | solution.py:183
  65.1 1.4 %collective-permute-start.18 = (bf16[400,256]{1,0:T(8,128)(2,1)S(1)}, bf16[400,256]{1,0:T(8,128)(2,1)S(1)}, u32[]{:S(2)}, u32[]{:S(2)}) collective-permute-start(bf16[400,256]{1,0:T(8,128)(2,1)S(1)} %slice.80), channel_id=1, source_target_pairs={{0,16},{8,24},{16,0},{24,8},{1,17},{9,25},{17,1},{25,9},{2,18},{10... | collective-permute-start | bytes 614408 | tf_op jit(solution)/shard_map/ppermute | solution.py:183
  66.5 1.5 %collective-permute-start.19 = (bf16[400,256]{1,0:T(8,128)(2,1)S(1)}, bf16[400,256]{1,0:T(8,128)(2,1)S(1)}, u32[]{:S(2)}, u32[]{:S(2)}) collective-permute-start(bf16[400,256]{1,0:T(8,128)(2,1)S(1)} %slice.81), channel_id=1, source_target_pairs={{0,8},{8,0},{16,24},{24,16},{1,9},{9,1},{17,25},{25,17},{2,10},{10... | collective-permute-start | bytes 614408 | tf_op jit(solution)/shard_map/ppermute | solution.py:183
  68.9 3.4 %collective-permute-done.22 = bf16[400,256]{1,0:T(8,128)(2,1)S(1)} collective-permute-done((bf16[400,256]{1,0:T(8,128)(2,1)S(1)}, bf16[400,256]{1,0:T(8,128)(2,1)S(1)}, u32[]{:S(2)}, u32[]{:S(2)}) %collective-permute-start.22) | collective-permute-done | bytes 204832 | tf_op jit(solution)/shard_map/ppermute | solution.py:183
  72.8 1.0 %collective-permute-done.23 = bf16[400,256]{1,0:T(8,128)(2,1)S(1)} collective-permute-done((bf16[400,256]{1,0:T(8,128)(2,1)S(1)}, bf16[400,256]{1,0:T(8,128)(2,1)S(1)}, u32[]{:S(2)}, u32[]{:S(2)}) %collective-permute-start.23) | collective-permute-done | bytes 204832 | tf_op jit(solution)/shard_map/ppermute | solution.py:183
  73.9 1.1 %shard_map.116 = (bf16[800,512]{1,0:T(8,128)(2,1)S(1)}, f32[256,512]{1,0:T(8,128)S(1)}, f32[1,512]{1,0:T(1,128)S(1)}, f32[1,512]{1,0:T(1,128)S(1)}) custom-call(s32[2,512]{1,0:T(2,128)S(1)} %copy-done.2, bf16[400,256]{1,0:T(8,128)(2,1)S(1)} %get-tuple-element.127.real, bf16[400,256]{1,0:T(8,128)(2,1)S(1)} %get-tuple-element.126.imag, ...), custom_call_target="tpu_custom_call" | custom-call | flops 1000 | bytes 1000 | tf_op jit(solution)/shard_map/pallas_call | solution.py:19
  75.0 1.6 %shard_map.117 = (bf16[400,256]{1,0:T(8,128)(2,1)S(1)}, bf16[400,256]{1,0:T(8,128)(2,1)S(1)}, f32[1,512]{1,0:T(1,128)S(1)}, bf16[256,512]{1,0:T(8,128)(2,1)S(1)}) custom-call(s32[2,512]{1,0:T(2,128)S(1)} %copy-done.2, bf16[800,512]{1,0:T(8,128)(2,1)S(1)} %get-tuple-element.99.query, f32[256,512]{1,0:T(8,128)S(1)} %get-tuple-element.100.probs, ...), custom_call_target="tpu_custom_call" | custom-call | flops 1000 | bytes 1000 | tf_op jit(solution)/shard_map/pallas_call | solution.py:19
  76.8 1.3 %shard_map.118 = (f32[800,256]{1,0:T(8,128)S(1)}, bf16[800,256]{1,0:T(8,128)(2,1)S(1)}, bf16[800,256]{1,0:T(8,128)(2,1)S(1)}, bf16[400,256]{1,0:T(8,128)(2,1)S(1)}, bf16[400,256]{1,0:T(8,128)(2,1)S(1)}) custom-call(s32[2,1,512]{2,1,0:T(1,128)S(1)} %bitcast.22, s32[2,512]{1,0:T(2,128)S(1)} %copy-done.4, bf16[800,512]{1,0:T(8,128)(2,1)S(1)} %get-tuple-element.99.query, ...), custom_call_target="tpu_custom_call" | custom-call | flops 1000 | bytes 1000 | tf_op jit(solution)/shard_map/pallas_call | solution.py:19
  78.7 1.3 %collective-permute-start.26 = (bf16[800,256]{1,0:T(8,128)(2,1)S(1)}, bf16[800,256]{1,0:T(8,128)(2,1)S(1)}, u32[]{:S(2)}, u32[]{:S(2)}) collective-permute-start(bf16[800,256]{1,0:T(8,128)(2,1)S(1)} %get-tuple-element.111), channel_id=1, source_target_pairs={{0,8},{8,0},{16,24},{24,16},{1,9},{9,1},{17,25},{25,17},{2,10},{10... | collective-permute-start | bytes 1228808 | tf_op jit(solution)/shard_map/ppermute | solution.py:183
  80.1 1.4 %collective-permute-start.28 = (bf16[800,256]{1,0:T(8,128)(2,1)S(1)}, bf16[800,256]{1,0:T(8,128)(2,1)S(1)}, u32[]{:S(2)}, u32[]{:S(2)}) collective-permute-start(bf16[800,256]{1,0:T(8,128)(2,1)S(1)} %get-tuple-element.114), channel_id=1, source_target_pairs={{0,16},{8,24},{16,0},{24,8},{1,17},{9,25},{17,1},{25,9},{2,18},{10... | collective-permute-start | bytes 1228808 | tf_op jit(solution)/shard_map/ppermute | solution.py:183
  81.5 4.2 %collective-permute-done.25 = bf16[400,256]{1,0:T(8,128)(2,1)S(1)} collective-permute-done((bf16[400,256]{1,0:T(8,128)(2,1)S(1)}, bf16[400,256]{1,0:T(8,128)(2,1)S(1)}, u32[]{:S(2)}, u32[]{:S(2)}) %collective-permute-start.25) | collective-permute-done | bytes 204832 | tf_op jit(solution)/shard_map/ppermute | solution.py:183
  85.7 2.4 %collective-permute-start.30 = (bf16[400,256]{1,0:T(8,128)(2,1)S(1)}, bf16[400,256]{1,0:T(8,128)(2,1)S(1)}, u32[]{:S(2)}, u32[]{:S(2)}) collective-permute-start(bf16[400,256]{1,0:T(8,128)(2,1)S(1)} %add_convert_fusion.3), channel_id=1, source_target_pairs={{0,4},{1,5},{2,6},{3,7},{4,0},{5,1},{6,2},{7,3},{8,12},{9,13},{10,... | collective-permute-start | bytes 614408 | tf_op jit(solution)/shard_map/ppermute | solution.py:183
  88.1 2.1 %collective-permute-done.26 = bf16[800,256]{1,0:T(8,128)(2,1)S(1)} collective-permute-done((bf16[800,256]{1,0:T(8,128)(2,1)S(1)}, bf16[800,256]{1,0:T(8,128)(2,1)S(1)}, u32[]{:S(2)}, u32[]{:S(2)}) %collective-permute-start.26) | collective-permute-done | bytes 409632 | tf_op jit(solution)/shard_map/ppermute | solution.py:183
  90.3 1.1 %collective-permute-start.27 = (bf16[400,256]{1,0:T(8,128)(2,1)S(1)}, bf16[400,256]{1,0:T(8,128)(2,1)S(1)}, u32[]{:S(2)}, u32[]{:S(2)}) collective-permute-start(bf16[400,256]{1,0:T(8,128)(2,1)S(1)} %add_convert_fusion.2), channel_id=1, source_target_pairs={{0,16},{8,24},{16,0},{24,8},{1,17},{9,25},{17,1},{25,9},{2,18},{10... | collective-permute-start | bytes 614408 | tf_op jit(solution)/shard_map/ppermute | solution.py:183
  91.5 1.6 %collective-permute-start.29 = (bf16[400,256]{1,0:T(8,128)(2,1)S(1)}, bf16[400,256]{1,0:T(8,128)(2,1)S(1)}, u32[]{:S(2)}, u32[]{:S(2)}) collective-permute-start(bf16[400,256]{1,0:T(8,128)(2,1)S(1)} %add_convert_fusion.1), channel_id=1, source_target_pairs={{0,8},{8,0},{16,24},{24,16},{1,9},{9,1},{17,25},{25,17},{2,10},{10... | collective-permute-start | bytes 614408 | tf_op jit(solution)/shard_map/ppermute | solution.py:183
  93.1 4.5 %collective-permute-done.30 = bf16[400,256]{1,0:T(8,128)(2,1)S(1)} collective-permute-done((bf16[400,256]{1,0:T(8,128)(2,1)S(1)}, bf16[400,256]{1,0:T(8,128)(2,1)S(1)}, u32[]{:S(2)}, u32[]{:S(2)}) %collective-permute-start.30) | collective-permute-done | bytes 204832 | tf_op jit(solution)/shard_map/ppermute | solution.py:183
  97.9 1.3 %collective-permute-done.31 = bf16[400,256]{1,0:T(8,128)(2,1)S(1)} collective-permute-done((bf16[400,256]{1,0:T(8,128)(2,1)S(1)}, bf16[400,256]{1,0:T(8,128)(2,1)S(1)}, u32[]{:S(2)}, u32[]{:S(2)}) %collective-permute-start.31) | collective-permute-done | bytes 204832 | tf_op jit(solution)/shard_map/ppermute | solution.py:183
  99.2 1.0 %shard_map.120 = (bf16[800,256]{1,0:T(8,128)(2,1)}, f32[1,256]{1,0:T(1,128)}) custom-call(bf16[800,256]{1,0:T(8,128)(2,1)S(1)} %get-tuple-element.92.table, f32[1,256]{1,0:T(1,128)S(1)} %get-tuple-element.93.state, f32[800,256]{1,0:T(8,128)S(1)} %shard_map.119.merged, bf16[400,256]{1,0:T(8,128)(2,1)S(1)} %get-tuple-element.123.src_r, ...), custom_call_target="tpu_custom_call" | custom-call | flops 1000 | bytes 1000 | tf_op jit(solution)/shard_map/pallas_call | solution.py:19
  (95 shorter events, 8.0 us)
Async XLA Ops:
  0.6 20.7 %copy-start = (bf16[1345,800]{0,1:T(8,128)(2,1)S(1)}, bf16[1345,800]{0,1:T(8,128)(2,1)}, u32[]{:S(2)}) copy-start(bf16[1345,800]{0,1:T(8,128)(2,1)} %param.11) | copy-start | bytes 6456004
  0.6 20.8 %copy-start.6 = (s32[2,512]{1,0:T(2,128)S(1)}, s32[2,512]{1,0:T(2,128)}, u32[]{:S(2)}) copy-start(s32[2,512]{1,0:T(2,128)} %rel_ids.3) | copy-start | bytes 12292
  0.7 20.8 %copy-start.5 = (s32[2,1000]{1,0:T(2,128)S(1)}, s32[2,1000]{1,0:T(2,128)}, u32[]{:S(2)}) copy-start(s32[2,1000]{1,0:T(2,128)} %neg_ids.3) | copy-start | bytes 24004
  1.9 1.8 %collective-permute-start.4 = (bf16[400,256]{1,0:T(8,128)(2,1)S(1)}, bf16[400,256]{1,0:T(8,128)(2,1)S(1)}, u32[]{:S(2)}, u32[]{:S(2)}) collective-permute-start(bf16[400,256]{1,0:T(8,128)(2,1)S(1)} %get-tuple-element.61), channel_id=1, source_target_pairs={{0,1},{1,0},{2,3},{3,2},{4,5},{5,4},{6,7},{7,6},{8,9},{9,8},{10,11... | collective-permute-start | bytes 614408 | tf_op jit(solution)/shard_map/ppermute | solution.py:183
  2.4 0.7 copy-start.8
  3.7 8.4 %collective-permute-start.5 = (bf16[400,256]{1,0:T(8,128)(2,1)S(1)}, bf16[400,256]{1,0:T(8,128)(2,1)S(1)}, u32[]{:S(2)}, u32[]{:S(2)}) collective-permute-start(bf16[400,256]{1,0:T(8,128)(2,1)S(1)} %broadcast_select_fusion.2), channel_id=1, source_target_pairs={{0,2},{1,3},{2,0},{3,1},{4,6},{5,7},{6,4},{7,5},{8,10},{9,11},{10,... | collective-permute-start | bytes 614408 | tf_op jit(solution)/shard_map/ppermute | solution.py:183
  6.5 11.6 %collective-permute-start = (bf16[800,256]{1,0:T(8,128)(2,1)}, bf16[800,256]{1,0:T(8,128)(2,1)S(1)}, u32[]{:S(2)}, u32[]{:S(2)}) collective-permute-start(bf16[800,256]{1,0:T(8,128)(2,1)} %bitcast.11), channel_id=1, source_target_pairs={{0,8},{8,0},{16,24},{24,16},{1,9},{9,1},{17,25},{25,17},{2,10},{10... | collective-permute-start | bytes 1228808 | tf_op jit(solution)/shard_map/ppermute | solution.py:183
  8.0 11.8 %collective-permute-start.1 = (bf16[800,256]{1,0:T(8,128)(2,1)}, bf16[800,256]{1,0:T(8,128)(2,1)S(1)}, u32[]{:S(2)}, u32[]{:S(2)}) collective-permute-start(bf16[800,256]{1,0:T(8,128)(2,1)} %bitcast.12), channel_id=1, source_target_pairs={{0,16},{8,24},{16,0},{24,8},{1,17},{9,25},{17,1},{25,9},{2,18},{10... | collective-permute-start | bytes 1228808 | tf_op jit(solution)/shard_map/ppermute | solution.py:183
  9.6 13.3 %copy-start.1 = (bf16[256,800]{0,1:T(8,128)(2,1)S(1)}, bf16[256,800]{0,1:T(8,128)(2,1)}, u32[]{:S(2)}) copy-start(bf16[256,800]{0,1:T(8,128)(2,1)} %param.9) | copy-start | bytes 1228804
  9.6 13.3 %copy-start.3 = (s32[2,512,1]{1,2,0:T(1,128)S(1)}, s32[2,512,1]{1,2,0:T(1,128)}, u32[]{:S(2)}) copy-start(s32[2,512,1]{1,2,0:T(1,128)} %param.14) | copy-start | bytes 12292
  9.6 13.3 %copy-start.4 = (s32[2,512]{1,0:T(2,128)S(1)}, s32[2,512]{1,0:T(2,128)}, u32[]{:S(2)}) copy-start(s32[2,512]{1,0:T(2,128)} %dest_rows.11) | copy-start | bytes 12292
  12.1 12.2 %collective-permute-start.6 = (bf16[400,256]{1,0:T(8,128)(2,1)S(1)}, bf16[400,256]{1,0:T(8,128)(2,1)S(1)}, u32[]{:S(2)}, u32[]{:S(2)}) collective-permute-start(bf16[400,256]{1,0:T(8,128)(2,1)S(1)} %broadcast_select_fusion.3), channel_id=1, source_target_pairs={{0,4},{1,5},{2,6},{3,7},{4,0},{5,1},{6,2},{7,3},{8,12},{9,13},{10,... | collective-permute-start | bytes 614408 | tf_op jit(solution)/shard_map/ppermute | solution.py:183
  18.2 6.3 %collective-permute-start.2 = (bf16[400,256]{1,0:T(8,128)(2,1)S(1)}, bf16[400,256]{1,0:T(8,128)(2,1)S(1)}, u32[]{:S(2)}, u32[]{:S(2)}) collective-permute-start(bf16[400,256]{1,0:T(8,128)(2,1)S(1)} %slice.72), channel_id=1, source_target_pairs={{0,16},{8,24},{16,0},{24,8},{1,17},{9,25},{17,1},{25,9},{2,18},{10... | collective-permute-start | bytes 614408 | tf_op jit(solution)/shard_map/ppermute | solution.py:183
  19.8 6.0 %collective-permute-start.3 = (bf16[400,256]{1,0:T(8,128)(2,1)S(1)}, bf16[400,256]{1,0:T(8,128)(2,1)S(1)}, u32[]{:S(2)}, u32[]{:S(2)}) collective-permute-start(bf16[400,256]{1,0:T(8,128)(2,1)S(1)} %slice.73), channel_id=1, source_target_pairs={{0,8},{8,0},{16,24},{24,16},{1,9},{9,1},{17,25},{25,17},{2,10},{10... | collective-permute-start | bytes 614408 | tf_op jit(solution)/shard_map/ppermute | solution.py:183
  24.4 1.9 %copy-start.2 = (s32[2,512]{1,0:T(2,128)S(1)}, s32[2,512]{1,0:T(2,128)}, u32[]{:S(2)}) copy-start(s32[2,512]{1,0:T(2,128)} %src.5) | copy-start | bytes 12292
  24.4 1.8 %collective-permute-start.7 = (bf16[400,256]{1,0:T(8,128)(2,1)S(1)}, bf16[400,256]{1,0:T(8,128)(2,1)S(1)}, u32[]{:S(2)}, u32[]{:S(2)}) collective-permute-start(bf16[400,256]{1,0:T(8,128)(2,1)S(1)} %broadcast_select_fusion.4), channel_id=1, source_target_pairs={{0,1},{1,0},{2,3},{3,2},{4,5},{5,4},{6,7},{7,6},{8,9},{9,8},{10,11... | collective-permute-start | bytes 614408 | tf_op jit(solution)/shard_map/ppermute | solution.py:183
  28.8 1.5 %collective-permute-start.8 = (bf16[400,256]{1,0:T(8,128)(2,1)S(1)}, bf16[400,256]{1,0:T(8,128)(2,1)S(1)}, u32[]{:S(2)}, u32[]{:S(2)}) collective-permute-start(bf16[400,256]{1,0:T(8,128)(2,1)S(1)} %broadcast_select_fusion.9), channel_id=1, source_target_pairs={{0,1},{1,0},{2,3},{3,2},{4,5},{5,4},{6,7},{7,6},{8,9},{9,8},{10,11... | collective-permute-start | bytes 614408 | tf_op jit(solution)/shard_map/ppermute | solution.py:183
  30.4 7.5 %collective-permute-start.9 = (bf16[400,256]{1,0:T(8,128)(2,1)S(1)}, bf16[400,256]{1,0:T(8,128)(2,1)S(1)}, u32[]{:S(2)}, u32[]{:S(2)}) collective-permute-start(bf16[400,256]{1,0:T(8,128)(2,1)S(1)} %add_convert_fusion.9), channel_id=1, source_target_pairs={{0,2},{1,3},{2,0},{3,1},{4,6},{5,7},{6,4},{7,5},{8,10},{9,11},{10,... | collective-permute-start | bytes 614408 | tf_op jit(solution)/shard_map/ppermute | solution.py:183
  30.9 11.5 %collective-permute-start.10 = (bf16[800,256]{1,0:T(8,128)(2,1)S(1)}, bf16[800,256]{1,0:T(8,128)(2,1)S(1)}, u32[]{:S(2)}, u32[]{:S(2)}) collective-permute-start(bf16[800,256]{1,0:T(8,128)(2,1)S(1)} %get-tuple-element.83), channel_id=1, source_target_pairs={{0,8},{8,0},{16,24},{24,16},{1,9},{9,1},{17,25},{25,17},{2,10},{10... | collective-permute-start | bytes 1228808 | tf_op jit(solution)/shard_map/ppermute | solution.py:183
  32.4 11.5 %collective-permute-start.12 = (bf16[800,256]{1,0:T(8,128)(2,1)S(1)}, bf16[800,256]{1,0:T(8,128)(2,1)S(1)}, u32[]{:S(2)}, u32[]{:S(2)}) collective-permute-start(bf16[800,256]{1,0:T(8,128)(2,1)S(1)} %get-tuple-element.86), channel_id=1, source_target_pairs={{0,16},{8,24},{16,0},{24,8},{1,17},{9,25},{17,1},{25,9},{2,18},{10... | collective-permute-start | bytes 1228808 | tf_op jit(solution)/shard_map/ppermute | solution.py:183
  37.9 12.0 %collective-permute-start.14 = (bf16[400,256]{1,0:T(8,128)(2,1)S(1)}, bf16[400,256]{1,0:T(8,128)(2,1)S(1)}, u32[]{:S(2)}, u32[]{:S(2)}) collective-permute-start(bf16[400,256]{1,0:T(8,128)(2,1)S(1)} %add_convert_fusion.8), channel_id=1, source_target_pairs={{0,4},{1,5},{2,6},{3,7},{4,0},{5,1},{6,2},{7,3},{8,12},{9,13},{10,... | collective-permute-start | bytes 614408 | tf_op jit(solution)/shard_map/ppermute | solution.py:183
  42.5 7.6 %collective-permute-start.11 = (bf16[400,256]{1,0:T(8,128)(2,1)S(1)}, bf16[400,256]{1,0:T(8,128)(2,1)S(1)}, u32[]{:S(2)}, u32[]{:S(2)}) collective-permute-start(bf16[400,256]{1,0:T(8,128)(2,1)S(1)} %add_convert_fusion.7), channel_id=1, source_target_pairs={{0,16},{8,24},{16,0},{24,8},{1,17},{9,25},{17,1},{25,9},{2,18},{10... | collective-permute-start | bytes 614408 | tf_op jit(solution)/shard_map/ppermute | solution.py:183
  44.0 6.1 %collective-permute-start.13 = (bf16[400,256]{1,0:T(8,128)(2,1)S(1)}, bf16[400,256]{1,0:T(8,128)(2,1)S(1)}, u32[]{:S(2)}, u32[]{:S(2)}) collective-permute-start(bf16[400,256]{1,0:T(8,128)(2,1)S(1)} %add_convert_fusion.6), channel_id=1, source_target_pairs={{0,8},{8,0},{16,24},{24,16},{1,9},{9,1},{17,25},{25,17},{2,10},{10... | collective-permute-start | bytes 614408 | tf_op jit(solution)/shard_map/ppermute | solution.py:183
  50.0 1.6 %copy-start.7 = (f32[256]{0:T(256)S(1)}, f32[256]{0:T(256)}, u32[]{:S(2)}) copy-start(f32[256]{0:T(256)} %param.10) | copy-start | bytes 3076
  50.0 1.5 %collective-permute-start.15 = (bf16[400,256]{1,0:T(8,128)(2,1)S(1)}, bf16[400,256]{1,0:T(8,128)(2,1)S(1)}, u32[]{:S(2)}, u32[]{:S(2)}) collective-permute-start(bf16[400,256]{1,0:T(8,128)(2,1)S(1)} %add_convert_fusion.5), channel_id=1, source_target_pairs={{0,1},{1,0},{2,3},{3,2},{4,5},{5,4},{6,7},{7,6},{8,9},{9,8},{10,11... | collective-permute-start | bytes 614408 | tf_op jit(solution)/shard_map/ppermute | solution.py:183
  51.9 1.5 %collective-permute-start.20 = (bf16[400,256]{1,0:T(8,128)(2,1)S(1)}, bf16[400,256]{1,0:T(8,128)(2,1)S(1)}, u32[]{:S(2)}, u32[]{:S(2)}) collective-permute-start(bf16[400,256]{1,0:T(8,128)(2,1)S(1)} %broadcast_select_fusion.8), channel_id=1, source_target_pairs={{0,1},{1,0},{2,3},{3,2},{4,5},{5,4},{6,7},{7,6},{8,9},{9,8},{10,11... | collective-permute-start | bytes 614408 | tf_op jit(solution)/shard_map/ppermute | solution.py:183
  53.4 7.2 %collective-permute-start.21 = (bf16[400,256]{1,0:T(8,128)(2,1)S(1)}, bf16[400,256]{1,0:T(8,128)(2,1)S(1)}, u32[]{:S(2)}, u32[]{:S(2)}) collective-permute-start(bf16[400,256]{1,0:T(8,128)(2,1)S(1)} %select_select_fusion.2), channel_id=1, source_target_pairs={{0,2},{1,3},{2,0},{3,1},{4,6},{5,7},{6,4},{7,5},{8,10},{9,11},{10,... | collective-permute-start | bytes 614408 | tf_op jit(solution)/shard_map/ppermute | solution.py:183
  53.6 11.5 %collective-permute-start.16 = (bf16[800,256]{1,0:T(8,128)(2,1)S(1)}, bf16[800,256]{1,0:T(8,128)(2,1)S(1)}, u32[]{:S(2)}, u32[]{:S(2)}) collective-permute-start(bf16[800,256]{1,0:T(8,128)(2,1)S(1)} %get-tuple-element.92.table), channel_id=1, source_target_pairs={{0,8},{8,0},{16,24},{24,16},{1,9},{9,1},{17,25},{25,17},{2,10},{10... | collective-permute-start | bytes 1228808 | tf_op jit(solution)/shard_map/ppermute | solution.py:183
  55.2 11.3 %collective-permute-start.17 = (bf16[800,256]{1,0:T(8,128)(2,1)S(1)}, bf16[800,256]{1,0:T(8,128)(2,1)S(1)}, u32[]{:S(2)}, u32[]{:S(2)}) collective-permute-start(bf16[800,256]{1,0:T(8,128)(2,1)S(1)} %get-tuple-element.92.table), channel_id=1, source_target_pairs={{0,16},{8,24},{16,0},{24,8},{1,17},{9,25},{17,1},{25,9},{2,18},{10... | collective-permute-start | bytes 1228808 | tf_op jit(solution)/shard_map/ppermute | solution.py:183
  60.6 11.6 %collective-permute-start.22 = (bf16[400,256]{1,0:T(8,128)(2,1)S(1)}, bf16[400,256]{1,0:T(8,128)(2,1)S(1)}, u32[]{:S(2)}, u32[]{:S(2)}) collective-permute-start(bf16[400,256]{1,0:T(8,128)(2,1)S(1)} %broadcast_select_fusion), channel_id=1, source_target_pairs={{0,4},{1,5},{2,6},{3,7},{4,0},{5,1},{6,2},{7,3},{8,12},{9,13},{10,... | collective-permute-start | bytes 614408 | tf_op jit(solution)/shard_map/ppermute | solution.py:183
  65.1 7.3 %collective-permute-start.18 = (bf16[400,256]{1,0:T(8,128)(2,1)S(1)}, bf16[400,256]{1,0:T(8,128)(2,1)S(1)}, u32[]{:S(2)}, u32[]{:S(2)}) collective-permute-start(bf16[400,256]{1,0:T(8,128)(2,1)S(1)} %slice.80), channel_id=1, source_target_pairs={{0,16},{8,24},{16,0},{24,8},{1,17},{9,25},{17,1},{25,9},{2,18},{10... | collective-permute-start | bytes 614408 | tf_op jit(solution)/shard_map/ppermute | solution.py:183
  66.5 5.9 %collective-permute-start.19 = (bf16[400,256]{1,0:T(8,128)(2,1)S(1)}, bf16[400,256]{1,0:T(8,128)(2,1)S(1)}, u32[]{:S(2)}, u32[]{:S(2)}) collective-permute-start(bf16[400,256]{1,0:T(8,128)(2,1)S(1)} %slice.81), channel_id=1, source_target_pairs={{0,8},{8,0},{16,24},{24,16},{1,9},{9,1},{17,25},{25,17},{2,10},{10... | collective-permute-start | bytes 614408 | tf_op jit(solution)/shard_map/ppermute | solution.py:183
  72.3 1.5 %collective-permute-start.23 = (bf16[400,256]{1,0:T(8,128)(2,1)S(1)}, bf16[400,256]{1,0:T(8,128)(2,1)S(1)}, u32[]{:S(2)}, u32[]{:S(2)}) collective-permute-start(bf16[400,256]{1,0:T(8,128)(2,1)S(1)} %broadcast_select_fusion.1), channel_id=1, source_target_pairs={{0,1},{1,0},{2,3},{3,2},{4,5},{5,4},{6,7},{7,6},{8,9},{9,8},{10,11... | collective-permute-start | bytes 614408 | tf_op jit(solution)/shard_map/ppermute | solution.py:183
  76.6 1.5 %collective-permute-start.24 = (bf16[400,256]{1,0:T(8,128)(2,1)S(1)}, bf16[400,256]{1,0:T(8,128)(2,1)S(1)}, u32[]{:S(2)}, u32[]{:S(2)}) collective-permute-start(bf16[400,256]{1,0:T(8,128)(2,1)S(1)} %broadcast_select_fusion.5), channel_id=1, source_target_pairs={{0,1},{1,0},{2,3},{3,2},{4,5},{5,4},{6,7},{7,6},{8,9},{9,8},{10,11... | collective-permute-start | bytes 614408 | tf_op jit(solution)/shard_map/ppermute | solution.py:183
  78.2 7.4 %collective-permute-start.25 = (bf16[400,256]{1,0:T(8,128)(2,1)S(1)}, bf16[400,256]{1,0:T(8,128)(2,1)S(1)}, u32[]{:S(2)}, u32[]{:S(2)}) collective-permute-start(bf16[400,256]{1,0:T(8,128)(2,1)S(1)} %add_convert_fusion.4), channel_id=1, source_target_pairs={{0,2},{1,3},{2,0},{3,1},{4,6},{5,7},{6,4},{7,5},{8,10},{9,11},{10,... | collective-permute-start | bytes 614408 | tf_op jit(solution)/shard_map/ppermute | solution.py:183
  78.7 11.5 %collective-permute-start.26 = (bf16[800,256]{1,0:T(8,128)(2,1)S(1)}, bf16[800,256]{1,0:T(8,128)(2,1)S(1)}, u32[]{:S(2)}, u32[]{:S(2)}) collective-permute-start(bf16[800,256]{1,0:T(8,128)(2,1)S(1)} %get-tuple-element.111), channel_id=1, source_target_pairs={{0,8},{8,0},{16,24},{24,16},{1,9},{9,1},{17,25},{25,17},{2,10},{10... | collective-permute-start | bytes 1228808 | tf_op jit(solution)/shard_map/ppermute | solution.py:183
  80.1 11.4 %collective-permute-start.28 = (bf16[800,256]{1,0:T(8,128)(2,1)S(1)}, bf16[800,256]{1,0:T(8,128)(2,1)S(1)}, u32[]{:S(2)}, u32[]{:S(2)}) collective-permute-start(bf16[800,256]{1,0:T(8,128)(2,1)S(1)} %get-tuple-element.114), channel_id=1, source_target_pairs={{0,16},{8,24},{16,0},{24,8},{1,17},{9,25},{17,1},{25,9},{2,18},{10... | collective-permute-start | bytes 1228808 | tf_op jit(solution)/shard_map/ppermute | solution.py:183
  85.7 11.9 %collective-permute-start.30 = (bf16[400,256]{1,0:T(8,128)(2,1)S(1)}, bf16[400,256]{1,0:T(8,128)(2,1)S(1)}, u32[]{:S(2)}, u32[]{:S(2)}) collective-permute-start(bf16[400,256]{1,0:T(8,128)(2,1)S(1)} %add_convert_fusion.3), channel_id=1, source_target_pairs={{0,4},{1,5},{2,6},{3,7},{4,0},{5,1},{6,2},{7,3},{8,12},{9,13},{10,... | collective-permute-start | bytes 614408 | tf_op jit(solution)/shard_map/ppermute | solution.py:183
  90.3 7.5 %collective-permute-start.27 = (bf16[400,256]{1,0:T(8,128)(2,1)S(1)}, bf16[400,256]{1,0:T(8,128)(2,1)S(1)}, u32[]{:S(2)}, u32[]{:S(2)}) collective-permute-start(bf16[400,256]{1,0:T(8,128)(2,1)S(1)} %add_convert_fusion.2), channel_id=1, source_target_pairs={{0,16},{8,24},{16,0},{24,8},{1,17},{9,25},{17,1},{25,9},{2,18},{10... | collective-permute-start | bytes 614408 | tf_op jit(solution)/shard_map/ppermute | solution.py:183
  91.5 6.3 %collective-permute-start.29 = (bf16[400,256]{1,0:T(8,128)(2,1)S(1)}, bf16[400,256]{1,0:T(8,128)(2,1)S(1)}, u32[]{:S(2)}, u32[]{:S(2)}) collective-permute-start(bf16[400,256]{1,0:T(8,128)(2,1)S(1)} %add_convert_fusion.1), channel_id=1, source_target_pairs={{0,8},{8,0},{16,24},{24,16},{1,9},{9,1},{17,25},{25,17},{2,10},{10... | collective-permute-start | bytes 614408 | tf_op jit(solution)/shard_map/ppermute | solution.py:183
  97.7 1.5 %collective-permute-start.31 = (bf16[400,256]{1,0:T(8,128)(2,1)S(1)}, bf16[400,256]{1,0:T(8,128)(2,1)S(1)}, u32[]{:S(2)}, u32[]{:S(2)}) collective-permute-start(bf16[400,256]{1,0:T(8,128)(2,1)S(1)} %add_convert_fusion), channel_id=1, source_target_pairs={{0,1},{1,0},{2,3},{3,2},{4,5},{5,4},{6,7},{7,6},{8,9},{9,8},{10,11... | collective-permute-start | bytes 614408 | tf_op jit(solution)/shard_map/ppermute | solution.py:183

commit v3 on v2

--- a/solution.py
+++ b/solution.py
@@ -59,72 +59,58 @@
         outs[(step + 1) * per_step - 1][...] = jnp.full(outs[0].shape, (root == member).astype(jnp.int32))
 
 
-def prepare_body(step, rel_ids, neg_ids, relation, tail, rel, counts):
-    full = relation.shape[1] // LANES * LANES
-    hot = onehot(rel_ids[step : step + 1, :], full + LANES)
-    rel[...] = (dot(relation[:, :full], hot[:full]) + dot(tail[...], hot[full:])).astype(BF)
+def prepare_body(step, rel_ids, neg_ids, relation, rel, counts):
+    hot = onehot(rel_ids[step : step + 1, :], relation.shape[1])
+    rel[...] = dot(relation[...], hot).astype(BF)
     negs = neg_ids[step : step + 1, :]
     sub = lax.broadcasted_iota(jnp.int32, (counts.shape[0], negs.shape[1]), 0)
     counts[...] = jnp.sum((sub == negs).astype(F32), 1, keepdims=True)
 
 
-def query_body(step, src, real, imag, rel, table, counts, query, probs, top, total):
+def place(step, groups, count, rows, dest_groups, dest_rows, first=0):
+    near = dest_groups[step] ^ lax.axis_index("group")
+    return onehot(near * rows + dest_rows[step : step + 1, :], count * rows, first * rows)
+
+
+def dest_body(step, groups, dest_groups, dest_rows, table, *refs):
+    shards, dest = refs[:-1], refs[-1]
+    hot = place(step, groups, groups - 1, table.shape[1], dest_groups, dest_rows)
+    whole = jnp.concatenate([x[...] for x in (table, *shards)], 1)
+    dest[...] = dot(whole, hot).astype(BF)
+
+
+def far_body(step, groups, dest_groups, dest_rows, near, first, second, dest):
+    rows, at = first.shape[1], first.shape[0]
+    hot = place(step, groups, 1, rows, dest_groups, dest_rows, groups - 1)
+    dest[:at, :] = near[:at, :] + dot(first[...], hot).astype(BF)
+    dest[at:, :] = near[at:, :] + dot(second[...], hot).astype(BF)
+
+
+def source_body(
+    step, src, real, imag, rel, table, counts, dest, query, out_r, out_i, coef_pos, coef_neg
+):
     rows, half = table.shape[1], real.shape[0]
-    hot = onehot(src[step : step + 1, :], rows)
-    sr, si = dot(real[...], hot), dot(imag[...], hot)
+    back = onehot(src[step : step + 1, :], rows)
+    sr, si = dot(real[...], back), dot(imag[...], back)
     rr, ri = rel[:half, :].astype(F32), rel[half:, :].astype(F32)
     query[:half, :] = (sr * rr - si * ri).astype(BF)
     query[half:, :] = (sr * ri + si * rr).astype(BF)
     scores = dot_c(table[...], query[...])
     count = counts[...]
     scores = jnp.where(count > 0.0, scores, -jnp.inf)
-    best = jnp.max(scores, 0, keepdims=True)
-    prob = count * jnp.exp(scores - best)
-    probs[...] = prob
-    top[...] = best
-    total[...] = jnp.sum(prob, 0, keepdims=True)
-
-
-def place(step, groups, count, rows, dest_groups, dest_rows, first=0):
-    near = dest_groups[step] ^ lax.axis_index("group")
-    return onehot(near * rows + dest_rows[step : step + 1, :], count * rows, first * rows)
-
-
-def dest_body(step, groups, dest_groups, dest_rows, table, *refs):
-    shards, dest = refs[:-1], refs[-1]
-    hot = place(step, groups, groups - 1, table.shape[1], dest_groups, dest_rows)
-    whole = jnp.concatenate([x[...] for x in (table, *shards)], 1)
-    dest[...] = dot(whole, hot).astype(BF)
-
-
-def far_body(step, groups, dest_groups, dest_rows, near, far_r, far_i, dest):
-    rows, half = far_r.shape[1], far_r.shape[0]
-    hot = place(step, groups, 1, rows, dest_groups, dest_rows, groups - 1)
-    for part, far in enumerate((far_r, far_i)):
-        span = slice(part * half, (part + 1) * half)
-        dest[span, :] = near[span, :] + dot(far[...], hot).astype(BF)
-
-
-def source_body(
-    step, src, query, probs, top_neg, total_neg, rel, table, dest, out_r, out_i, coef_pos, coef_neg
-):
-    rows, half = table.shape[1], out_r.shape[0]
     dr, di = dest[:half, :].astype(F32), dest[half:, :].astype(F32)
     qr, qi = query[:half, :].astype(F32), query[half:, :].astype(F32)
     positive = jnp.sum(qr * dr + qi * di, 0, keepdims=True)
-    best = top_neg[...]
-    top = jnp.maximum(best, positive)
+    top = jnp.maximum(jnp.max(scores, 0, keepdims=True), positive)
     pos_exp = jnp.exp(positive - top)
-    scale = jnp.exp(best - top)
-    total = pos_exp + scale * total_neg[...]
+    neg_exp = count * jnp.exp(scores - top)
+    total = pos_exp + jnp.sum(neg_exp, 0, keepdims=True)
     pos = pos_exp / total - 1.0
-    neg = (probs[...] * (scale / total)).astype(BF)
+    neg = (neg_exp * (1.0 / total)).astype(BF)
     coef_pos[...] = pos
     coef_neg[...] = neg
     gr = pos * dr + dot(table[:half, :], neg)
     gi = pos * di + dot(table[half:, :], neg)
-    rr, ri = rel[:half, :].astype(F32), rel[half:, :].astype(F32)
-    back = onehot(src[step : step + 1, :], rows)
     out_r[...] = dot_t((gr * rr + gi * ri).astype(BF), back).astype(BF)
     out_i[...] = dot_t((gi * rr - gr * ri).astype(BF), back).astype(BF)
 
@@ -137,14 +123,8 @@
         q = query[span, :]
         spread = dot_t((coef_pos[...] * q.astype(F32)).astype(BF), hot)
         base_grad[span, :] = spread[:, :rows] + dot_t(q, coef_neg[...])
-        grads = [spread[:, k * rows : (k + 1) * rows].astype(BF) for k in range(1, groups)]
-        if groups == 4:
-            sends[part][:half, :] = grads[2]
-            sends[part][half:, :] = grads[part]
-            sends[2 + part][...] = grads[1 - part]
-        else:
-            for send, grad in zip(sends, grads):
-                send[span, :] = grad
+        for k in range(1, groups):
+            sends[2 * k - 2 + part][...] = spread[:, k * rows : (k + 1) * rows].astype(BF)
 
 
 def merge_body(halves, base_grad, *refs):
@@ -197,28 +177,30 @@
 
 
 def gather_shards(table):
-    groups, half = lax.axis_size("group"), table.shape[0] // 2
+    groups, width = lax.axis_size("group"), table.shape[0]
     near = [shift(table, "group", k) for k in range(1, groups - 1)]
     if groups != 4:
-        far = [shift(table[:half], "group", groups - 1), shift(table[half:], "group", groups - 1)]
-    else:
-        far = [shift(near[0][:half], "group", 2), shift(near[1][half:], "group", 1)]
-    return near + far
+        far = shift(table, "group", groups - 1)
+        return near + [far[: width // 2], far[width // 2 :]]
+    at = width * 3 // 5 // 16 * 16
+    return near + [shift(near[0][:at], "group", 2), shift(near[1][at:], "group", 1)]
 
 
 def spread_grads(sends):
-    groups, half = lax.axis_size("group"), sends[0].shape[0] // 2
+    groups = lax.axis_size("group")
     if groups != 4:
-        got = [(None, shift(x, "group", k + 1)) for k, x in enumerate(sends)]
-        return lambda *earlier: got
-    x, y = shift(sends[0], "group", 1), shift(sends[1], "group", 2)
+        parts = [(p, shift(sends[2 * k - 2 + p], "group", k)) for k in range(1, groups) for p in (0, 1)]
+        return [x for _, x in parts[:2]], lambda *earlier: parts
+    xr, xi, yr, yi, dr, di = sends
+    x, y = shift(dr, "group", 1), shift(di, "group", 2)
+    real, imag = shift(xr, "group", 1), shift(yi, "group", 2)
 
     def rest(*earlier):
-        y_real = shift(add(after(sends[2], *earlier), x[:half]), "group", 2)
-        x_imag = shift(add(after(sends[3], *earlier), y[:half]), "group", 1)
-        return [(0, y_real), (1, x_imag), (0, x[half:]), (1, y[half:])]
-
-    return rest
+        y_real = shift(add(after(yr, *earlier), x), "group", 2)
+        x_imag = shift(add(after(xi, *earlier), y), "group", 1)
+        return [(0, y_real), (1, x_imag), (0, real), (1, imag)]
+
+    return [x, y], rest
 
 
 def per_device(
@@ -240,8 +222,6 @@
     table = entity.T
     state = adagrad_state[None, :]
     rel_t = relation.T
-    full = rel_t.shape[1] // LANES * LANES
-    groups = lax.axis_size("group")
     dest_groups = jnp.transpose(dest_groups, (0, 2, 1))
     bits = z_bits()
     kinds = 2 + len(bits)
@@ -250,12 +230,10 @@
         return call(masks_body, [sds((1, rows), jnp.int32)] * (steps * kinds), owners, smem=(0,))
 
     def prepare(step, earlier):
-        held = after(rel_t, earlier)
-        tail = jnp.pad(held[:, full:], ((0, 0), (0, LANES - rel_t.shape[1] + full)))
         return call(
             functools.partial(prepare_body, step),
             [sds((width, edges), BF), sds((rows, 1), F32)],
-            relation_ids, negative_ids, held, tail,
+            relation_ids, negative_ids, after(rel_t, earlier),
         )
 
     for step in range(steps):
@@ -284,24 +262,20 @@
             dest_groups, dest_rows, near, *shards[-2:],
             flops=8 * 10**9,
         )
-        query, probs, top, total = call(
-            functools.partial(query_body, step),
-            [sds((width, edges), BF), sds((rows, edges), F32), sds((1, edges), F32), sds((1, edges), F32)],
-            after(source_ids, dest), *block, rel, table, counts,
-        )
-        out_r, out_i, coef_pos, coef_neg = call(
+        query, out_r, out_i, coef_pos, coef_neg = call(
             functools.partial(source_body, step),
-            [sds((half, rows), BF)] * 2 + [sds((1, edges), F32), sds((rows, edges), BF)],
-            source_ids, query, probs, top, total, rel, table, dest,
+            [sds((width, edges), BF)]
+            + [sds((half, rows), BF)] * 2
+            + [sds((1, edges), F32), sds((rows, edges), BF)],
+            source_ids, *block, rel, table, counts, dest,
         )
         give = shift(jnp.where(first, out_i, out_r), "member", 1)
-        shapes = [(width, rows)] * 2 + [(half, rows)] * 2 if groups == 4 else [(width, rows)] * (groups - 1)
         base_grad, *sends = call(
             functools.partial(spread_body, step, groups),
-            [sds((width, rows), F32)] + [sds(shape, BF) for shape in shapes],
+            [sds((width, rows), F32)] + [sds((half, rows), BF)] * (2 * groups - 2),
             dest_groups, dest_rows, query, coef_pos, coef_neg,
         )
-        rest = spread_grads(sends)
+        early, rest = spread_grads(sends)
         part = add(jnp.where(first, out_r, out_i), after(give, base_grad))
         for turn, bit in enumerate(bits):
             part = add(part, shift(part, "member", bit))

time: 100 us -> 99.4 us (level)
  waiting for transfers between devices: 42 us -> 37 us
  starting transfers between devices: 38.5 us -> 43.2 us
    ppermute x32 -> x36, waiting for transfers between devices: 42 us -> 37 us  [shift(): return lax.ppermute(value, axis, [(i, i ^ bit) for i in range(size)])]
    ppermute x32 -> x36, starting transfers between devices: 38.5 us -> 43.2 us  [shift(): return lax.ppermute(value, axis, [(i, i ^ bit) for i in range(size)])]
    pallas_call x17 -> x15, Pallas kernels: 15.3 us -> 14.8 us  [call(): pl.pallas_call(body, out_shape=outs, in_specs=[SMEM if i in smem else VME...]
  transfers between devices with their start and end apart: 32 -> 36, of which waited for: 18 -> 17; matrix products, arithmetic and copies ran while one was open for 1% -> 1% of each run, Pallas kernels for 9% -> 9%
where the time goes in v3:
time: 99.4 us; the launch traced here: 99.2 us
  starting transfers between devices  43.2 us (43%)
  waiting for transfers between devices  37 us (37%)
  Pallas kernels  14.8 us (15%)
  other arithmetic  2.37 us (2%)
  between operations  1.11 us (1%)
    ppermute x36, starting transfers between devices, shift(): return lax.ppermute(value, axis, [(i, i ^ bit) for i in range(size)])  43.2 us
    ppermute x36, waiting for transfers between devices, shift(): return lax.ppermute(value, axis, [(i, i ^ bit) for i in range(size)])  37 us
    pallas_call x15, Pallas kernels, call(): pl.pallas_call(body, out_shape=outs, in_specs=[SMEM if i in smem else VME...  14.8 us
  transfers between devices with their start and end apart: 36, of which 17 were waited for; matrix products, arithmetic and copies ran while one was open for 1% of the time, Pallas kernels for 9%

profile of v3, /device:TPU:0, one launch (start us, length us, event | category | flops | bytes accessed | tf_op | source)
XLA Modules:
  0.0 99.2 jit_solution(7438482367368444823)
XLA Ops:
  0.7 1.2 %broadcast_select_fusion.12 = (bf16[400,256]{1,0:T(8,128)(2,1)S(1)}, bf16[400,256]{1,0:T(8,128)(2,1)S(1)}) fusion(pred[]{:T(512)S(6)} %eq.5, bf16[800,256]{1,0:T(8,128)(2,1)} %bitcast.8), kind=kLoop, calls=%fused_computation.27 | loop fusion | flops 204800 | bytes 819201 | tf_op jit(solution)/shard_map/jit(_where)/select_n | solution.py:241
  2.4 0.7 copy-done.8
  3.8 2.8 %collective-permute-start.1 = (bf16[400,256]{1,0:T(8,128)(2,1)S(1)}, bf16[400,256]{1,0:T(8,128)(2,1)S(1)}, u32[]{:S(2)}, u32[]{:S(2)}) collective-permute-start(bf16[400,256]{1,0:T(8,128)(2,1)S(1)} %broadcast_select_fusion.2), channel_id=1, source_target_pairs={{0,2},{1,3},{2,0},{3,1},{4,6},{5,7},{6,4},{7,5},{8,10},{9,11},{10,... | collective-permute-start | bytes 614408 | tf_op jit(solution)/shard_map/ppermute | solution.py:163
  6.6 1.5 %collective-permute-start.3 = (bf16[800,256]{1,0:T(8,128)(2,1)}, bf16[800,256]{1,0:T(8,128)(2,1)S(1)}, u32[]{:S(2)}, u32[]{:S(2)}) collective-permute-start(bf16[800,256]{1,0:T(8,128)(2,1)} %bitcast.9), channel_id=1, source_target_pairs={{0,8},{8,0},{16,24},{24,16},{1,9},{9,1},{17,25},{25,17},{2,10},{10... | collective-permute-start | bytes 1228808 | tf_op jit(solution)/shard_map/ppermute | solution.py:163
  8.1 1.5 %collective-permute-start.4 = (bf16[800,256]{1,0:T(8,128)(2,1)}, bf16[800,256]{1,0:T(8,128)(2,1)S(1)}, u32[]{:S(2)}, u32[]{:S(2)}) collective-permute-start(bf16[800,256]{1,0:T(8,128)(2,1)} %bitcast.10), channel_id=1, source_target_pairs={{0,16},{8,24},{16,0},{24,8},{1,17},{9,25},{17,1},{25,9},{2,18},{10... | collective-permute-start | bytes 1228808 | tf_op jit(solution)/shard_map/ppermute | solution.py:163
  9.6 2.6 %collective-permute-done.1 = bf16[400,256]{1,0:T(8,128)(2,1)S(1)} collective-permute-done((bf16[400,256]{1,0:T(8,128)(2,1)S(1)}, bf16[400,256]{1,0:T(8,128)(2,1)S(1)}, u32[]{:S(2)}, u32[]{:S(2)}) %collective-permute-start.1) | collective-permute-done | bytes 204832 | tf_op jit(solution)/shard_map/ppermute | solution.py:163
  12.2 2.8 %collective-permute-start.2 = (bf16[400,256]{1,0:T(8,128)(2,1)S(1)}, bf16[400,256]{1,0:T(8,128)(2,1)S(1)}, u32[]{:S(2)}, u32[]{:S(2)}) collective-permute-start(bf16[400,256]{1,0:T(8,128)(2,1)S(1)} %broadcast_select_fusion.3), channel_id=1, source_target_pairs={{0,4},{1,5},{2,6},{3,7},{4,0},{5,1},{6,2},{7,3},{8,12},{9,13},{10,... | collective-permute-start | bytes 614408 | tf_op jit(solution)/shard_map/ppermute | solution.py:163
  15.0 3.2 %collective-permute-done.3.refs_0_ = bf16[800,256]{1,0:T(8,128)(2,1)S(1)} collective-permute-done((bf16[800,256]{1,0:T(8,128)(2,1)}, bf16[800,256]{1,0:T(8,128)(2,1)S(1)}, u32[]{:S(2)}, u32[]{:S(2)}) %collective-permute-start.3) | collective-permute-done | bytes 409632 | tf_op jit(solution)/shard_map/ppermute | solution.py:163
  18.2 1.6 %collective-permute-start.6 = (bf16[480,256]{1,0:T(8,128)(2,1)S(1)}, bf16[480,256]{1,0:T(8,128)(2,1)S(1)}, u32[]{:S(2)}, u32[]{:S(2)}) collective-permute-start(bf16[480,256]{1,0:T(8,128)(2,1)S(1)} %slice.34), channel_id=1, source_target_pairs={{0,16},{8,24},{16,0},{24,8},{1,17},{9,25},{17,1},{25,9},{2,18},{10... | collective-permute-start | bytes 737288 | tf_op jit(solution)/shard_map/ppermute | solution.py:163
  19.9 1.6 %collective-permute-start.7 = (bf16[320,256]{1,0:T(8,128)(2,1)S(1)}, bf16[320,256]{1,0:T(8,128)(2,1)S(1)}, u32[]{:S(2)}, u32[]{:S(2)}) collective-permute-start(bf16[320,256]{1,0:T(8,128)(2,1)S(1)} %slice.35), channel_id=1, source_target_pairs={{0,8},{8,0},{16,24},{24,16},{1,9},{9,1},{17,25},{25,17},{2,10},{10... | collective-permute-start | bytes 491528 | tf_op jit(solution)/shard_map/ppermute | solution.py:163
  21.4 1.4 %shard_map.106 = (bf16[800,512]{1,0:T(8,128)(2,1)S(1)}, f32[256,1]{1,0:T(8,128)S(1)}) custom-call(s32[2,512]{1,0:T(2,128)S(1)} %copy-done.5, s32[2,1000]{1,0:T(2,128)S(1)} %copy-done.4, bf16[800,1345]{1,0:T(8,128)(2,1)S(1)} %bitcast.6), custom_call_target="tpu_custom_call" | custom-call | flops 1000 | bytes 1000 | tf_op jit(solution)/shard_map/pallas_call | solution.py:19
  22.9 0.8 shard_map.105.near
  24.4 0.8 collective-permute-done.7.second
  25.9 2.2 %shard_map.108 = (bf16[800,512]{1,0:T(8,128)(2,1)S(1)}, bf16[400,256]{1,0:T(8,128)(2,1)S(1)}, bf16[400,256]{1,0:T(8,128)(2,1)S(1)}, f32[1,512]{1,0:T(1,128)S(1)}, bf16[256,512]{1,0:T(8,128)(2,1)S(1)}) custom-call(s32[2,512]{1,0:T(2,128)S(1)} %copy-done.6, bf16[400,256]{1,0:T(8,128)(2,1)S(1)} %get-tuple-element.121.real, ...), custom_call_target="tpu_custom_call" | custom-call | flops 1000 | bytes 1000 | tf_op jit(solution)/shard_map/pallas_call | solution.py:19
  28.3 1.3 %shard_map.109 = (f32[800,256]{1,0:T(8,128)S(1)}, bf16[400,256]{1,0:T(8,128)(2,1)S(1)}, bf16[400,256]{1,0:T(8,128)(2,1)S(1)}, bf16[400,256]{1,0:T(8,128)(2,1)S(1...) custom-call(s32[2,1,512]{2,1,0:T(1,128)S(1)} %bitcast.16, ...), custom_call_target="tpu_custom_call" | custom-call | flops 1000 | bytes 1000 | tf_op jit(solution)/shard_map/pallas_call | solution.py:19
  29.8 0.7 collective-permute-start.9
  30.5 1.5 %collective-permute-start.10 = (bf16[400,256]{1,0:T(8,128)(2,1)S(1)}, bf16[400,256]{1,0:T(8,128)(2,1)S(1)}, u32[]{:S(2)}, u32[]{:S(2)}) collective-permute-start(bf16[400,256]{1,0:T(8,128)(2,1)S(1)} %get-tuple-element.75), channel_id=1, source_target_pairs={{0,8},{8,0},{16,24},{24,16},{1,9},{9,1},{17,25},{25,17},{2,10},{10... | collective-permute-start | bytes 614408 | tf_op jit(solution)/shard_map/ppermute | solution.py:163
  32.1 1.5 %collective-permute-start.12 = (bf16[400,256]{1,0:T(8,128)(2,1)S(1)}, bf16[400,256]{1,0:T(8,128)(2,1)S(1)}, u32[]{:S(2)}, u32[]{:S(2)}) collective-permute-start(bf16[400,256]{1,0:T(8,128)(2,1)S(1)} %get-tuple-element.78), channel_id=1, source_target_pairs={{0,16},{8,24},{16,0},{24,8},{1,17},{9,25},{17,1},{25,9},{2,18},{10... | collective-permute-start | bytes 614408 | tf_op jit(solution)/shard_map/ppermute | solution.py:163
  34.6 2.6 %collective-permute-done.9 = bf16[400,256]{1,0:T(8,128)(2,1)S(1)} collective-permute-done((bf16[400,256]{1,0:T(8,128)(2,1)S(1)}, bf16[400,256]{1,0:T(8,128)(2,1)S(1)}, u32[]{:S(2)}, u32[]{:S(2)}) %collective-permute-start.9) | collective-permute-done | bytes 204832 | tf_op jit(solution)/shard_map/ppermute | solution.py:163
  37.3 2.6 %collective-permute-start.16 = (bf16[400,256]{1,0:T(8,128)(2,1)S(1)}, bf16[400,256]{1,0:T(8,128)(2,1)S(1)}, u32[]{:S(2)}, u32[]{:S(2)}) collective-permute-start(bf16[400,256]{1,0:T(8,128)(2,1)S(1)} %add_convert_fusion.8), channel_id=1, source_target_pairs={{0,4},{1,5},{2,6},{3,7},{4,0},{5,1},{6,2},{7,3},{8,12},{9,13},{10,... | collective-permute-start | bytes 614408 | tf_op jit(solution)/shard_map/ppermute | solution.py:163
  40.0 1.6 %collective-permute-start.11 = (bf16[400,256]{1,0:T(8,128)(2,1)S(1)}, bf16[400,256]{1,0:T(8,128)(2,1)S(1)}, u32[]{:S(2)}, u32[]{:S(2)}) collective-permute-start(bf16[400,256]{1,0:T(8,128)(2,1)S(1)} %add_convert_fusion.7), channel_id=1, source_target_pairs={{0,16},{8,24},{16,0},{24,8},{1,17},{9,25},{17,1},{25,9},{2,18},{10... | collective-permute-start | bytes 614408 | tf_op jit(solution)/shard_map/ppermute | solution.py:163
  41.6 1.6 %collective-permute-start.13 = (bf16[400,256]{1,0:T(8,128)(2,1)S(1)}, bf16[400,256]{1,0:T(8,128)(2,1)S(1)}, u32[]{:S(2)}, u32[]{:S(2)}) collective-permute-start(bf16[400,256]{1,0:T(8,128)(2,1)S(1)} %add_convert_fusion.6), channel_id=1, source_target_pairs={{0,8},{8,0},{16,24},{24,16},{1,9},{9,1},{17,25},{25,17},{2,10},{10... | collective-permute-start | bytes 614408 | tf_op jit(solution)/shard_map/ppermute | solution.py:163
  43.2 1.4 %shard_map.111 = (bf16[800,512]{1,0:T(8,128)(2,1)S(1)}, f32[256,1]{1,0:T(8,128)S(1)}) custom-call(s32[2,512]{1,0:T(2,128)S(1)} %copy-done.5, s32[2,1000]{1,0:T(2,128)S(1)} %copy-done.4, bf16[800,1345]{1,0:T(8,128)(2,1)S(1)} %bitcast.7), custom_call_target="tpu_custom_call" | custom-call | flops 1000 | bytes 1000 | tf_op jit(solution)/shard_map/pallas_call | solution.py:19
  44.6 4.6 %collective-permute-done.16 = bf16[400,256]{1,0:T(8,128)(2,1)S(1)} collective-permute-done((bf16[400,256]{1,0:T(8,128)(2,1)S(1)}, bf16[400,256]{1,0:T(8,128)(2,1)S(1)}, u32[]{:S(2)}, u32[]{:S(2)}) %collective-permute-start.16) | collective-permute-done | bytes 204832 | tf_op jit(solution)/shard_map/ppermute | solution.py:163
  49.5 1.3 %collective-permute-done.17 = bf16[400,256]{1,0:T(8,128)(2,1)S(1)} collective-permute-done((bf16[400,256]{1,0:T(8,128)(2,1)S(1)}, bf16[400,256]{1,0:T(8,128)(2,1)S(1)}, u32[]{:S(2)}, u32[]{:S(2)}) %collective-permute-start.17) | collective-permute-done | bytes 204832 | tf_op jit(solution)/shard_map/ppermute | solution.py:163
  51.4 1.3 %collective-permute-done.18 = bf16[400,256]{1,0:T(8,128)(2,1)S(1)} collective-permute-done((bf16[400,256]{1,0:T(8,128)(2,1)S(1)}, bf16[400,256]{1,0:T(8,128)(2,1)S(1)}, u32[]{:S(2)}, u32[]{:S(2)}) %collective-permute-start.18) | collective-permute-done | bytes 204832 | tf_op jit(solution)/shard_map/ppermute | solution.py:163
  53.4 1.5 %collective-permute-start.21 = (bf16[800,256]{1,0:T(8,128)(2,1)S(1)}, bf16[800,256]{1,0:T(8,128)(2,1)S(1)}, u32[]{:S(2)}, u32[]{:S(2)}) collective-permute-start(bf16[800,256]{1,0:T(8,128)(2,1)S(1)} %get-tuple-element.86.table), channel_id=1, source_target_pairs={{0,8},{8,0},{16,24},{24,16},{1,9},{9,1},{17,25},{25,17},{2,10},{10... | collective-permute-start | bytes 1228808 | tf_op jit(solution)/shard_map/ppermute | solution.py:163
  54.9 1.6 %collective-permute-start.22 = (bf16[800,256]{1,0:T(8,128)(2,1)S(1)}, bf16[800,256]{1,0:T(8,128)(2,1)S(1)}, u32[]{:S(2)}, u32[]{:S(2)}) collective-permute-start(bf16[800,256]{1,0:T(8,128)(2,1)S(1)} %get-tuple-element.86.table), channel_id=1, source_target_pairs={{0,16},{8,24},{16,0},{24,8},{1,17},{9,25},{17,1},{25,9},{2,18},{10... | collective-permute-start | bytes 1228808 | tf_op jit(solution)/shard_map/ppermute | solution.py:163
  56.4 3.4 %collective-permute-done.19 = bf16[400,256]{1,0:T(8,128)(2,1)S(1)} collective-permute-done((bf16[400,256]{1,0:T(8,128)(2,1)S(1)}, bf16[400,256]{1,0:T(8,128)(2,1)S(1)}, u32[]{:S(2)}, u32[]{:S(2)}) %collective-permute-start.19) | collective-permute-done | bytes 204832 | tf_op jit(solution)/shard_map/ppermute | solution.py:163
  59.9 2.3 %collective-permute-start.20 = (bf16[400,256]{1,0:T(8,128)(2,1)S(1)}, bf16[400,256]{1,0:T(8,128)(2,1)S(1)}, u32[]{:S(2)}, u32[]{:S(2)}) collective-permute-start(bf16[400,256]{1,0:T(8,128)(2,1)S(1)} %broadcast_select_fusion), channel_id=1, source_target_pairs={{0,4},{1,5},{2,6},{3,7},{4,0},{5,1},{6,2},{7,3},{8,12},{9,13},{10,... | collective-permute-start | bytes 614408 | tf_op jit(solution)/shard_map/ppermute | solution.py:163
  62.2 2.4 %collective-permute-done.21.refs_0_ = bf16[800,256]{1,0:T(8,128)(2,1)S(1)} collective-permute-done((bf16[800,256]{1,0:T(8,128)(2,1)S(1)}, bf16[800,256]{1,0:T(8,128)(2,1)S(1)}, u32[]{:S(2)}, u32[]{:S(2)}) %collective-permute-start.21) | collective-permute-done | bytes 409632 | tf_op jit(solution)/shard_map/ppermute | solution.py:163
  64.6 1.6 %collective-permute-start.24 = (bf16[480,256]{1,0:T(8,128)(2,1)S(1)}, bf16[480,256]{1,0:T(8,128)(2,1)S(1)}, u32[]{:S(2)}, u32[]{:S(2)}) collective-permute-start(bf16[480,256]{1,0:T(8,128)(2,1)S(1)} %slice.36), channel_id=1, source_target_pairs={{0,16},{8,24},{16,0},{24,8},{1,17},{9,25},{17,1},{25,9},{2,18},{10... | collective-permute-start | bytes 737288 | tf_op jit(solution)/shard_map/ppermute | solution.py:163
  66.2 1.5 %collective-permute-start.25 = (bf16[320,256]{1,0:T(8,128)(2,1)S(1)}, bf16[320,256]{1,0:T(8,128)(2,1)S(1)}, u32[]{:S(2)}, u32[]{:S(2)}) collective-permute-start(bf16[320,256]{1,0:T(8,128)(2,1)S(1)} %slice.37), channel_id=1, source_target_pairs={{0,8},{8,0},{16,24},{24,16},{1,9},{9,1},{17,25},{25,17},{2,10},{10... | collective-permute-start | bytes 491528 | tf_op jit(solution)/shard_map/ppermute | solution.py:163
  67.8 0.8 shard_map.113.near
  68.6 2.9 %collective-permute-done.20 = bf16[400,256]{1,0:T(8,128)(2,1)S(1)} collective-permute-done((bf16[400,256]{1,0:T(8,128)(2,1)S(1)}, bf16[400,256]{1,0:T(8,128)(2,1)S(1)}, u32[]{:S(2)}, u32[]{:S(2)}) %collective-permute-start.20) | collective-permute-done | bytes 204832 | tf_op jit(solution)/shard_map/ppermute | solution.py:163
  72.1 1.0 %collective-permute-done.23 = bf16[400,256]{1,0:T(8,128)(2,1)S(1)} collective-permute-done((bf16[400,256]{1,0:T(8,128)(2,1)S(1)}, bf16[400,256]{1,0:T(8,128)(2,1)S(1)}, u32[]{:S(2)}, u32[]{:S(2)}) %collective-permute-start.23) | collective-permute-done | bytes 204832 | tf_op jit(solution)/shard_map/ppermute | solution.py:163
  73.1 2.4 %shard_map.115 = (bf16[800,512]{1,0:T(8,128)(2,1)S(1)}, bf16[400,256]{1,0:T(8,128)(2,1)S(1)}, bf16[400,256]{1,0:T(8,128)(2,1)S(1)}, f32[1,512]{1,0:T(1,128)S(1)}, bf16[256,512]{1,0:T(8,128)(2,1)S(1)}) custom-call(s32[2,512]{1,0:T(2,128)S(1)} %copy-done.6, bf16[400,256]{1,0:T(8,128)(2,1)S(1)} %get-tuple-element.119.real, ...), custom_call_target="tpu_custom_call" | custom-call | flops 1000 | bytes 1000 | tf_op jit(solution)/shard_map/pallas_call | solution.py:19
  75.8 1.4 %shard_map.116 = (f32[800,256]{1,0:T(8,128)S(1)}, bf16[400,256]{1,0:T(8,128)(2,1)S(1)}, bf16[400,256]{1,0:T(8,128)(2,1)S(1)}, bf16[400,256]{1,0:T(8,128)(2,1)S(1...) custom-call(s32[2,1,512]{2,1,0:T(1,128)S(1)} %bitcast.19, ...), custom_call_target="tpu_custom_call" | custom-call | flops 1000 | bytes 1000 | tf_op jit(solution)/shard_map/pallas_call | solution.py:19
  77.2 0.7 collective-permute-start.27
  77.9 1.5 %collective-permute-start.28 = (bf16[400,256]{1,0:T(8,128)(2,1)S(1)}, bf16[400,256]{1,0:T(8,128)(2,1)S(1)}, u32[]{:S(2)}, u32[]{:S(2)}) collective-permute-start(bf16[400,256]{1,0:T(8,128)(2,1)S(1)} %get-tuple-element.101), channel_id=1, source_target_pairs={{0,8},{8,0},{16,24},{24,16},{1,9},{9,1},{17,25},{25,17},{2,10},{10... | collective-permute-start | bytes 614408 | tf_op jit(solution)/shard_map/ppermute | solution.py:163
  79.5 1.5 %collective-permute-start.30 = (bf16[400,256]{1,0:T(8,128)(2,1)S(1)}, bf16[400,256]{1,0:T(8,128)(2,1)S(1)}, u32[]{:S(2)}, u32[]{:S(2)}) collective-permute-start(bf16[400,256]{1,0:T(8,128)(2,1)S(1)} %get-tuple-element.104), channel_id=1, source_target_pairs={{0,16},{8,24},{16,0},{24,8},{1,17},{9,25},{17,1},{25,9},{2,18},{10... | collective-permute-start | bytes 614408 | tf_op jit(solution)/shard_map/ppermute | solution.py:163
  82.0 2.6 %collective-permute-done.27 = bf16[400,256]{1,0:T(8,128)(2,1)S(1)} collective-permute-done((bf16[400,256]{1,0:T(8,128)(2,1)S(1)}, bf16[400,256]{1,0:T(8,128)(2,1)S(1)}, u32[]{:S(2)}, u32[]{:S(2)}) %collective-permute-start.27) | collective-permute-done | bytes 204832 | tf_op jit(solution)/shard_map/ppermute | solution.py:163
  84.7 2.4 %collective-permute-start.34 = (bf16[400,256]{1,0:T(8,128)(2,1)S(1)}, bf16[400,256]{1,0:T(8,128)(2,1)S(1)}, u32[]{:S(2)}, u32[]{:S(2)}) collective-permute-start(bf16[400,256]{1,0:T(8,128)(2,1)S(1)} %add_convert_fusion.3), channel_id=1, source_target_pairs={{0,4},{1,5},{2,6},{3,7},{4,0},{5,1},{6,2},{7,3},{8,12},{9,13},{10,... | collective-permute-start | bytes 614408 | tf_op jit(solution)/shard_map/ppermute | solution.py:163
  87.2 1.5 %collective-permute-start.29 = (bf16[400,256]{1,0:T(8,128)(2,1)S(1)}, bf16[400,256]{1,0:T(8,128)(2,1)S(1)}, u32[]{:S(2)}, u32[]{:S(2)}) collective-permute-start(bf16[400,256]{1,0:T(8,128)(2,1)S(1)} %add_convert_fusion.2), channel_id=1, source_target_pairs={{0,16},{8,24},{16,0},{24,8},{1,17},{9,25},{17,1},{25,9},{2,18},{10... | collective-permute-start | bytes 614408 | tf_op jit(solution)/shard_map/ppermute | solution.py:163
  88.7 1.5 %collective-permute-start.31 = (bf16[400,256]{1,0:T(8,128)(2,1)S(1)}, bf16[400,256]{1,0:T(8,128)(2,1)S(1)}, u32[]{:S(2)}, u32[]{:S(2)}) collective-permute-start(bf16[400,256]{1,0:T(8,128)(2,1)S(1)} %add_convert_fusion.1), channel_id=1, source_target_pairs={{0,8},{8,0},{16,24},{24,16},{1,9},{9,1},{17,25},{25,17},{2,10},{10... | collective-permute-start | bytes 614408 | tf_op jit(solution)/shard_map/ppermute | solution.py:163
  90.3 6.3 %collective-permute-done.34 = bf16[400,256]{1,0:T(8,128)(2,1)S(1)} collective-permute-done((bf16[400,256]{1,0:T(8,128)(2,1)S(1)}, bf16[400,256]{1,0:T(8,128)(2,1)S(1)}, u32[]{:S(2)}, u32[]{:S(2)}) %collective-permute-start.34) | collective-permute-done | bytes 204832 | tf_op jit(solution)/shard_map/ppermute | solution.py:163
  96.9 1.3 %collective-permute-done.35 = bf16[400,256]{1,0:T(8,128)(2,1)S(1)} collective-permute-done((bf16[400,256]{1,0:T(8,128)(2,1)S(1)}, bf16[400,256]{1,0:T(8,128)(2,1)S(1)}, u32[]{:S(2)}, u32[]{:S(2)}) %collective-permute-start.35) | collective-permute-done | bytes 204832 | tf_op jit(solution)/shard_map/ppermute | solution.py:163
  98.2 1.0 %shard_map.118 = (bf16[800,256]{1,0:T(8,128)(2,1)}, f32[1,256]{1,0:T(1,128)}) custom-call(bf16[800,256]{1,0:T(8,128)(2,1)S(1)} %get-tuple-element.86.table, f32[1,256]{1,0:T(1,128)S(1)} %get-tuple-element.87.state, f32[800,256]{1,0:T(8,128)S(1)} %shard_map.117.merged, bf16[400,256]{1,0:T(8,128)(2,1)S(1)} %get-tuple-element.115.src_r, ...), custom_call_target="tpu_custom_call" | custom-call | flops 1000 | bytes 1000 | tf_op jit(solution)/shard_map/pallas_call | solution.py:19
  (93 shorter events, 8.2 us)
Async XLA Ops:
  0.6 20.8 %copy-start = (bf16[1345,800]{0,1:T(8,128)(2,1)S(1)}, bf16[1345,800]{0,1:T(8,128)(2,1)}, u32[]{:S(2)}) copy-start(bf16[1345,800]{0,1:T(8,128)(2,1)} %param.11) | copy-start | bytes 6456004
  0.6 20.8 %copy-start.5 = (s32[2,512]{1,0:T(2,128)S(1)}, s32[2,512]{1,0:T(2,128)}, u32[]{:S(2)}) copy-start(s32[2,512]{1,0:T(2,128)} %rel_ids.3) | copy-start | bytes 12292
  0.7 20.8 %copy-start.4 = (s32[2,1000]{1,0:T(2,128)S(1)}, s32[2,1000]{1,0:T(2,128)}, u32[]{:S(2)}) copy-start(s32[2,1000]{1,0:T(2,128)} %neg_ids.3) | copy-start | bytes 24004
  1.9 21.0 %copy-start.1 = (bf16[256,800]{0,1:T(8,128)(2,1)S(1)}, bf16[256,800]{0,1:T(8,128)(2,1)}, u32[]{:S(2)}) copy-start(bf16[256,800]{0,1:T(8,128)(2,1)} %param.9) | copy-start | bytes 1228804
  1.9 21.0 %copy-start.2 = (s32[2,512,1]{1,2,0:T(1,128)S(1)}, s32[2,512,1]{1,2,0:T(1,128)}, u32[]{:S(2)}) copy-start(s32[2,512,1]{1,2,0:T(1,128)} %param.14) | copy-start | bytes 12292
  1.9 21.0 %copy-start.3 = (s32[2,512]{1,0:T(2,128)S(1)}, s32[2,512]{1,0:T(2,128)}, u32[]{:S(2)}) copy-start(s32[2,512]{1,0:T(2,128)} %dest_rows.11) | copy-start | bytes 12292
  1.9 1.8 %collective-permute-start = (bf16[400,256]{1,0:T(8,128)(2,1)S(1)}, bf16[400,256]{1,0:T(8,128)(2,1)S(1)}, u32[]{:S(2)}, u32[]{:S(2)}) collective-permute-start(bf16[400,256]{1,0:T(8,128)(2,1)S(1)} %get-tuple-element.56), channel_id=1, source_target_pairs={{0,1},{1,0},{2,3},{3,2},{4,5},{5,4},{6,7},{7,6},{8,9},{9,8},{10,11... | collective-permute-start | bytes 614408 | tf_op jit(solution)/shard_map/ppermute | solution.py:163
  2.4 0.7 copy-start.8
  3.8 8.4 %collective-permute-start.1 = (bf16[400,256]{1,0:T(8,128)(2,1)S(1)}, bf16[400,256]{1,0:T(8,128)(2,1)S(1)}, u32[]{:S(2)}, u32[]{:S(2)}) collective-permute-start(bf16[400,256]{1,0:T(8,128)(2,1)S(1)} %broadcast_select_fusion.2), channel_id=1, source_target_pairs={{0,2},{1,3},{2,0},{3,1},{4,6},{5,7},{6,4},{7,5},{8,10},{9,11},{10,... | collective-permute-start | bytes 614408 | tf_op jit(solution)/shard_map/ppermute | solution.py:163
  6.6 11.6 %collective-permute-start.3 = (bf16[800,256]{1,0:T(8,128)(2,1)}, bf16[800,256]{1,0:T(8,128)(2,1)S(1)}, u32[]{:S(2)}, u32[]{:S(2)}) collective-permute-start(bf16[800,256]{1,0:T(8,128)(2,1)} %bitcast.9), channel_id=1, source_target_pairs={{0,8},{8,0},{16,24},{24,16},{1,9},{9,1},{17,25},{25,17},{2,10},{10... | collective-permute-start | bytes 1228808 | tf_op jit(solution)/shard_map/ppermute | solution.py:163
  8.1 11.8 %collective-permute-start.4 = (bf16[800,256]{1,0:T(8,128)(2,1)}, bf16[800,256]{1,0:T(8,128)(2,1)S(1)}, u32[]{:S(2)}, u32[]{:S(2)}) collective-permute-start(bf16[800,256]{1,0:T(8,128)(2,1)} %bitcast.10), channel_id=1, source_target_pairs={{0,16},{8,24},{16,0},{24,8},{1,17},{9,25},{17,1},{25,9},{2,18},{10... | collective-permute-start | bytes 1228808 | tf_op jit(solution)/shard_map/ppermute | solution.py:163
  12.2 12.1 %collective-permute-start.2 = (bf16[400,256]{1,0:T(8,128)(2,1)S(1)}, bf16[400,256]{1,0:T(8,128)(2,1)S(1)}, u32[]{:S(2)}, u32[]{:S(2)}) collective-permute-start(bf16[400,256]{1,0:T(8,128)(2,1)S(1)} %broadcast_select_fusion.3), channel_id=1, source_target_pairs={{0,4},{1,5},{2,6},{3,7},{4,0},{5,1},{6,2},{7,3},{8,12},{9,13},{10,... | collective-permute-start | bytes 614408 | tf_op jit(solution)/shard_map/ppermute | solution.py:163
  18.2 7.2 %collective-permute-start.6 = (bf16[480,256]{1,0:T(8,128)(2,1)S(1)}, bf16[480,256]{1,0:T(8,128)(2,1)S(1)}, u32[]{:S(2)}, u32[]{:S(2)}) collective-permute-start(bf16[480,256]{1,0:T(8,128)(2,1)S(1)} %slice.34), channel_id=1, source_target_pairs={{0,16},{8,24},{16,0},{24,8},{1,17},{9,25},{17,1},{25,9},{2,18},{10... | collective-permute-start | bytes 737288 | tf_op jit(solution)/shard_map/ppermute | solution.py:163
  19.9 5.4 %collective-permute-start.7 = (bf16[320,256]{1,0:T(8,128)(2,1)S(1)}, bf16[320,256]{1,0:T(8,128)(2,1)S(1)}, u32[]{:S(2)}, u32[]{:S(2)}) collective-permute-start(bf16[320,256]{1,0:T(8,128)(2,1)S(1)} %slice.35), channel_id=1, source_target_pairs={{0,8},{8,0},{16,24},{24,16},{1,9},{9,1},{17,25},{25,17},{2,10},{10... | collective-permute-start | bytes 491528 | tf_op jit(solution)/shard_map/ppermute | solution.py:163
  24.3 1.6 %copy-start.6 = (s32[2,512]{1,0:T(2,128)S(1)}, s32[2,512]{1,0:T(2,128)}, u32[]{:S(2)}) copy-start(s32[2,512]{1,0:T(2,128)} %src.3) | copy-start | bytes 12292
  24.3 1.5 %collective-permute-start.5 = (bf16[400,256]{1,0:T(8,128)(2,1)S(1)}, bf16[400,256]{1,0:T(8,128)(2,1)S(1)}, u32[]{:S(2)}, u32[]{:S(2)}) collective-permute-start(bf16[400,256]{1,0:T(8,128)(2,1)S(1)} %broadcast_select_fusion.4), channel_id=1, source_target_pairs={{0,1},{1,0},{2,3},{3,2},{4,5},{5,4},{6,7},{7,6},{8,9},{9,8},{10,11... | collective-permute-start | bytes 614408 | tf_op jit(solution)/shard_map/ppermute | solution.py:163
  28.1 1.5 %collective-permute-start.8 = (bf16[400,256]{1,0:T(8,128)(2,1)S(1)}, bf16[400,256]{1,0:T(8,128)(2,1)S(1)}, u32[]{:S(2)}, u32[]{:S(2)}) collective-permute-start(bf16[400,256]{1,0:T(8,128)(2,1)S(1)} %broadcast_select_fusion.9), channel_id=1, source_target_pairs={{0,1},{1,0},{2,3},{3,2},{4,5},{5,4},{6,7},{7,6},{8,9},{9,8},{10,11... | collective-permute-start | bytes 614408 | tf_op jit(solution)/shard_map/ppermute | solution.py:163
  29.8 7.4 %collective-permute-start.9 = (bf16[400,256]{1,0:T(8,128)(2,1)S(1)}, bf16[400,256]{1,0:T(8,128)(2,1)S(1)}, u32[]{:S(2)}, u32[]{:S(2)}) collective-permute-start(bf16[400,256]{1,0:T(8,128)(2,1)S(1)} %add_convert_fusion.9), channel_id=1, source_target_pairs={{0,2},{1,3},{2,0},{3,1},{4,6},{5,7},{6,4},{7,5},{8,10},{9,11},{10,... | collective-permute-start | bytes 614408 | tf_op jit(solution)/shard_map/ppermute | solution.py:163
  30.5 9.4 %collective-permute-start.10 = (bf16[400,256]{1,0:T(8,128)(2,1)S(1)}, bf16[400,256]{1,0:T(8,128)(2,1)S(1)}, u32[]{:S(2)}, u32[]{:S(2)}) collective-permute-start(bf16[400,256]{1,0:T(8,128)(2,1)S(1)} %get-tuple-element.75), channel_id=1, source_target_pairs={{0,8},{8,0},{16,24},{24,16},{1,9},{9,1},{17,25},{25,17},{2,10},{10... | collective-permute-start | bytes 614408 | tf_op jit(solution)/shard_map/ppermute | solution.py:163
  32.1 9.5 %collective-permute-start.12 = (bf16[400,256]{1,0:T(8,128)(2,1)S(1)}, bf16[400,256]{1,0:T(8,128)(2,1)S(1)}, u32[]{:S(2)}, u32[]{:S(2)}) collective-permute-start(bf16[400,256]{1,0:T(8,128)(2,1)S(1)} %get-tuple-element.78), channel_id=1, source_target_pairs={{0,16},{8,24},{16,0},{24,8},{1,17},{9,25},{17,1},{25,9},{2,18},{10... | collective-permute-start | bytes 614408 | tf_op jit(solution)/shard_map/ppermute | solution.py:163
  33.6 15.7 %collective-permute-start.14 = (bf16[400,256]{1,0:T(8,128)(2,1)S(1)}, bf16[400,256]{1,0:T(8,128)(2,1)S(1)}, u32[]{:S(2)}, u32[]{:S(2)}) collective-permute-start(bf16[400,256]{1,0:T(8,128)(2,1)S(1)} %get-tuple-element.79), channel_id=1, source_target_pairs={{0,8},{8,0},{16,24},{24,16},{1,9},{9,1},{17,25},{25,17},{2,10},{10... | collective-permute-start | bytes 614408 | tf_op jit(solution)/shard_map/ppermute | solution.py:163
  34.1 15.2 %collective-permute-start.15 = (bf16[400,256]{1,0:T(8,128)(2,1)S(1)}, bf16[400,256]{1,0:T(8,128)(2,1)S(1)}, u32[]{:S(2)}, u32[]{:S(2)}) collective-permute-start(bf16[400,256]{1,0:T(8,128)(2,1)S(1)} %get-tuple-element.80), channel_id=1, source_target_pairs={{0,16},{8,24},{16,0},{24,8},{1,17},{9,25},{17,1},{25,9},{2,18},{10... | collective-permute-start | bytes 614408 | tf_op jit(solution)/shard_map/ppermute | solution.py:163
  37.3 11.9 %collective-permute-start.16 = (bf16[400,256]{1,0:T(8,128)(2,1)S(1)}, bf16[400,256]{1,0:T(8,128)(2,1)S(1)}, u32[]{:S(2)}, u32[]{:S(2)}) collective-permute-start(bf16[400,256]{1,0:T(8,128)(2,1)S(1)} %add_convert_fusion.8), channel_id=1, source_target_pairs={{0,4},{1,5},{2,6},{3,7},{4,0},{5,1},{6,2},{7,3},{8,12},{9,13},{10,... | collective-permute-start | bytes 614408 | tf_op jit(solution)/shard_map/ppermute | solution.py:163
  40.0 9.4 %collective-permute-start.11 = (bf16[400,256]{1,0:T(8,128)(2,1)S(1)}, bf16[400,256]{1,0:T(8,128)(2,1)S(1)}, u32[]{:S(2)}, u32[]{:S(2)}) collective-permute-start(bf16[400,256]{1,0:T(8,128)(2,1)S(1)} %add_convert_fusion.7), channel_id=1, source_target_pairs={{0,16},{8,24},{16,0},{24,8},{1,17},{9,25},{17,1},{25,9},{2,18},{10... | collective-permute-start | bytes 614408 | tf_op jit(solution)/shard_map/ppermute | solution.py:163
  41.6 7.8 %collective-permute-start.13 = (bf16[400,256]{1,0:T(8,128)(2,1)S(1)}, bf16[400,256]{1,0:T(8,128)(2,1)S(1)}, u32[]{:S(2)}, u32[]{:S(2)}) collective-permute-start(bf16[400,256]{1,0:T(8,128)(2,1)S(1)} %add_convert_fusion.6), channel_id=1, source_target_pairs={{0,8},{8,0},{16,24},{24,16},{1,9},{9,1},{17,25},{25,17},{2,10},{10... | collective-permute-start | bytes 614408 | tf_op jit(solution)/shard_map/ppermute | solution.py:163
  49.2 1.6 %copy-start.7 = (f32[256]{0:T(256)S(1)}, f32[256]{0:T(256)}, u32[]{:S(2)}) copy-start(f32[256]{0:T(256)} %param.10) | copy-start | bytes 3076
  49.2 1.5 %collective-permute-start.17 = (bf16[400,256]{1,0:T(8,128)(2,1)S(1)}, bf16[400,256]{1,0:T(8,128)(2,1)S(1)}, u32[]{:S(2)}, u32[]{:S(2)}) collective-permute-start(bf16[400,256]{1,0:T(8,128)(2,1)S(1)} %add_convert_fusion.5), channel_id=1, source_target_pairs={{0,1},{1,0},{2,3},{3,2},{4,5},{5,4},{6,7},{7,6},{8,9},{9,8},{10,11... | collective-permute-start | bytes 614408 | tf_op jit(solution)/shard_map/ppermute | solution.py:163
  51.1 1.5 %collective-permute-start.18 = (bf16[400,256]{1,0:T(8,128)(2,1)S(1)}, bf16[400,256]{1,0:T(8,128)(2,1)S(1)}, u32[]{:S(2)}, u32[]{:S(2)}) collective-permute-start(bf16[400,256]{1,0:T(8,128)(2,1)S(1)} %broadcast_select_fusion.8), channel_id=1, source_target_pairs={{0,1},{1,0},{2,3},{3,2},{4,5},{5,4},{6,7},{7,6},{8,9},{9,8},{10,11... | collective-permute-start | bytes 614408 | tf_op jit(solution)/shard_map/ppermute | solution.py:163
  52.7 7.2 %collective-permute-start.19 = (bf16[400,256]{1,0:T(8,128)(2,1)S(1)}, bf16[400,256]{1,0:T(8,128)(2,1)S(1)}, u32[]{:S(2)}, u32[]{:S(2)}) collective-permute-start(bf16[400,256]{1,0:T(8,128)(2,1)S(1)} %select_select_fusion.2), channel_id=1, source_target_pairs={{0,2},{1,3},{2,0},{3,1},{4,6},{5,7},{6,4},{7,5},{8,10},{9,11},{10,... | collective-permute-start | bytes 614408 | tf_op jit(solution)/shard_map/ppermute | solution.py:163
  53.4 11.2 %collective-permute-start.21 = (bf16[800,256]{1,0:T(8,128)(2,1)S(1)}, bf16[800,256]{1,0:T(8,128)(2,1)S(1)}, u32[]{:S(2)}, u32[]{:S(2)}) collective-permute-start(bf16[800,256]{1,0:T(8,128)(2,1)S(1)} %get-tuple-element.86.table), channel_id=1, source_target_pairs={{0,8},{8,0},{16,24},{24,16},{1,9},{9,1},{17,25},{25,17},{2,10},{10... | collective-permute-start | bytes 1228808 | tf_op jit(solution)/shard_map/ppermute | solution.py:163
  54.9 11.4 %collective-permute-start.22 = (bf16[800,256]{1,0:T(8,128)(2,1)S(1)}, bf16[800,256]{1,0:T(8,128)(2,1)S(1)}, u32[]{:S(2)}, u32[]{:S(2)}) collective-permute-start(bf16[800,256]{1,0:T(8,128)(2,1)S(1)} %get-tuple-element.86.table), channel_id=1, source_target_pairs={{0,16},{8,24},{16,0},{24,8},{1,17},{9,25},{17,1},{25,9},{2,18},{10... | collective-permute-start | bytes 1228808 | tf_op jit(solution)/shard_map/ppermute | solution.py:163
  59.9 11.6 %collective-permute-start.20 = (bf16[400,256]{1,0:T(8,128)(2,1)S(1)}, bf16[400,256]{1,0:T(8,128)(2,1)S(1)}, u32[]{:S(2)}, u32[]{:S(2)}) collective-permute-start(bf16[400,256]{1,0:T(8,128)(2,1)S(1)} %broadcast_select_fusion), channel_id=1, source_target_pairs={{0,4},{1,5},{2,6},{3,7},{4,0},{5,1},{6,2},{7,3},{8,12},{9,13},{10,... | collective-permute-start | bytes 614408 | tf_op jit(solution)/shard_map/ppermute | solution.py:163
  64.6 7.1 %collective-permute-start.24 = (bf16[480,256]{1,0:T(8,128)(2,1)S(1)}, bf16[480,256]{1,0:T(8,128)(2,1)S(1)}, u32[]{:S(2)}, u32[]{:S(2)}) collective-permute-start(bf16[480,256]{1,0:T(8,128)(2,1)S(1)} %slice.36), channel_id=1, source_target_pairs={{0,16},{8,24},{16,0},{24,8},{1,17},{9,25},{17,1},{25,9},{2,18},{10... | collective-permute-start | bytes 737288 | tf_op jit(solution)/shard_map/ppermute | solution.py:163
  66.2 5.4 %collective-permute-start.25 = (bf16[320,256]{1,0:T(8,128)(2,1)S(1)}, bf16[320,256]{1,0:T(8,128)(2,1)S(1)}, u32[]{:S(2)}, u32[]{:S(2)}) collective-permute-start(bf16[320,256]{1,0:T(8,128)(2,1)S(1)} %slice.37), channel_id=1, source_target_pairs={{0,8},{8,0},{16,24},{24,16},{1,9},{9,1},{17,25},{25,17},{2,10},{10... | collective-permute-start | bytes 491528 | tf_op jit(solution)/shard_map/ppermute | solution.py:163
  71.6 1.5 %collective-permute-start.23 = (bf16[400,256]{1,0:T(8,128)(2,1)S(1)}, bf16[400,256]{1,0:T(8,128)(2,1)S(1)}, u32[]{:S(2)}, u32[]{:S(2)}) collective-permute-start(bf16[400,256]{1,0:T(8,128)(2,1)S(1)} %broadcast_select_fusion.1), channel_id=1, source_target_pairs={{0,1},{1,0},{2,3},{3,2},{4,5},{5,4},{6,7},{7,6},{8,9},{9,8},{10,11... | collective-permute-start | bytes 614408 | tf_op jit(solution)/shard_map/ppermute | solution.py:163
  75.6 1.6 %collective-permute-start.26 = (bf16[400,256]{1,0:T(8,128)(2,1)S(1)}, bf16[400,256]{1,0:T(8,128)(2,1)S(1)}, u32[]{:S(2)}, u32[]{:S(2)}) collective-permute-start(bf16[400,256]{1,0:T(8,128)(2,1)S(1)} %broadcast_select_fusion.5), channel_id=1, source_target_pairs={{0,1},{1,0},{2,3},{3,2},{4,5},{5,4},{6,7},{7,6},{8,9},{9,8},{10,11... | collective-permute-start | bytes 614408 | tf_op jit(solution)/shard_map/ppermute | solution.py:163
  77.2 7.4 %collective-permute-start.27 = (bf16[400,256]{1,0:T(8,128)(2,1)S(1)}, bf16[400,256]{1,0:T(8,128)(2,1)S(1)}, u32[]{:S(2)}, u32[]{:S(2)}) collective-permute-start(bf16[400,256]{1,0:T(8,128)(2,1)S(1)} %add_convert_fusion.4), channel_id=1, source_target_pairs={{0,2},{1,3},{2,0},{3,1},{4,6},{5,7},{6,4},{7,5},{8,10},{9,11},{10,... | collective-permute-start | bytes 614408 | tf_op jit(solution)/shard_map/ppermute | solution.py:163
  77.9 9.2 %collective-permute-start.28 = (bf16[400,256]{1,0:T(8,128)(2,1)S(1)}, bf16[400,256]{1,0:T(8,128)(2,1)S(1)}, u32[]{:S(2)}, u32[]{:S(2)}) collective-permute-start(bf16[400,256]{1,0:T(8,128)(2,1)S(1)} %get-tuple-element.101), channel_id=1, source_target_pairs={{0,8},{8,0},{16,24},{24,16},{1,9},{9,1},{17,25},{25,17},{2,10},{10... | collective-permute-start | bytes 614408 | tf_op jit(solution)/shard_map/ppermute | solution.py:163
  79.5 9.2 %collective-permute-start.30 = (bf16[400,256]{1,0:T(8,128)(2,1)S(1)}, bf16[400,256]{1,0:T(8,128)(2,1)S(1)}, u32[]{:S(2)}, u32[]{:S(2)}) collective-permute-start(bf16[400,256]{1,0:T(8,128)(2,1)S(1)} %get-tuple-element.104), channel_id=1, source_target_pairs={{0,16},{8,24},{16,0},{24,8},{1,17},{9,25},{17,1},{25,9},{2,18},{10... | collective-permute-start | bytes 614408 | tf_op jit(solution)/shard_map/ppermute | solution.py:163
  81.0 15.7 %collective-permute-start.32 = (bf16[400,256]{1,0:T(8,128)(2,1)S(1)}, bf16[400,256]{1,0:T(8,128)(2,1)S(1)}, u32[]{:S(2)}, u32[]{:S(2)}) collective-permute-start(bf16[400,256]{1,0:T(8,128)(2,1)S(1)} %get-tuple-element.105), channel_id=1, source_target_pairs={{0,8},{8,0},{16,24},{24,16},{1,9},{9,1},{17,25},{25,17},{2,10},{10... | collective-permute-start | bytes 614408 | tf_op jit(solution)/shard_map/ppermute | solution.py:163
  81.5 15.2 %collective-permute-start.33 = (bf16[400,256]{1,0:T(8,128)(2,1)S(1)}, bf16[400,256]{1,0:T(8,128)(2,1)S(1)}, u32[]{:S(2)}, u32[]{:S(2)}) collective-permute-start(bf16[400,256]{1,0:T(8,128)(2,1)S(1)} %get-tuple-element.106), channel_id=1, source_target_pairs={{0,16},{8,24},{16,0},{24,8},{1,17},{9,25},{17,1},{25,9},{2,18},{10... | collective-permute-start | bytes 614408 | tf_op jit(solution)/shard_map/ppermute | solution.py:163
  84.7 11.9 %collective-permute-start.34 = (bf16[400,256]{1,0:T(8,128)(2,1)S(1)}, bf16[400,256]{1,0:T(8,128)(2,1)S(1)}, u32[]{:S(2)}, u32[]{:S(2)}) collective-permute-start(bf16[400,256]{1,0:T(8,128)(2,1)S(1)} %add_convert_fusion.3), channel_id=1, source_target_pairs={{0,4},{1,5},{2,6},{3,7},{4,0},{5,1},{6,2},{7,3},{8,12},{9,13},{10,... | collective-permute-start | bytes 614408 | tf_op jit(solution)/shard_map/ppermute | solution.py:163
  87.2 9.6 %collective-permute-start.29 = (bf16[400,256]{1,0:T(8,128)(2,1)S(1)}, bf16[400,256]{1,0:T(8,128)(2,1)S(1)}, u32[]{:S(2)}, u32[]{:S(2)}) collective-permute-start(bf16[400,256]{1,0:T(8,128)(2,1)S(1)} %add_convert_fusion.2), channel_id=1, source_target_pairs={{0,16},{8,24},{16,0},{24,8},{1,17},{9,25},{17,1},{25,9},{2,18},{10... | collective-permute-start | bytes 614408 | tf_op jit(solution)/shard_map/ppermute | solution.py:163
  88.7 8.0 %collective-permute-start.31 = (bf16[400,256]{1,0:T(8,128)(2,1)S(1)}, bf16[400,256]{1,0:T(8,128)(2,1)S(1)}, u32[]{:S(2)}, u32[]{:S(2)}) collective-permute-start(bf16[400,256]{1,0:T(8,128)(2,1)S(1)} %add_convert_fusion.1), channel_id=1, source_target_pairs={{0,8},{8,0},{16,24},{24,16},{1,9},{9,1},{17,25},{25,17},{2,10},{10... | collective-permute-start | bytes 614408 | tf_op jit(solution)/shard_map/ppermute | solution.py:163
  96.6 1.5 %collective-permute-start.35 = (bf16[400,256]{1,0:T(8,128)(2,1)S(1)}, bf16[400,256]{1,0:T(8,128)(2,1)S(1)}, u32[]{:S(2)}, u32[]{:S(2)}) collective-permute-start(bf16[400,256]{1,0:T(8,128)(2,1)S(1)} %add_convert_fusion), channel_id=1, source_target_pairs={{0,1},{1,0},{2,3},{3,2},{4,5},{5,4},{6,7},{7,6},{8,9},{9,8},{10,11... | collective-permute-start | bytes 614408 | tf_op jit(solution)/shard_map/ppermute | solution.py:163

commit v4 on v3

--- a/solution.py
+++ b/solution.py
@@ -276,7 +276,7 @@
             dest_groups, dest_rows, query, coef_pos, coef_neg,
         )
         early, rest = spread_grads(sends)
-        part = add(jnp.where(first, out_r, out_i), after(give, base_grad))
+        part = add(jnp.where(first, out_r, out_i), give)
         for turn, bit in enumerate(bits):
             part = add(part, shift(part, "member", bit))
             if turn == 0:

time: 99.4 us -> 98.4 us (0.990)
  transfers between devices with their start and end apart: 36 -> 36, of which waited for: 17 -> 21; matrix products, arithmetic and copies ran while one was open for 1% -> 1% of each run, Pallas kernels for 9% -> 9%
where the time goes in v4:
time: 98.4 us; the launch traced here: 98.3 us
  starting transfers between devices  42.9 us (44%)
  waiting for transfers between devices  36.3 us (37%)
  Pallas kernels  14.7 us (15%)
  other arithmetic  2.42 us (2%)
  between operations  1.08 us (1%)
    ppermute x36, starting transfers between devices, shift(): return lax.ppermute(value, axis, [(i, i ^ bit) for i in range(size)])  42.9 us
    ppermute x36, waiting for transfers between devices, shift(): return lax.ppermute(value, axis, [(i, i ^ bit) for i in range(size)])  36.3 us
    pallas_call x15, Pallas kernels, call(): pl.pallas_call(body, out_shape=outs, in_specs=[SMEM if i in smem else VME...  14.7 us
  transfers between devices with their start and end apart: 36, of which 21 were waited for; matrix products, arithmetic and copies ran while one was open for 1% of the time, Pallas kernels for 9%

profile of v4, /device:TPU:0, one launch (start us, length us, event | category | flops | bytes accessed | tf_op | source)
XLA Modules:
  0.0 98.3 jit_solution(7694085916664080067)
XLA Ops:
  0.7 1.2 %broadcast_select_fusion.12 = (bf16[400,256]{1,0:T(8,128)(2,1)S(1)}, bf16[400,256]{1,0:T(8,128)(2,1)S(1)}) fusion(pred[]{:T(512)S(6)} %eq.5, bf16[800,256]{1,0:T(8,128)(2,1)} %bitcast.8), kind=kLoop, calls=%fused_computation.27 | loop fusion | flops 204800 | bytes 819201 | tf_op jit(solution)/shard_map/jit(_where)/select_n | solution.py:241
  2.4 0.7 copy-done.8
  3.8 2.8 %collective-permute-start.1 = (bf16[400,256]{1,0:T(8,128)(2,1)S(1)}, bf16[400,256]{1,0:T(8,128)(2,1)S(1)}, u32[]{:S(2)}, u32[]{:S(2)}) collective-permute-start(bf16[400,256]{1,0:T(8,128)(2,1)S(1)} %broadcast_select_fusion.2), channel_id=1, source_target_pairs={{0,2},{1,3},{2,0},{3,1},{4,6},{5,7},{6,4},{7,5},{8,10},{9,11},{10,... | collective-permute-start | bytes 614408 | tf_op jit(solution)/shard_map/ppermute | solution.py:163
  6.6 1.5 %collective-permute-start.3 = (bf16[800,256]{1,0:T(8,128)(2,1)}, bf16[800,256]{1,0:T(8,128)(2,1)S(1)}, u32[]{:S(2)}, u32[]{:S(2)}) collective-permute-start(bf16[800,256]{1,0:T(8,128)(2,1)} %bitcast.9), channel_id=1, source_target_pairs={{0,8},{8,0},{16,24},{24,16},{1,9},{9,1},{17,25},{25,17},{2,10},{10... | collective-permute-start | bytes 1228808 | tf_op jit(solution)/shard_map/ppermute | solution.py:163
  8.1 1.5 %collective-permute-start.4 = (bf16[800,256]{1,0:T(8,128)(2,1)}, bf16[800,256]{1,0:T(8,128)(2,1)S(1)}, u32[]{:S(2)}, u32[]{:S(2)}) collective-permute-start(bf16[800,256]{1,0:T(8,128)(2,1)} %bitcast.10), channel_id=1, source_target_pairs={{0,16},{8,24},{16,0},{24,8},{1,17},{9,25},{17,1},{25,9},{2,18},{10... | collective-permute-start | bytes 1228808 | tf_op jit(solution)/shard_map/ppermute | solution.py:163
  9.6 2.5 %collective-permute-done.1 = bf16[400,256]{1,0:T(8,128)(2,1)S(1)} collective-permute-done((bf16[400,256]{1,0:T(8,128)(2,1)S(1)}, bf16[400,256]{1,0:T(8,128)(2,1)S(1)}, u32[]{:S(2)}, u32[]{:S(2)}) %collective-permute-start.1) | collective-permute-done | bytes 204832 | tf_op jit(solution)/shard_map/ppermute | solution.py:163
  12.2 2.8 %collective-permute-start.2 = (bf16[400,256]{1,0:T(8,128)(2,1)S(1)}, bf16[400,256]{1,0:T(8,128)(2,1)S(1)}, u32[]{:S(2)}, u32[]{:S(2)}) collective-permute-start(bf16[400,256]{1,0:T(8,128)(2,1)S(1)} %broadcast_select_fusion.3), channel_id=1, source_target_pairs={{0,4},{1,5},{2,6},{3,7},{4,0},{5,1},{6,2},{7,3},{8,12},{9,13},{10,... | collective-permute-start | bytes 614408 | tf_op jit(solution)/shard_map/ppermute | solution.py:163
  15.0 3.2 %collective-permute-done.3.refs_0_ = bf16[800,256]{1,0:T(8,128)(2,1)S(1)} collective-permute-done((bf16[800,256]{1,0:T(8,128)(2,1)}, bf16[800,256]{1,0:T(8,128)(2,1)S(1)}, u32[]{:S(2)}, u32[]{:S(2)}) %collective-permute-start.3) | collective-permute-done | bytes 409632 | tf_op jit(solution)/shard_map/ppermute | solution.py:163
  18.2 1.6 %collective-permute-start.6 = (bf16[480,256]{1,0:T(8,128)(2,1)S(1)}, bf16[480,256]{1,0:T(8,128)(2,1)S(1)}, u32[]{:S(2)}, u32[]{:S(2)}) collective-permute-start(bf16[480,256]{1,0:T(8,128)(2,1)S(1)} %slice.34), channel_id=1, source_target_pairs={{0,16},{8,24},{16,0},{24,8},{1,17},{9,25},{17,1},{25,9},{2,18},{10... | collective-permute-start | bytes 737288 | tf_op jit(solution)/shard_map/ppermute | solution.py:163
  19.9 1.6 %collective-permute-start.7 = (bf16[320,256]{1,0:T(8,128)(2,1)S(1)}, bf16[320,256]{1,0:T(8,128)(2,1)S(1)}, u32[]{:S(2)}, u32[]{:S(2)}) collective-permute-start(bf16[320,256]{1,0:T(8,128)(2,1)S(1)} %slice.35), channel_id=1, source_target_pairs={{0,8},{8,0},{16,24},{24,16},{1,9},{9,1},{17,25},{25,17},{2,10},{10... | collective-permute-start | bytes 491528 | tf_op jit(solution)/shard_map/ppermute | solution.py:163
  21.4 1.4 %shard_map.106 = (bf16[800,512]{1,0:T(8,128)(2,1)S(1)}, f32[256,1]{1,0:T(8,128)S(1)}) custom-call(s32[2,512]{1,0:T(2,128)S(1)} %copy-done.5, s32[2,1000]{1,0:T(2,128)S(1)} %copy-done.4, bf16[800,1345]{1,0:T(8,128)(2,1)S(1)} %bitcast.6), custom_call_target="tpu_custom_call" | custom-call | flops 1000 | bytes 1000 | tf_op jit(solution)/shard_map/pallas_call | solution.py:19
  22.9 0.8 shard_map.105.near
  24.5 0.7 collective-permute-done.7.second
  26.0 2.2 %shard_map.108 = (bf16[800,512]{1,0:T(8,128)(2,1)S(1)}, bf16[400,256]{1,0:T(8,128)(2,1)S(1)}, bf16[400,256]{1,0:T(8,128)(2,1)S(1)}, f32[1,512]{1,0:T(1,128)S(1)}, bf16[256,512]{1,0:T(8,128)(2,1)S(1)}) custom-call(s32[2,512]{1,0:T(2,128)S(1)} %copy-done.6, bf16[400,256]{1,0:T(8,128)(2,1)S(1)} %get-tuple-element.117.real, ...), custom_call_target="tpu_custom_call" | custom-call | flops 1000 | bytes 1000 | tf_op jit(solution)/shard_map/pallas_call | solution.py:19
  28.4 1.3 %collective-permute-done.8 = bf16[400,256]{1,0:T(8,128)(2,1)S(1)} collective-permute-done((bf16[400,256]{1,0:T(8,128)(2,1)S(1)}, bf16[400,256]{1,0:T(8,128)(2,1)S(1)}, u32[]{:S(2)}, u32[]{:S(2)}) %collective-permute-start.8) | collective-permute-done | bytes 204832 | tf_op jit(solution)/shard_map/ppermute | solution.py:163
  30.5 1.3 %shard_map.109 = (f32[800,256]{1,0:T(8,128)S(1)}, bf16[400,256]{1,0:T(8,128)(2,1)S(1)}, bf16[400,256]{1,0:T(8,128)(2,1)S(1)}, bf16[400,256]{1,0:T(8,128)(2,1)S(1...) custom-call(s32[2,1,512]{2,1,0:T(1,128)S(1)} %bitcast.16, ...), custom_call_target="tpu_custom_call" | custom-call | flops 1000 | bytes 1000 | tf_op jit(solution)/shard_map/pallas_call | solution.py:19
  31.8 1.5 %collective-permute-start.10 = (bf16[400,256]{1,0:T(8,128)(2,1)S(1)}, bf16[400,256]{1,0:T(8,128)(2,1)S(1)}, u32[]{:S(2)}, u32[]{:S(2)}) collective-permute-start(bf16[400,256]{1,0:T(8,128)(2,1)S(1)} %get-tuple-element.72), channel_id=1, source_target_pairs={{0,8},{8,0},{16,24},{24,16},{1,9},{9,1},{17,25},{25,17},{2,10},{10... | collective-permute-start | bytes 614408 | tf_op jit(solution)/shard_map/ppermute | solution.py:163
  33.4 1.5 %collective-permute-start.12 = (bf16[400,256]{1,0:T(8,128)(2,1)S(1)}, bf16[400,256]{1,0:T(8,128)(2,1)S(1)}, u32[]{:S(2)}, u32[]{:S(2)}) collective-permute-start(bf16[400,256]{1,0:T(8,128)(2,1)S(1)} %get-tuple-element.75), channel_id=1, source_target_pairs={{0,16},{8,24},{16,0},{24,8},{1,17},{9,25},{17,1},{25,9},{2,18},{10... | collective-permute-start | bytes 614408 | tf_op jit(solution)/shard_map/ppermute | solution.py:163
  35.9 1.1 %collective-permute-done.9 = bf16[400,256]{1,0:T(8,128)(2,1)S(1)} collective-permute-done((bf16[400,256]{1,0:T(8,128)(2,1)S(1)}, bf16[400,256]{1,0:T(8,128)(2,1)S(1)}, u32[]{:S(2)}, u32[]{:S(2)}) %collective-permute-start.9) | collective-permute-done | bytes 204832 | tf_op jit(solution)/shard_map/ppermute | solution.py:163
  37.1 2.5 %collective-permute-start.16 = (bf16[400,256]{1,0:T(8,128)(2,1)S(1)}, bf16[400,256]{1,0:T(8,128)(2,1)S(1)}, u32[]{:S(2)}, u32[]{:S(2)}) collective-permute-start(bf16[400,256]{1,0:T(8,128)(2,1)S(1)} %add_convert_fusion.8), channel_id=1, source_target_pairs={{0,4},{1,5},{2,6},{3,7},{4,0},{5,1},{6,2},{7,3},{8,12},{9,13},{10,... | collective-permute-start | bytes 614408 | tf_op jit(solution)/shard_map/ppermute | solution.py:163
  39.9 1.6 %collective-permute-start.11 = (bf16[400,256]{1,0:T(8,128)(2,1)S(1)}, bf16[400,256]{1,0:T(8,128)(2,1)S(1)}, u32[]{:S(2)}, u32[]{:S(2)}) collective-permute-start(bf16[400,256]{1,0:T(8,128)(2,1)S(1)} %add_convert_fusion.7), channel_id=1, source_target_pairs={{0,16},{8,24},{16,0},{24,8},{1,17},{9,25},{17,1},{25,9},{2,18},{10... | collective-permute-start | bytes 614408 | tf_op jit(solution)/shard_map/ppermute | solution.py:163
  41.6 1.5 %collective-permute-start.13 = (bf16[400,256]{1,0:T(8,128)(2,1)S(1)}, bf16[400,256]{1,0:T(8,128)(2,1)S(1)}, u32[]{:S(2)}, u32[]{:S(2)}) collective-permute-start(bf16[400,256]{1,0:T(8,128)(2,1)S(1)} %add_convert_fusion.6), channel_id=1, source_target_pairs={{0,8},{8,0},{16,24},{24,16},{1,9},{9,1},{17,25},{25,17},{2,10},{10... | collective-permute-start | bytes 614408 | tf_op jit(solution)/shard_map/ppermute | solution.py:163
  43.1 1.4 %shard_map.111 = (bf16[800,512]{1,0:T(8,128)(2,1)S(1)}, f32[256,1]{1,0:T(8,128)S(1)}) custom-call(s32[2,512]{1,0:T(2,128)S(1)} %copy-done.5, s32[2,1000]{1,0:T(2,128)S(1)} %copy-done.4, bf16[800,1345]{1,0:T(8,128)(2,1)S(1)} %bitcast.7), custom_call_target="tpu_custom_call" | custom-call | flops 1000 | bytes 1000 | tf_op jit(solution)/shard_map/pallas_call | solution.py:19
  44.5 4.2 %collective-permute-done.16 = bf16[400,256]{1,0:T(8,128)(2,1)S(1)} collective-permute-done((bf16[400,256]{1,0:T(8,128)(2,1)S(1)}, bf16[400,256]{1,0:T(8,128)(2,1)S(1)}, u32[]{:S(2)}, u32[]{:S(2)}) %collective-permute-start.16) | collective-permute-done | bytes 204832 | tf_op jit(solution)/shard_map/ppermute | solution.py:163
  49.1 1.3 %collective-permute-done.17 = bf16[400,256]{1,0:T(8,128)(2,1)S(1)} collective-permute-done((bf16[400,256]{1,0:T(8,128)(2,1)S(1)}, bf16[400,256]{1,0:T(8,128)(2,1)S(1)}, u32[]{:S(2)}, u32[]{:S(2)}) %collective-permute-start.17) | collective-permute-done | bytes 204832 | tf_op jit(solution)/shard_map/ppermute | solution.py:163
  50.9 1.3 %collective-permute-done.18 = bf16[400,256]{1,0:T(8,128)(2,1)S(1)} collective-permute-done((bf16[400,256]{1,0:T(8,128)(2,1)S(1)}, bf16[400,256]{1,0:T(8,128)(2,1)S(1)}, u32[]{:S(2)}, u32[]{:S(2)}) %collective-permute-start.18) | collective-permute-done | bytes 204832 | tf_op jit(solution)/shard_map/ppermute | solution.py:163
  52.8 1.5 %collective-permute-start.21 = (bf16[800,256]{1,0:T(8,128)(2,1)S(1)}, bf16[800,256]{1,0:T(8,128)(2,1)S(1)}, u32[]{:S(2)}, u32[]{:S(2)}) collective-permute-start(bf16[800,256]{1,0:T(8,128)(2,1)S(1)} %get-tuple-element.83.table), channel_id=1, source_target_pairs={{0,8},{8,0},{16,24},{24,16},{1,9},{9,1},{17,25},{25,17},{2,10},{10... | collective-permute-start | bytes 1228808 | tf_op jit(solution)/shard_map/ppermute | solution.py:163
  54.4 1.6 %collective-permute-start.22 = (bf16[800,256]{1,0:T(8,128)(2,1)S(1)}, bf16[800,256]{1,0:T(8,128)(2,1)S(1)}, u32[]{:S(2)}, u32[]{:S(2)}) collective-permute-start(bf16[800,256]{1,0:T(8,128)(2,1)S(1)} %get-tuple-element.83.table), channel_id=1, source_target_pairs={{0,16},{8,24},{16,0},{24,8},{1,17},{9,25},{17,1},{25,9},{2,18},{10... | collective-permute-start | bytes 1228808 | tf_op jit(solution)/shard_map/ppermute | solution.py:163
  55.9 3.5 %collective-permute-done.19 = bf16[400,256]{1,0:T(8,128)(2,1)S(1)} collective-permute-done((bf16[400,256]{1,0:T(8,128)(2,1)S(1)}, bf16[400,256]{1,0:T(8,128)(2,1)S(1)}, u32[]{:S(2)}, u32[]{:S(2)}) %collective-permute-start.19) | collective-permute-done | bytes 204832 | tf_op jit(solution)/shard_map/ppermute | solution.py:163
  59.5 2.4 %collective-permute-start.20 = (bf16[400,256]{1,0:T(8,128)(2,1)S(1)}, bf16[400,256]{1,0:T(8,128)(2,1)S(1)}, u32[]{:S(2)}, u32[]{:S(2)}) collective-permute-start(bf16[400,256]{1,0:T(8,128)(2,1)S(1)} %broadcast_select_fusion), channel_id=1, source_target_pairs={{0,4},{1,5},{2,6},{3,7},{4,0},{5,1},{6,2},{7,3},{8,12},{9,13},{10,... | collective-permute-start | bytes 614408 | tf_op jit(solution)/shard_map/ppermute | solution.py:163
  61.9 2.1 %collective-permute-done.21.refs_0_ = bf16[800,256]{1,0:T(8,128)(2,1)S(1)} collective-permute-done((bf16[800,256]{1,0:T(8,128)(2,1)S(1)}, bf16[800,256]{1,0:T(8,128)(2,1)S(1)}, u32[]{:S(2)}, u32[]{:S(2)}) %collective-permute-start.21) | collective-permute-done | bytes 409632 | tf_op jit(solution)/shard_map/ppermute | solution.py:163
  64.1 1.6 %collective-permute-start.24 = (bf16[480,256]{1,0:T(8,128)(2,1)S(1)}, bf16[480,256]{1,0:T(8,128)(2,1)S(1)}, u32[]{:S(2)}, u32[]{:S(2)}) collective-permute-start(bf16[480,256]{1,0:T(8,128)(2,1)S(1)} %slice.36), channel_id=1, source_target_pairs={{0,16},{8,24},{16,0},{24,8},{1,17},{9,25},{17,1},{25,9},{2,18},{10... | collective-permute-start | bytes 737288 | tf_op jit(solution)/shard_map/ppermute | solution.py:163
  65.7 1.6 %collective-permute-start.25 = (bf16[320,256]{1,0:T(8,128)(2,1)S(1)}, bf16[320,256]{1,0:T(8,128)(2,1)S(1)}, u32[]{:S(2)}, u32[]{:S(2)}) collective-permute-start(bf16[320,256]{1,0:T(8,128)(2,1)S(1)} %slice.37), channel_id=1, source_target_pairs={{0,8},{8,0},{16,24},{24,16},{1,9},{9,1},{17,25},{25,17},{2,10},{10... | collective-permute-start | bytes 491528 | tf_op jit(solution)/shard_map/ppermute | solution.py:163
  67.3 0.8 shard_map.113.near
  68.1 3.0 %collective-permute-done.20 = bf16[400,256]{1,0:T(8,128)(2,1)S(1)} collective-permute-done((bf16[400,256]{1,0:T(8,128)(2,1)S(1)}, bf16[400,256]{1,0:T(8,128)(2,1)S(1)}, u32[]{:S(2)}, u32[]{:S(2)}) %collective-permute-start.20) | collective-permute-done | bytes 204832 | tf_op jit(solution)/shard_map/ppermute | solution.py:163
  71.7 1.0 %collective-permute-done.23 = bf16[400,256]{1,0:T(8,128)(2,1)S(1)} collective-permute-done((bf16[400,256]{1,0:T(8,128)(2,1)S(1)}, bf16[400,256]{1,0:T(8,128)(2,1)S(1)}, u32[]{:S(2)}, u32[]{:S(2)}) %collective-permute-start.23) | collective-permute-done | bytes 204832 | tf_op jit(solution)/shard_map/ppermute | solution.py:163
  72.7 2.4 %shard_map.115 = (bf16[800,512]{1,0:T(8,128)(2,1)S(1)}, bf16[400,256]{1,0:T(8,128)(2,1)S(1)}, bf16[400,256]{1,0:T(8,128)(2,1)S(1)}, f32[1,512]{1,0:T(1,128)S(1)}, bf16[256,512]{1,0:T(8,128)(2,1)S(1)}) custom-call(s32[2,512]{1,0:T(2,128)S(1)} %copy-done.6, bf16[400,256]{1,0:T(8,128)(2,1)S(1)} %get-tuple-element.115.real, ...), custom_call_target="tpu_custom_call" | custom-call | flops 1000 | bytes 1000 | tf_op jit(solution)/shard_map/pallas_call | solution.py:19
  75.3 1.3 %collective-permute-done.26 = bf16[400,256]{1,0:T(8,128)(2,1)S(1)} collective-permute-done((bf16[400,256]{1,0:T(8,128)(2,1)S(1)}, bf16[400,256]{1,0:T(8,128)(2,1)S(1)}, u32[]{:S(2)}, u32[]{:S(2)}) %collective-permute-start.26) | collective-permute-done | bytes 204832 | tf_op jit(solution)/shard_map/ppermute | solution.py:163
  77.3 1.3 %shard_map.116 = (f32[800,256]{1,0:T(8,128)S(1)}, bf16[400,256]{1,0:T(8,128)(2,1)S(1)}, bf16[400,256]{1,0:T(8,128)(2,1)S(1)}, bf16[400,256]{1,0:T(8,128)(2,1)S(1...) custom-call(s32[2,1,512]{2,1,0:T(1,128)S(1)} %bitcast.19, ...), custom_call_target="tpu_custom_call" | custom-call | flops 1000 | bytes 1000 | tf_op jit(solution)/shard_map/pallas_call | solution.py:19
  78.6 1.6 %collective-permute-start.28 = (bf16[400,256]{1,0:T(8,128)(2,1)S(1)}, bf16[400,256]{1,0:T(8,128)(2,1)S(1)}, u32[]{:S(2)}, u32[]{:S(2)}) collective-permute-start(bf16[400,256]{1,0:T(8,128)(2,1)S(1)} %get-tuple-element.97), channel_id=1, source_target_pairs={{0,8},{8,0},{16,24},{24,16},{1,9},{9,1},{17,25},{25,17},{2,10},{10... | collective-permute-start | bytes 614408 | tf_op jit(solution)/shard_map/ppermute | solution.py:163
  80.3 1.5 %collective-permute-start.30 = (bf16[400,256]{1,0:T(8,128)(2,1)S(1)}, bf16[400,256]{1,0:T(8,128)(2,1)S(1)}, u32[]{:S(2)}, u32[]{:S(2)}) collective-permute-start(bf16[400,256]{1,0:T(8,128)(2,1)S(1)} %get-tuple-element.100), channel_id=1, source_target_pairs={{0,16},{8,24},{16,0},{24,8},{1,17},{9,25},{17,1},{25,9},{2,18},{10... | collective-permute-start | bytes 614408 | tf_op jit(solution)/shard_map/ppermute | solution.py:163
  82.8 1.2 %collective-permute-done.27 = bf16[400,256]{1,0:T(8,128)(2,1)S(1)} collective-permute-done((bf16[400,256]{1,0:T(8,128)(2,1)S(1)}, bf16[400,256]{1,0:T(8,128)(2,1)S(1)}, u32[]{:S(2)}, u32[]{:S(2)}) %collective-permute-start.27) | collective-permute-done | bytes 204832 | tf_op jit(solution)/shard_map/ppermute | solution.py:163
  84.0 2.3 %collective-permute-start.34 = (bf16[400,256]{1,0:T(8,128)(2,1)S(1)}, bf16[400,256]{1,0:T(8,128)(2,1)S(1)}, u32[]{:S(2)}, u32[]{:S(2)}) collective-permute-start(bf16[400,256]{1,0:T(8,128)(2,1)S(1)} %add_convert_fusion.3), channel_id=1, source_target_pairs={{0,4},{1,5},{2,6},{3,7},{4,0},{5,1},{6,2},{7,3},{8,12},{9,13},{10,... | collective-permute-start | bytes 614408 | tf_op jit(solution)/shard_map/ppermute | solution.py:163
  86.7 1.6 %collective-permute-start.29 = (bf16[400,256]{1,0:T(8,128)(2,1)S(1)}, bf16[400,256]{1,0:T(8,128)(2,1)S(1)}, u32[]{:S(2)}, u32[]{:S(2)}) collective-permute-start(bf16[400,256]{1,0:T(8,128)(2,1)S(1)} %add_convert_fusion.2), channel_id=1, source_target_pairs={{0,16},{8,24},{16,0},{24,8},{1,17},{9,25},{17,1},{25,9},{2,18},{10... | collective-permute-start | bytes 614408 | tf_op jit(solution)/shard_map/ppermute | solution.py:163
  88.4 1.6 %collective-permute-start.31 = (bf16[400,256]{1,0:T(8,128)(2,1)S(1)}, bf16[400,256]{1,0:T(8,128)(2,1)S(1)}, u32[]{:S(2)}, u32[]{:S(2)}) collective-permute-start(bf16[400,256]{1,0:T(8,128)(2,1)S(1)} %add_convert_fusion.1), channel_id=1, source_target_pairs={{0,8},{8,0},{16,24},{24,16},{1,9},{9,1},{17,25},{25,17},{2,10},{10... | collective-permute-start | bytes 614408 | tf_op jit(solution)/shard_map/ppermute | solution.py:163
  90.0 5.6 %collective-permute-done.34 = bf16[400,256]{1,0:T(8,128)(2,1)S(1)} collective-permute-done((bf16[400,256]{1,0:T(8,128)(2,1)S(1)}, bf16[400,256]{1,0:T(8,128)(2,1)S(1)}, u32[]{:S(2)}, u32[]{:S(2)}) %collective-permute-start.34) | collective-permute-done | bytes 204832 | tf_op jit(solution)/shard_map/ppermute | solution.py:163
  95.9 1.3 %collective-permute-done.35 = bf16[400,256]{1,0:T(8,128)(2,1)S(1)} collective-permute-done((bf16[400,256]{1,0:T(8,128)(2,1)S(1)}, bf16[400,256]{1,0:T(8,128)(2,1)S(1)}, u32[]{:S(2)}, u32[]{:S(2)}) %collective-permute-start.35) | collective-permute-done | bytes 204832 | tf_op jit(solution)/shard_map/ppermute | solution.py:163
  97.2 1.0 %shard_map.118 = (bf16[800,256]{1,0:T(8,128)(2,1)}, f32[1,256]{1,0:T(1,128)}) custom-call(bf16[800,256]{1,0:T(8,128)(2,1)S(1)} %get-tuple-element.83.table, f32[1,256]{1,0:T(1,128)S(1)} %get-tuple-element.84.state, f32[800,256]{1,0:T(8,128)S(1)} %shard_map.117.merged, bf16[400,256]{1,0:T(8,128)(2,1)S(1)} %get-tuple-element.111.src_r, ...), custom_call_target="tpu_custom_call" | custom-call | flops 1000 | bytes 1000 | tf_op jit(solution)/shard_map/pallas_call | solution.py:19
  (93 shorter events, 10.0 us)
Async XLA Ops:
  0.6 20.8 %copy-start = (bf16[1345,800]{0,1:T(8,128)(2,1)S(1)}, bf16[1345,800]{0,1:T(8,128)(2,1)}, u32[]{:S(2)}) copy-start(bf16[1345,800]{0,1:T(8,128)(2,1)} %param.11) | copy-start | bytes 6456004
  0.6 20.8 %copy-start.5 = (s32[2,512]{1,0:T(2,128)S(1)}, s32[2,512]{1,0:T(2,128)}, u32[]{:S(2)}) copy-start(s32[2,512]{1,0:T(2,128)} %rel_ids.3) | copy-start | bytes 12292
  0.7 20.8 %copy-start.4 = (s32[2,1000]{1,0:T(2,128)S(1)}, s32[2,1000]{1,0:T(2,128)}, u32[]{:S(2)}) copy-start(s32[2,1000]{1,0:T(2,128)} %neg_ids.3) | copy-start | bytes 24004
  1.9 21.0 %copy-start.1 = (bf16[256,800]{0,1:T(8,128)(2,1)S(1)}, bf16[256,800]{0,1:T(8,128)(2,1)}, u32[]{:S(2)}) copy-start(bf16[256,800]{0,1:T(8,128)(2,1)} %param.9) | copy-start | bytes 1228804
  1.9 21.0 %copy-start.2 = (s32[2,512,1]{1,2,0:T(1,128)S(1)}, s32[2,512,1]{1,2,0:T(1,128)}, u32[]{:S(2)}) copy-start(s32[2,512,1]{1,2,0:T(1,128)} %param.14) | copy-start | bytes 12292
  1.9 21.0 %copy-start.3 = (s32[2,512]{1,0:T(2,128)S(1)}, s32[2,512]{1,0:T(2,128)}, u32[]{:S(2)}) copy-start(s32[2,512]{1,0:T(2,128)} %dest_rows.11) | copy-start | bytes 12292
  1.9 1.8 %collective-permute-start = (bf16[400,256]{1,0:T(8,128)(2,1)S(1)}, bf16[400,256]{1,0:T(8,128)(2,1)S(1)}, u32[]{:S(2)}, u32[]{:S(2)}) collective-permute-start(bf16[400,256]{1,0:T(8,128)(2,1)S(1)} %get-tuple-element.54), channel_id=1, source_target_pairs={{0,1},{1,0},{2,3},{3,2},{4,5},{5,4},{6,7},{7,6},{8,9},{9,8},{10,11... | collective-permute-start | bytes 614408 | tf_op jit(solution)/shard_map/ppermute | solution.py:163
  2.4 0.7 copy-start.8
  3.8 8.4 %collective-permute-start.1 = (bf16[400,256]{1,0:T(8,128)(2,1)S(1)}, bf16[400,256]{1,0:T(8,128)(2,1)S(1)}, u32[]{:S(2)}, u32[]{:S(2)}) collective-permute-start(bf16[400,256]{1,0:T(8,128)(2,1)S(1)} %broadcast_select_fusion.2), channel_id=1, source_target_pairs={{0,2},{1,3},{2,0},{3,1},{4,6},{5,7},{6,4},{7,5},{8,10},{9,11},{10,... | collective-permute-start | bytes 614408 | tf_op jit(solution)/shard_map/ppermute | solution.py:163
  6.6 11.6 %collective-permute-start.3 = (bf16[800,256]{1,0:T(8,128)(2,1)}, bf16[800,256]{1,0:T(8,128)(2,1)S(1)}, u32[]{:S(2)}, u32[]{:S(2)}) collective-permute-start(bf16[800,256]{1,0:T(8,128)(2,1)} %bitcast.9), channel_id=1, source_target_pairs={{0,8},{8,0},{16,24},{24,16},{1,9},{9,1},{17,25},{25,17},{2,10},{10... | collective-permute-start | bytes 1228808 | tf_op jit(solution)/shard_map/ppermute | solution.py:163
  8.1 11.8 %collective-permute-start.4 = (bf16[800,256]{1,0:T(8,128)(2,1)}, bf16[800,256]{1,0:T(8,128)(2,1)S(1)}, u32[]{:S(2)}, u32[]{:S(2)}) collective-permute-start(bf16[800,256]{1,0:T(8,128)(2,1)} %bitcast.10), channel_id=1, source_target_pairs={{0,16},{8,24},{16,0},{24,8},{1,17},{9,25},{17,1},{25,9},{2,18},{10... | collective-permute-start | bytes 1228808 | tf_op jit(solution)/shard_map/ppermute | solution.py:163
  12.2 12.2 %collective-permute-start.2 = (bf16[400,256]{1,0:T(8,128)(2,1)S(1)}, bf16[400,256]{1,0:T(8,128)(2,1)S(1)}, u32[]{:S(2)}, u32[]{:S(2)}) collective-permute-start(bf16[400,256]{1,0:T(8,128)(2,1)S(1)} %broadcast_select_fusion.3), channel_id=1, source_target_pairs={{0,4},{1,5},{2,6},{3,7},{4,0},{5,1},{6,2},{7,3},{8,12},{9,13},{10,... | collective-permute-start | bytes 614408 | tf_op jit(solution)/shard_map/ppermute | solution.py:163
  18.2 7.1 %collective-permute-start.6 = (bf16[480,256]{1,0:T(8,128)(2,1)S(1)}, bf16[480,256]{1,0:T(8,128)(2,1)S(1)}, u32[]{:S(2)}, u32[]{:S(2)}) collective-permute-start(bf16[480,256]{1,0:T(8,128)(2,1)S(1)} %slice.34), channel_id=1, source_target_pairs={{0,16},{8,24},{16,0},{24,8},{1,17},{9,25},{17,1},{25,9},{2,18},{10... | collective-permute-start | bytes 737288 | tf_op jit(solution)/shard_map/ppermute | solution.py:163
  19.9 5.4 %collective-permute-start.7 = (bf16[320,256]{1,0:T(8,128)(2,1)S(1)}, bf16[320,256]{1,0:T(8,128)(2,1)S(1)}, u32[]{:S(2)}, u32[]{:S(2)}) collective-permute-start(bf16[320,256]{1,0:T(8,128)(2,1)S(1)} %slice.35), channel_id=1, source_target_pairs={{0,8},{8,0},{16,24},{24,16},{1,9},{9,1},{17,25},{25,17},{2,10},{10... | collective-permute-start | bytes 491528 | tf_op jit(solution)/shard_map/ppermute | solution.py:163
  24.4 1.6 %copy-start.6 = (s32[2,512]{1,0:T(2,128)S(1)}, s32[2,512]{1,0:T(2,128)}, u32[]{:S(2)}) copy-start(s32[2,512]{1,0:T(2,128)} %src.3) | copy-start | bytes 12292
  24.4 1.5 %collective-permute-start.5 = (bf16[400,256]{1,0:T(8,128)(2,1)S(1)}, bf16[400,256]{1,0:T(8,128)(2,1)S(1)}, u32[]{:S(2)}, u32[]{:S(2)}) collective-permute-start(bf16[400,256]{1,0:T(8,128)(2,1)S(1)} %broadcast_select_fusion.4), channel_id=1, source_target_pairs={{0,1},{1,0},{2,3},{3,2},{4,5},{5,4},{6,7},{7,6},{8,9},{9,8},{10,11... | collective-permute-start | bytes 614408 | tf_op jit(solution)/shard_map/ppermute | solution.py:163
  28.2 1.5 %collective-permute-start.8 = (bf16[400,256]{1,0:T(8,128)(2,1)S(1)}, bf16[400,256]{1,0:T(8,128)(2,1)S(1)}, u32[]{:S(2)}, u32[]{:S(2)}) collective-permute-start(bf16[400,256]{1,0:T(8,128)(2,1)S(1)} %broadcast_select_fusion.9), channel_id=1, source_target_pairs={{0,1},{1,0},{2,3},{3,2},{4,5},{5,4},{6,7},{7,6},{8,9},{9,8},{10,11... | collective-permute-start | bytes 614408 | tf_op jit(solution)/shard_map/ppermute | solution.py:163
  29.8 7.2 %collective-permute-start.9 = (bf16[400,256]{1,0:T(8,128)(2,1)S(1)}, bf16[400,256]{1,0:T(8,128)(2,1)S(1)}, u32[]{:S(2)}, u32[]{:S(2)}) collective-permute-start(bf16[400,256]{1,0:T(8,128)(2,1)S(1)} %add_convert_fusion.9), channel_id=1, source_target_pairs={{0,2},{1,3},{2,0},{3,1},{4,6},{5,7},{6,4},{7,5},{8,10},{9,11},{10,... | collective-permute-start | bytes 614408 | tf_op jit(solution)/shard_map/ppermute | solution.py:163
  31.8 8.0 %collective-permute-start.10 = (bf16[400,256]{1,0:T(8,128)(2,1)S(1)}, bf16[400,256]{1,0:T(8,128)(2,1)S(1)}, u32[]{:S(2)}, u32[]{:S(2)}) collective-permute-start(bf16[400,256]{1,0:T(8,128)(2,1)S(1)} %get-tuple-element.72), channel_id=1, source_target_pairs={{0,8},{8,0},{16,24},{24,16},{1,9},{9,1},{17,25},{25,17},{2,10},{10... | collective-permute-start | bytes 614408 | tf_op jit(solution)/shard_map/ppermute | solution.py:163
  33.4 8.1 %collective-permute-start.12 = (bf16[400,256]{1,0:T(8,128)(2,1)S(1)}, bf16[400,256]{1,0:T(8,128)(2,1)S(1)}, u32[]{:S(2)}, u32[]{:S(2)}) collective-permute-start(bf16[400,256]{1,0:T(8,128)(2,1)S(1)} %get-tuple-element.75), channel_id=1, source_target_pairs={{0,16},{8,24},{16,0},{24,8},{1,17},{9,25},{17,1},{25,9},{2,18},{10... | collective-permute-start | bytes 614408 | tf_op jit(solution)/shard_map/ppermute | solution.py:163
  34.9 14.0 %collective-permute-start.14 = (bf16[400,256]{1,0:T(8,128)(2,1)S(1)}, bf16[400,256]{1,0:T(8,128)(2,1)S(1)}, u32[]{:S(2)}, u32[]{:S(2)}) collective-permute-start(bf16[400,256]{1,0:T(8,128)(2,1)S(1)} %get-tuple-element.76), channel_id=1, source_target_pairs={{0,8},{8,0},{16,24},{24,16},{1,9},{9,1},{17,25},{25,17},{2,10},{10... | collective-permute-start | bytes 614408 | tf_op jit(solution)/shard_map/ppermute | solution.py:163
  35.4 13.5 %collective-permute-start.15 = (bf16[400,256]{1,0:T(8,128)(2,1)S(1)}, bf16[400,256]{1,0:T(8,128)(2,1)S(1)}, u32[]{:S(2)}, u32[]{:S(2)}) collective-permute-start(bf16[400,256]{1,0:T(8,128)(2,1)S(1)} %get-tuple-element.77), channel_id=1, source_target_pairs={{0,16},{8,24},{16,0},{24,8},{1,17},{9,25},{17,1},{25,9},{2,18},{10... | collective-permute-start | bytes 614408 | tf_op jit(solution)/shard_map/ppermute | solution.py:163
  37.1 11.6 %collective-permute-start.16 = (bf16[400,256]{1,0:T(8,128)(2,1)S(1)}, bf16[400,256]{1,0:T(8,128)(2,1)S(1)}, u32[]{:S(2)}, u32[]{:S(2)}) collective-permute-start(bf16[400,256]{1,0:T(8,128)(2,1)S(1)} %add_convert_fusion.8), channel_id=1, source_target_pairs={{0,4},{1,5},{2,6},{3,7},{4,0},{5,1},{6,2},{7,3},{8,12},{9,13},{10,... | collective-permute-start | bytes 614408 | tf_op jit(solution)/shard_map/ppermute | solution.py:163
  39.9 9.0 %collective-permute-start.11 = (bf16[400,256]{1,0:T(8,128)(2,1)S(1)}, bf16[400,256]{1,0:T(8,128)(2,1)S(1)}, u32[]{:S(2)}, u32[]{:S(2)}) collective-permute-start(bf16[400,256]{1,0:T(8,128)(2,1)S(1)} %add_convert_fusion.7), channel_id=1, source_target_pairs={{0,16},{8,24},{16,0},{24,8},{1,17},{9,25},{17,1},{25,9},{2,18},{10... | collective-permute-start | bytes 614408 | tf_op jit(solution)/shard_map/ppermute | solution.py:163
  41.6 7.4 %collective-permute-start.13 = (bf16[400,256]{1,0:T(8,128)(2,1)S(1)}, bf16[400,256]{1,0:T(8,128)(2,1)S(1)}, u32[]{:S(2)}, u32[]{:S(2)}) collective-permute-start(bf16[400,256]{1,0:T(8,128)(2,1)S(1)} %add_convert_fusion.6), channel_id=1, source_target_pairs={{0,8},{8,0},{16,24},{24,16},{1,9},{9,1},{17,25},{25,17},{2,10},{10... | collective-permute-start | bytes 614408 | tf_op jit(solution)/shard_map/ppermute | solution.py:163
  48.8 1.5 %collective-permute-start.17 = (bf16[400,256]{1,0:T(8,128)(2,1)S(1)}, bf16[400,256]{1,0:T(8,128)(2,1)S(1)}, u32[]{:S(2)}, u32[]{:S(2)}) collective-permute-start(bf16[400,256]{1,0:T(8,128)(2,1)S(1)} %add_convert_fusion.5), channel_id=1, source_target_pairs={{0,1},{1,0},{2,3},{3,2},{4,5},{5,4},{6,7},{7,6},{8,9},{9,8},{10,11... | collective-permute-start | bytes 614408 | tf_op jit(solution)/shard_map/ppermute | solution.py:163
  48.9 1.5 %copy-start.7 = (f32[256]{0:T(256)S(1)}, f32[256]{0:T(256)}, u32[]{:S(2)}) copy-start(f32[256]{0:T(256)} %param.10) | copy-start | bytes 3076
  50.7 1.5 %collective-permute-start.18 = (bf16[400,256]{1,0:T(8,128)(2,1)S(1)}, bf16[400,256]{1,0:T(8,128)(2,1)S(1)}, u32[]{:S(2)}, u32[]{:S(2)}) collective-permute-start(bf16[400,256]{1,0:T(8,128)(2,1)S(1)} %broadcast_select_fusion.8), channel_id=1, source_target_pairs={{0,1},{1,0},{2,3},{3,2},{4,5},{5,4},{6,7},{7,6},{8,9},{9,8},{10,11... | collective-permute-start | bytes 614408 | tf_op jit(solution)/shard_map/ppermute | solution.py:163
  52.3 7.2 %collective-permute-start.19 = (bf16[400,256]{1,0:T(8,128)(2,1)S(1)}, bf16[400,256]{1,0:T(8,128)(2,1)S(1)}, u32[]{:S(2)}, u32[]{:S(2)}) collective-permute-start(bf16[400,256]{1,0:T(8,128)(2,1)S(1)} %select_select_fusion.2), channel_id=1, source_target_pairs={{0,2},{1,3},{2,0},{3,1},{4,6},{5,7},{6,4},{7,5},{8,10},{9,11},{10,... | collective-permute-start | bytes 614408 | tf_op jit(solution)/shard_map/ppermute | solution.py:163
  52.8 11.2 %collective-permute-start.21 = (bf16[800,256]{1,0:T(8,128)(2,1)S(1)}, bf16[800,256]{1,0:T(8,128)(2,1)S(1)}, u32[]{:S(2)}, u32[]{:S(2)}) collective-permute-start(bf16[800,256]{1,0:T(8,128)(2,1)S(1)} %get-tuple-element.83.table), channel_id=1, source_target_pairs={{0,8},{8,0},{16,24},{24,16},{1,9},{9,1},{17,25},{25,17},{2,10},{10... | collective-permute-start | bytes 1228808 | tf_op jit(solution)/shard_map/ppermute | solution.py:163
  54.4 11.3 %collective-permute-start.22 = (bf16[800,256]{1,0:T(8,128)(2,1)S(1)}, bf16[800,256]{1,0:T(8,128)(2,1)S(1)}, u32[]{:S(2)}, u32[]{:S(2)}) collective-permute-start(bf16[800,256]{1,0:T(8,128)(2,1)S(1)} %get-tuple-element.83.table), channel_id=1, source_target_pairs={{0,16},{8,24},{16,0},{24,8},{1,17},{9,25},{17,1},{25,9},{2,18},{10... | collective-permute-start | bytes 1228808 | tf_op jit(solution)/shard_map/ppermute | solution.py:163
  59.5 11.6 %collective-permute-start.20 = (bf16[400,256]{1,0:T(8,128)(2,1)S(1)}, bf16[400,256]{1,0:T(8,128)(2,1)S(1)}, u32[]{:S(2)}, u32[]{:S(2)}) collective-permute-start(bf16[400,256]{1,0:T(8,128)(2,1)S(1)} %broadcast_select_fusion), channel_id=1, source_target_pairs={{0,4},{1,5},{2,6},{3,7},{4,0},{5,1},{6,2},{7,3},{8,12},{9,13},{10,... | collective-permute-start | bytes 614408 | tf_op jit(solution)/shard_map/ppermute | solution.py:163
  64.1 7.2 %collective-permute-start.24 = (bf16[480,256]{1,0:T(8,128)(2,1)S(1)}, bf16[480,256]{1,0:T(8,128)(2,1)S(1)}, u32[]{:S(2)}, u32[]{:S(2)}) collective-permute-start(bf16[480,256]{1,0:T(8,128)(2,1)S(1)} %slice.36), channel_id=1, source_target_pairs={{0,16},{8,24},{16,0},{24,8},{1,17},{9,25},{17,1},{25,9},{2,18},{10... | collective-permute-start | bytes 737288 | tf_op jit(solution)/shard_map/ppermute | solution.py:163
  65.7 5.5 %collective-permute-start.25 = (bf16[320,256]{1,0:T(8,128)(2,1)S(1)}, bf16[320,256]{1,0:T(8,128)(2,1)S(1)}, u32[]{:S(2)}, u32[]{:S(2)}) collective-permute-start(bf16[320,256]{1,0:T(8,128)(2,1)S(1)} %slice.37), channel_id=1, source_target_pairs={{0,8},{8,0},{16,24},{24,16},{1,9},{9,1},{17,25},{25,17},{2,10},{10... | collective-permute-start | bytes 491528 | tf_op jit(solution)/shard_map/ppermute | solution.py:163
  71.2 1.5 %collective-permute-start.23 = (bf16[400,256]{1,0:T(8,128)(2,1)S(1)}, bf16[400,256]{1,0:T(8,128)(2,1)S(1)}, u32[]{:S(2)}, u32[]{:S(2)}) collective-permute-start(bf16[400,256]{1,0:T(8,128)(2,1)S(1)} %broadcast_select_fusion.1), channel_id=1, source_target_pairs={{0,1},{1,0},{2,3},{3,2},{4,5},{5,4},{6,7},{7,6},{8,9},{9,8},{10,11... | collective-permute-start | bytes 614408 | tf_op jit(solution)/shard_map/ppermute | solution.py:163
  75.1 1.5 %collective-permute-start.26 = (bf16[400,256]{1,0:T(8,128)(2,1)S(1)}, bf16[400,256]{1,0:T(8,128)(2,1)S(1)}, u32[]{:S(2)}, u32[]{:S(2)}) collective-permute-start(bf16[400,256]{1,0:T(8,128)(2,1)S(1)} %broadcast_select_fusion.5), channel_id=1, source_target_pairs={{0,1},{1,0},{2,3},{3,2},{4,5},{5,4},{6,7},{7,6},{8,9},{9,8},{10,11... | collective-permute-start | bytes 614408 | tf_op jit(solution)/shard_map/ppermute | solution.py:163
  76.7 7.2 %collective-permute-start.27 = (bf16[400,256]{1,0:T(8,128)(2,1)S(1)}, bf16[400,256]{1,0:T(8,128)(2,1)S(1)}, u32[]{:S(2)}, u32[]{:S(2)}) collective-permute-start(bf16[400,256]{1,0:T(8,128)(2,1)S(1)} %add_convert_fusion.4), channel_id=1, source_target_pairs={{0,2},{1,3},{2,0},{3,1},{4,6},{5,7},{6,4},{7,5},{8,10},{9,11},{10,... | collective-permute-start | bytes 614408 | tf_op jit(solution)/shard_map/ppermute | solution.py:163
  78.6 8.0 %collective-permute-start.28 = (bf16[400,256]{1,0:T(8,128)(2,1)S(1)}, bf16[400,256]{1,0:T(8,128)(2,1)S(1)}, u32[]{:S(2)}, u32[]{:S(2)}) collective-permute-start(bf16[400,256]{1,0:T(8,128)(2,1)S(1)} %get-tuple-element.97), channel_id=1, source_target_pairs={{0,8},{8,0},{16,24},{24,16},{1,9},{9,1},{17,25},{25,17},{2,10},{10... | collective-permute-start | bytes 614408 | tf_op jit(solution)/shard_map/ppermute | solution.py:163
  80.3 8.1 %collective-permute-start.30 = (bf16[400,256]{1,0:T(8,128)(2,1)S(1)}, bf16[400,256]{1,0:T(8,128)(2,1)S(1)}, u32[]{:S(2)}, u32[]{:S(2)}) collective-permute-start(bf16[400,256]{1,0:T(8,128)(2,1)S(1)} %get-tuple-element.100), channel_id=1, source_target_pairs={{0,16},{8,24},{16,0},{24,8},{1,17},{9,25},{17,1},{25,9},{2,18},{10... | collective-permute-start | bytes 614408 | tf_op jit(solution)/shard_map/ppermute | solution.py:163
  81.8 14.0 %collective-permute-start.32 = (bf16[400,256]{1,0:T(8,128)(2,1)S(1)}, bf16[400,256]{1,0:T(8,128)(2,1)S(1)}, u32[]{:S(2)}, u32[]{:S(2)}) collective-permute-start(bf16[400,256]{1,0:T(8,128)(2,1)S(1)} %get-tuple-element.101), channel_id=1, source_target_pairs={{0,8},{8,0},{16,24},{24,16},{1,9},{9,1},{17,25},{25,17},{2,10},{10... | collective-permute-start | bytes 614408 | tf_op jit(solution)/shard_map/ppermute | solution.py:163
  82.3 13.5 %collective-permute-start.33 = (bf16[400,256]{1,0:T(8,128)(2,1)S(1)}, bf16[400,256]{1,0:T(8,128)(2,1)S(1)}, u32[]{:S(2)}, u32[]{:S(2)}) collective-permute-start(bf16[400,256]{1,0:T(8,128)(2,1)S(1)} %get-tuple-element.102), channel_id=1, source_target_pairs={{0,16},{8,24},{16,0},{24,8},{1,17},{9,25},{17,1},{25,9},{2,18},{10... | collective-permute-start | bytes 614408 | tf_op jit(solution)/shard_map/ppermute | solution.py:163
  84.0 11.6 %collective-permute-start.34 = (bf16[400,256]{1,0:T(8,128)(2,1)S(1)}, bf16[400,256]{1,0:T(8,128)(2,1)S(1)}, u32[]{:S(2)}, u32[]{:S(2)}) collective-permute-start(bf16[400,256]{1,0:T(8,128)(2,1)S(1)} %add_convert_fusion.3), channel_id=1, source_target_pairs={{0,4},{1,5},{2,6},{3,7},{4,0},{5,1},{6,2},{7,3},{8,12},{9,13},{10,... | collective-permute-start | bytes 614408 | tf_op jit(solution)/shard_map/ppermute | solution.py:163
  86.7 9.1 %collective-permute-start.29 = (bf16[400,256]{1,0:T(8,128)(2,1)S(1)}, bf16[400,256]{1,0:T(8,128)(2,1)S(1)}, u32[]{:S(2)}, u32[]{:S(2)}) collective-permute-start(bf16[400,256]{1,0:T(8,128)(2,1)S(1)} %add_convert_fusion.2), channel_id=1, source_target_pairs={{0,16},{8,24},{16,0},{24,8},{1,17},{9,25},{17,1},{25,9},{2,18},{10... | collective-permute-start | bytes 614408 | tf_op jit(solution)/shard_map/ppermute | solution.py:163
  88.4 7.4 %collective-permute-start.31 = (bf16[400,256]{1,0:T(8,128)(2,1)S(1)}, bf16[400,256]{1,0:T(8,128)(2,1)S(1)}, u32[]{:S(2)}, u32[]{:S(2)}) collective-permute-start(bf16[400,256]{1,0:T(8,128)(2,1)S(1)} %add_convert_fusion.1), channel_id=1, source_target_pairs={{0,8},{8,0},{16,24},{24,16},{1,9},{9,1},{17,25},{25,17},{2,10},{10... | collective-permute-start | bytes 614408 | tf_op jit(solution)/shard_map/ppermute | solution.py:163
  95.7 1.5 %collective-permute-start.35 = (bf16[400,256]{1,0:T(8,128)(2,1)S(1)}, bf16[400,256]{1,0:T(8,128)(2,1)S(1)}, u32[]{:S(2)}, u32[]{:S(2)}) collective-permute-start(bf16[400,256]{1,0:T(8,128)(2,1)S(1)} %add_convert_fusion), channel_id=1, source_target_pairs={{0,1},{1,0},{2,3},{3,2},{4,5},{5,4},{6,7},{7,6},{8,9},{9,8},{10,11... | collective-permute-start | bytes 614408 | tf_op jit(solution)/shard_map/ppermute | solution.py:163
